TPU v7x, 128 devices: a whole 4x4x4 slice. The times are simulated.
128 devices in a mesh: shard: 16 (over y, z), context: 2 (over x_lo), tensor: 4 (over x_hi, core).
Axes of the slice: x: 4 (x_hi: 2, x_lo: 2; x = x_hi * 2 + x_lo), y: 4, z: 4, core: 2. Of those that a mesh axis runs over, the one named last changes fastest.
Arguments:
- tokens: bfloat16 [16, 1024, 1024], P('shard', ('context', 'tensor')), may hold values from -6 to 6
- cotangent: bfloat16 [16, 1024, 1024], P('shard', ('context', 'tensor')), may hold values from -6 to 6
- attention_gain: bfloat16 [1024], P('shard'), may hold values from 0.099609375 to 1.8984375
- query_weight: bfloat16 [1024, 1024], P('shard'), may hold values from -0.1875 to 0.1875
- key_weight: bfloat16 [1024, 512], P('shard'), may hold values from -0.1875 to 0.1875
- value_weight: bfloat16 [1024, 512], P('shard'), may hold values from -0.1875 to 0.1875
- query_gain: bfloat16 [64], P('shard'), may hold values from 0.099609375 to 1.8984375
- key_gain: bfloat16 [64], P('shard'), may hold values from 0.099609375 to 1.8984375
- out_weight: bfloat16 [1024, 1024], P('shard'), may hold values from -0.375 to 0.375
- feed_gain: bfloat16 [1024], P('shard'), may hold values from 0.099609375 to 1.8984375
- gate_weight: bfloat16 [1024, 4608], P('shard', 'tensor'), may hold values from -0.1875 to 0.1875
- up_weight: bfloat16 [1024, 4608], P('shard', 'tensor'), may hold values from -0.1875 to 0.1875
- down_weight: bfloat16 [4608, 1024], P('tensor', 'shard'), may hold values from -0.09375 to 0.09375
Outputs:
- output: bfloat16 [16, 1024, 1024], P('shard', ('context', 'tensor'))
- input_gradient: bfloat16 [16, 1024, 1024], P('shard', ('context', 'tensor'))
- attention_gain_gradient: float32 [1024], P('shard')
- query_weight_gradient: float32 [1024, 1024], P('shard')
- key_weight_gradient: float32 [1024, 512], P('shard')
- value_weight_gradient: float32 [1024, 512], P('shard')
- query_gain_gradient: float32 [64], P('shard')
- key_gain_gradient: float32 [64], P('shard')
- out_weight_gradient: float32 [1024, 1024], P('shard')
- feed_gain_gradient: float32 [1024], P('shard')
- gate_weight_gradient: float32 [1024, 4608], P('shard', 'tensor')
- up_weight_gradient: float32 [1024, 4608], P('shard', 'tensor')
- down_weight_gradient: float32 [4608, 1024], P('tensor', 'shard')
All inputs are finite; a program needn't handle non-finite values.
Results may differ from a plain program's by a relative error of at most 0.015.
Values may be sent and summed in bfloat16 or wider, within the bound.
No kernel may reach another device: no remote copies, remote signals or barrier semaphores. Data moves between devices by JAX's collectives and lax.ppermute only.
A program may use at most 128 MiB of HBM per device.

v0:
```python
import jax
import jax.numpy as jnp
from jax import lax
from jax.sharding import PartitionSpec as P

epsilon = 1e-05
rope_base = 1000000.0
masked_score = -1e30


def rope_tables(positions, head_dim):
    exponent = jnp.arange(0, head_dim, 2).astype(jnp.float32) / head_dim
    frequency = 1.0 / rope_base**exponent
    angle = positions.astype(jnp.float32)[:, None] * frequency[None, :]
    angle = jnp.concatenate([angle, angle], axis=-1)
    return (jnp.cos(angle), jnp.sin(angle))


def rotate(value, cosine, sine):
    half = value.shape[-1] // 2
    turned = jnp.concatenate([-value[..., half:], value[..., :half]], axis=-1)
    return value * cosine + turned * sine


def rotate_back(grad_value, cosine, sine):
    half = grad_value.shape[-1] // 2
    moved = grad_value * sine
    turned = jnp.concatenate([moved[..., half:], -moved[..., :half]], axis=-1)
    return grad_value * cosine + turned


def rms_parts(value):
    inverse = lax.rsqrt(jnp.mean(value * value, axis=-1, keepdims=True) + epsilon)
    return (value * inverse, inverse)


def norm_back(grad_value, normed, inverse, gain):
    scaled = grad_value * gain
    return inverse * (scaled - normed * jnp.mean(scaled * normed, axis=-1, keepdims=True))


def masked_scores(queries, keys, start, scale):
    count = queries.shape[1]
    stop = keys.shape[1]
    score = (
        jnp.einsum("sqhgd,skhd->shgqk", queries, keys, preferred_element_type=jnp.float32) * scale
    )
    allowed = jnp.arange(stop)[None, :] <= (start + jnp.arange(count))[:, None]
    return jnp.where(allowed, score, masked_score)


def split_gains(packed, first_width, head_width):
    flat = packed.reshape(-1)
    middle = first_width + head_width
    return (
        flat[:first_width],
        flat[first_width:middle],
        flat[middle : middle + head_width],
        flat[middle + head_width :],
    )


def on_device(
    tokens,
    cotangent,
    attention_gain,
    query_weight,
    key_weight,
    value_weight,
    query_gain,
    key_gain,
    out_weight,
    feed_gain,
    gate_weight,
    up_weight,
    down_weight,
):
    gathered = (
        lax.all_gather(attention_gain, "shard", axis=0, tiled=True),
        lax.all_gather(query_weight, "shard", axis=0, tiled=True),
        lax.all_gather(key_weight, "shard", axis=0, tiled=True),
        lax.all_gather(value_weight, "shard", axis=0, tiled=True),
        lax.all_gather(query_gain, "shard", axis=0, tiled=True),
        lax.all_gather(key_gain, "shard", axis=0, tiled=True),
        lax.all_gather(out_weight, "shard", axis=0, tiled=True),
        lax.all_gather(feed_gain, "shard", axis=0, tiled=True),
        lax.all_gather(gate_weight, "shard", axis=0, tiled=True),
        lax.all_gather(up_weight, "shard", axis=0, tiled=True),
        lax.all_gather(down_weight, "shard", axis=1, tiled=True),
    )
    (
        gain_first,
        query_full,
        key_full,
        value_full,
        gain_query,
        gain_key,
        out_full,
        gain_second,
        gate_full,
        up_full,
        down_full,
    ) = gathered
    gain_first = gain_first.astype(jnp.float32)
    gain_query = gain_query.astype(jnp.float32)
    gain_key = gain_key.astype(jnp.float32)
    gain_second = gain_second.astype(jnp.float32)
    seq_count, piece, width = tokens.shape
    head_dim = gain_query.shape[0]
    query_width = query_full.shape[1]
    shared_width = key_full.shape[1]
    query_heads = query_width // head_dim
    shared_heads = shared_width // head_dim
    group = query_heads // shared_heads
    shard_count = lax.axis_size("shard")
    tensor_count = lax.axis_size("tensor")
    piece_count = lax.axis_size("context") * tensor_count
    shared_local = shared_heads // piece_count
    length = piece * piece_count
    row_count = seq_count * piece
    scale = head_dim ** (-0.5)
    group_width = group * head_dim
    inputs = tokens.reshape(row_count, width).astype(jnp.float32)
    normed_first, inverse_first = rms_parts(inputs)
    mixer_input = (normed_first * gain_first).astype(jnp.bfloat16)
    query_raw = jnp.dot(mixer_input, query_full, preferred_element_type=jnp.float32)
    key_raw = jnp.dot(mixer_input, key_full, preferred_element_type=jnp.float32)
    value_low = jnp.dot(mixer_input, value_full, preferred_element_type=jnp.float32).astype(
        jnp.bfloat16
    )
    place = lax.axis_index("context") * tensor_count + lax.axis_index("tensor")
    cosine, sine = rope_tables(place * piece + jnp.arange(piece), head_dim)
    cosine = cosine[:, None, :]
    sine = sine[:, None, :]
    normed_query, inverse_query = rms_parts(
        query_raw.reshape(seq_count, piece, query_heads, head_dim)
    )
    normed_key, inverse_key = rms_parts(key_raw.reshape(seq_count, piece, shared_heads, head_dim))
    query_low = rotate(normed_query * gain_query, cosine, sine).astype(jnp.bfloat16)
    key_low = rotate(normed_key * gain_key, cosine, sine).astype(jnp.bfloat16)
    packed = jnp.concatenate(
        [
            query_low.reshape(seq_count, piece, shared_heads, group_width),
            key_low,
            value_low.reshape(seq_count, piece, shared_heads, head_dim),
        ],
        axis=-1,
    )
    by_heads = lax.all_to_all(
        packed, ("context", "tensor"), split_axis=2, concat_axis=1, tiled=True
    )
    queries = by_heads[..., :group_width].reshape(seq_count, length, shared_local, group, head_dim)
    keys = by_heads[..., group_width : group_width + head_dim]
    values = by_heads[..., group_width + head_dim :]
    block = 512
    starts = list(range(0, length, block))
    result_blocks = []
    log_sums = []
    for start in starts:
        stop = start + block
        score = masked_scores(queries[:, start:stop], keys[:, :stop], start, scale)
        peak = jnp.max(score, axis=-1, keepdims=True)
        raised = jnp.exp(score - peak)
        total = jnp.sum(raised, axis=-1, keepdims=True)
        chance = (raised / total).astype(jnp.bfloat16)
        result_blocks.append(
            jnp.einsum(
                "shgqk,skhd->sqhgd", chance, values[:, :stop], preferred_element_type=jnp.float32
            ).astype(jnp.bfloat16)
        )
        log_sums.append(peak + jnp.log(total))
    attended_heads = jnp.concatenate(result_blocks, axis=1).reshape(
        seq_count, length, shared_local, group_width
    )
    attended = lax.all_to_all(
        attended_heads, ("context", "tensor"), split_axis=1, concat_axis=2, tiled=True
    ).reshape(row_count, query_width)
    branch = jnp.dot(attended, out_full, preferred_element_type=jnp.float32)
    mixed = inputs + branch
    normed_second, inverse_second = rms_parts(mixed)
    feed_input = (normed_second * gain_second).astype(jnp.bfloat16)
    seed_rows = cotangent.reshape(row_count, width)
    feed_all, seed_all = (
        lax.all_gather(feed_input, "tensor", axis=0, tiled=True),
        lax.all_gather(seed_rows, "tensor", axis=0, tiled=True),
    )
    gate = jnp.dot(feed_all, gate_full, preferred_element_type=jnp.float32)
    upward = jnp.dot(feed_all, up_full, preferred_element_type=jnp.float32)
    squashed = jax.nn.sigmoid(gate)
    activated = gate * squashed
    hidden = (activated * upward).astype(jnp.bfloat16)
    feed_rows = lax.psum_scatter(
        jnp.dot(hidden, down_full, preferred_element_type=jnp.float32),
        "tensor",
        scatter_dimension=0,
        tiled=True,
    )
    output = (mixed + feed_rows).astype(jnp.bfloat16).reshape(seq_count, piece, width)
    grad_hidden = jnp.dot(seed_all, down_full.T, preferred_element_type=jnp.float32)
    grad_gate = (grad_hidden * upward * squashed * (1.0 + gate * (1.0 - squashed))).astype(
        jnp.bfloat16
    )
    grad_up = (grad_hidden * activated).astype(jnp.bfloat16)
    gate_sum = jnp.dot(feed_all.T, grad_gate, preferred_element_type=jnp.float32)
    up_sum = jnp.dot(feed_all.T, grad_up, preferred_element_type=jnp.float32)
    down_sum = jnp.dot(hidden.T, seed_all, preferred_element_type=jnp.float32)
    grad_feed = lax.psum_scatter(
        jnp.dot(grad_gate, gate_full.T, preferred_element_type=jnp.float32)
        + jnp.dot(grad_up, up_full.T, preferred_element_type=jnp.float32),
        "tensor",
        scatter_dimension=0,
        tiled=True,
    )
    feed_gain_sum = jnp.sum(grad_feed * normed_second, axis=0)
    grad_mixed = seed_rows.astype(jnp.float32) + norm_back(
        grad_feed, normed_second, inverse_second, gain_second
    )
    grad_branch = grad_mixed.astype(jnp.bfloat16)
    out_sum = jnp.dot(attended.T, grad_branch, preferred_element_type=jnp.float32)
    grad_attended = jnp.dot(grad_branch, out_full.T, preferred_element_type=jnp.float32).astype(
        jnp.bfloat16
    )
    grad_attended = grad_attended.reshape(seq_count, piece, shared_heads, group_width)
    grad_heads = lax.all_to_all(
        grad_attended, ("context", "tensor"), split_axis=2, concat_axis=1, tiled=True
    ).reshape(seq_count, length, shared_local, group, head_dim)
    key_grad = jnp.zeros((seq_count, length, shared_local, head_dim), jnp.float32)
    value_grad = jnp.zeros((seq_count, length, shared_local, head_dim), jnp.float32)
    query_blocks = []
    for index, start in enumerate(starts):
        stop = start + block
        query_block = queries[:, start:stop]
        score = masked_scores(query_block, keys[:, :stop], start, scale)
        chance_full = jnp.exp(score - log_sums[index])
        chance_low = chance_full.astype(jnp.bfloat16)
        grad_block = grad_heads[:, start:stop]
        grad_chance = jnp.einsum(
            "sqhgd,skhd->shgqk", grad_block, values[:, :stop], preferred_element_type=jnp.float32
        )
        inner = jnp.sum(chance_full * grad_chance, axis=-1, keepdims=True)
        grad_score = (chance_full * (grad_chance - inner)).astype(jnp.bfloat16)
        query_blocks.append(
            (
                jnp.einsum(
                    "shgqk,skhd->sqhgd",
                    grad_score,
                    keys[:, :stop],
                    preferred_element_type=jnp.float32,
                )
                * scale
            ).astype(jnp.bfloat16)
        )
        key_grad = key_grad.at[:, :stop].add(
            jnp.einsum(
                "shgqk,sqhgd->skhd", grad_score, query_block, preferred_element_type=jnp.float32
            )
            * scale
        )
        value_grad = value_grad.at[:, :stop].add(
            jnp.einsum(
                "shgqk,sqhgd->skhd", chance_low, grad_block, preferred_element_type=jnp.float32
            )
        )
    query_grad = jnp.concatenate(query_blocks, axis=1).reshape(
        seq_count, length, shared_local, group_width
    )
    packed_back = jnp.concatenate(
        [query_grad, key_grad.astype(jnp.bfloat16), value_grad.astype(jnp.bfloat16)], axis=-1
    )
    by_tokens = lax.all_to_all(
        packed_back, ("context", "tensor"), split_axis=1, concat_axis=2, tiled=True
    )
    grad_query_turned = (
        by_tokens[..., :group_width]
        .reshape(seq_count, piece, query_heads, head_dim)
        .astype(jnp.float32)
    )
    grad_key_turned = by_tokens[..., group_width : group_width + head_dim].astype(jnp.float32)
    grad_value = by_tokens[..., group_width + head_dim :].reshape(row_count, shared_width)
    grad_query_normed = rotate_back(grad_query_turned, cosine, sine)
    grad_key_normed = rotate_back(grad_key_turned, cosine, sine)
    query_gain_sum = jnp.sum(grad_query_normed * normed_query, axis=(0, 1, 2))
    key_gain_sum = jnp.sum(grad_key_normed * normed_key, axis=(0, 1, 2))
    grad_query_raw = (
        norm_back(grad_query_normed, normed_query, inverse_query, gain_query)
        .astype(jnp.bfloat16)
        .reshape(row_count, query_width)
    )
    grad_key_raw = (
        norm_back(grad_key_normed, normed_key, inverse_key, gain_key)
        .astype(jnp.bfloat16)
        .reshape(row_count, shared_width)
    )
    query_sum = jnp.dot(mixer_input.T, grad_query_raw, preferred_element_type=jnp.float32)
    key_sum = jnp.dot(mixer_input.T, grad_key_raw, preferred_element_type=jnp.float32)
    value_sum = jnp.dot(mixer_input.T, grad_value, preferred_element_type=jnp.float32)
    grad_mixer = jnp.dot(grad_query_raw, query_full.T, preferred_element_type=jnp.float32)
    grad_mixer = grad_mixer + jnp.dot(grad_key_raw, key_full.T, preferred_element_type=jnp.float32)
    grad_mixer = grad_mixer + jnp.dot(grad_value, value_full.T, preferred_element_type=jnp.float32)
    first_gain_sum = jnp.sum(grad_mixer * normed_first, axis=0)
    input_gradient = (
        (grad_mixed + norm_back(grad_mixer, normed_first, inverse_first, gain_first))
        .astype(jnp.bfloat16)
        .reshape(seq_count, piece, width)
    )
    gain_pack = jnp.concatenate(
        [
            first_gain_sum.reshape(shard_count, -1),
            query_gain_sum.reshape(shard_count, -1),
            key_gain_sum.reshape(shard_count, -1),
            feed_gain_sum.reshape(shard_count, -1),
        ],
        axis=1,
    )
    first_width = width // shard_count
    head_width = head_dim // shard_count
    query_part, key_part, value_part, out_part, gain_part, gate_part, up_part, down_part = (
        lax.psum_scatter(query_sum, "shard", scatter_dimension=0, tiled=True),
        lax.psum_scatter(key_sum, "shard", scatter_dimension=0, tiled=True),
        lax.psum_scatter(value_sum, "shard", scatter_dimension=0, tiled=True),
        lax.psum_scatter(out_sum, "shard", scatter_dimension=0, tiled=True),
        lax.psum_scatter(gain_pack, "shard", scatter_dimension=0, tiled=True),
        lax.psum_scatter(gate_sum, "shard", scatter_dimension=0, tiled=True),
        lax.psum_scatter(up_sum, "shard", scatter_dimension=0, tiled=True),
        lax.psum_scatter(down_sum, "shard", scatter_dimension=1, tiled=True),
    )
    query_part, key_part, value_part, out_part, gain_part = lax.psum(
        (query_part, key_part, value_part, out_part, gain_part), ("context", "tensor")
    )
    gate_part, up_part, down_part = lax.psum((gate_part, up_part, down_part), "context")
    first_gain_grad, query_gain_grad, key_gain_grad, feed_gain_grad = split_gains(
        gain_part, first_width, head_width
    )
    return (
        output,
        input_gradient,
        first_gain_grad,
        query_part,
        key_part,
        value_part,
        query_gain_grad,
        key_gain_grad,
        out_part,
        feed_gain_grad,
        gate_part,
        up_part,
        down_part,
    )


def solution(mesh):
    placed = (
        P("shard", ("context", "tensor"), None),
        P("shard", ("context", "tensor"), None),
        P("shard"),
        P("shard", None),
        P("shard", None),
        P("shard", None),
        P("shard"),
        P("shard"),
        P("shard", None),
        P("shard"),
        P("shard", "tensor"),
        P("shard", "tensor"),
        P("tensor", "shard"),
    )
    return jax.shard_map(
        on_device,
        mesh=mesh,
        in_specs=placed,
        out_specs=(
            P("shard", ("context", "tensor"), None),
            P("shard", ("context", "tensor"), None),
            P("shard"),
            P("shard", None),
            P("shard", None),
            P("shard", None),
            P("shard"),
            P("shard"),
            P("shard", None),
            P("shard"),
            P("shard", "tensor"),
            P("shard", "tensor"),
            P("tensor", "shard"),
        ),
        check_vma=False,
    )
```

profile of v0, /device:TPU:1, one launch (start us, length us, event | category | flops | bytes accessed | tf_op | source)
XLA Modules:
  0.0 1153.8 jit_solution(10786583412152606544)
XLA Ops:
  16.6 36.2 %all-reduce.9 = (bf16[1024]{0:T(1024)(128)(2,1)S(1)}, bf16[64]{0:T(256)(128)(2,1)S(1)}, bf16[64]{0:T(256)(128)(2,1)S(1)}, bf16[1024]{0:T(1024)(128)(2,1)S(1)}) all-reduce(bf16[1024]{0:T(1024)(128)(2,1)S(1)} %dynamic-update-slice.10, ...), channel_id=1, replica_groups=mesh['shard'=16,'context'=2,'tensor'=4] {'shard'}, use_global_device_ids=true, to_apply=%add.2 | all-reduce | flops 2176 | bytes 8704
  55.0 1.7 convolution_convert_fusion.2
  56.8 42.4 %all-gather.13.cloned.1.call-done = bf16[1024,512]{1,0:T(8,128)(2,1)} async-done(((bf16[64,512]{1,0:T(8,128)(2,1)}), bf16[1024,512]{1,0:T(8,128)(2,1)}) %all-gather.13.cloned.1.call-update) | async-done | bytes 1048592 | tf_op jit(solution)/shard_map/all_gather | solution.py:81
  99.2 1.8 fusion.94
  101.3 45.0 %all-gather.11.cloned.1.call-done = bf16[1024,1024]{1,0:T(8,128)(2,1)} async-done(((bf16[64,1024]{1,0:T(8,128)(2,1)}), bf16[1024,1024]{1,0:T(8,128)(2,1)}) %all-gather.11.cloned.1.call-update) | async-done | bytes 2097168 | tf_op jit(solution)/shard_map/all_gather | solution.py:80
  146.3 2.1 fusion.96
  152.0 6.0 all-to-all-start
  160.0 6.7 all-to-all-done
  166.9 1.8 fusion.102
  174.5 3.1 reduce.20
  178.4 4.6 all-to-all-start.1
  183.1 6.6 all-to-all-done.1
  190.7 1.8 copy.153
  193.6 2.2 multiply_reduce_fusion.3
  199.9 40.2 %all-gather.21.cloned.1.call-done = bf16[1024,1152]{1,0:T(8,128)(2,1)} async-done(((bf16[64,1152]{1,0:T(8,128)(2,1)}), bf16[1024,1152]{1,0:T(8,128)(2,1)}) %all-gather.21.cloned.1.call-update) | async-done | bytes 2359312 | tf_op jit(solution)/shard_map/all_gather | solution.py:87
  240.1 23.4 %all-gather.19.cloned.1.call-done = bf16[512,1024]{1,0:T(8,128)(2,1)} async-done(((bf16[128,1024]{1,0:T(8,128)(2,1)}), bf16[512,1024]{1,0:T(8,128)(2,1)}) %all-gather.19.cloned.1.call-update) | async-done | bytes 1048592 | tf_op jit(solution)/shard_map/all_gather | solution.py:184
  263.6 5.0 fusion.104
  268.6 41.1 %all-gather.23.cloned.1.call-done = bf16[1024,1152]{1,0:T(8,128)(2,1)} async-done(((bf16[64,1152]{1,0:T(8,128)(2,1)}), bf16[1024,1152]{1,0:T(8,128)(2,1)}) %all-gather.23.cloned.1.call-update) | async-done | bytes 2359312 | tf_op jit(solution)/shard_map/all_gather | solution.py:88
  309.7 4.9 fusion.105
  314.7 18.1 %all-gather.27.cloned.1.call-done = bf16[1,512,1024]{2,1,0:T(8,128)(2,1)} async-done(((bf16[1,128,1024]{2,1,0:T(8,128)(2,1)}), bf16[1,512,1024]{2,1,0:T(8,128)(2,1)}) %all-gather.27.cloned.1.call-update) | async-done | bytes 1048592 | tf_op jit(solution)/shard_map/all_gather | solution.py:185
  332.7 46.2 %all-gather.25.cloned.1.call-done = bf16[1152,1024]{0,1:T(8,128)(2,1)} async-done(((bf16[1152,64]{0,1:T(8,128)(2,1)}), bf16[1152,1024]{0,1:T(8,128)(2,1)}) %all-gather.25.cloned.1.call-update) | async-done | bytes 2359312 | tf_op jit(solution)/shard_map/all_gather | solution.py:89
  378.9 6.7 multiply_convert_fusion
  385.6 1.6 fusion.107
  388.1 2.9 convolution_add_fusion
  391.0 4.9 fusion.106
  396.0 5.3 fusion.109
  401.4 5.6 fusion.110
  407.1 5.4 fusion.48
  412.5 17.2 %reduce-scatter.12.cloned.1.call-done = f32[128,1024]{1,0:T(8,128)} async-done(((f32[512,1024]{1,0:T(8,128)}), f32[128,1024]{1,0:T(8,128)}) %reduce-scatter.12.cloned.1.call-update) | async-done | bytes 524304 | tf_op jit(solution)/shard_map/reduce_scatter | solution.py:207
  429.6 1.4 multiply_reduce_fusion
  431.1 39.2 %reduce-scatter.10.cloned.1.call-done = f32[128,1024]{1,0:T(8,128)} async-done(((f32[512,1024]{1,0:T(8,128)}), f32[128,1024]{1,0:T(8,128)}) %reduce-scatter.10.cloned.1.call-update) | async-done | bytes 524304 | tf_op jit(solution)/shard_map/reduce_scatter | solution.py:192
  470.3 2.5 convert_add_fusion
  474.4 4.0 all-to-all-start.2
  478.6 6.2 all-to-all-done.2
  487.2 3.7 fusion.28
  490.9 1.9 copy.134
  496.9 1.8 fusion
  501.7 1.6 fusion.44
  503.3 1.4 fusion.38
  505.1 3.3 fusion.103
  508.4 3.8 reduce.21
  512.4 12.7 %all_to_all.66 = bf16[8,2,16384]{2,1,0:T(2,128)(2,1)S(1)} all-to-all(bf16[8,2,16384]{2,1,0:T(2,128)(2,1)S(1)} %reshape.938), channel_id=1, replica_groups=mesh['shard'=16,'context'=2,'tensor'=4] {'context','tensor'}, dimensions={0} | all-to-all | bytes 1048576 | tf_op jit(solution)/shard_map/all_to_all | solution.py:270
  526.3 1.9 fusion.87
  528.6 1.9 fusion.85
  530.6 2.7 fusion.80
  540.1 1.8 multiply_convert_fusion.3
  541.9 2.8 fusion.91
  545.6 1.5 fusion.71
  547.9 1.9 fusion.108
  549.8 1.5 convolution_add_fusion.2
  551.3 79.7 %reduce-scatter.24.cloned.1.call-done = f32[64,1152]{1,0:T(8,128)} async-done(((f32[1024,1152]{1,0:T(8,128)}), f32[64,1152]{1,0:T(8,128)}) %reduce-scatter.24.cloned.1.call-update) | async-done | bytes 294928 | tf_op jit(solution)/shard_map/reduce_scatter | solution.py:324
  631.0 81.1 %reduce-scatter.26.cloned.1.call-done = f32[1152,64]{0,1:T(8,128)} async-done(((f32[1152,1024]{0,1:T(8,128)}), f32[1152,64]{0,1:T(8,128)}) %reduce-scatter.26.cloned.1.call-update) | async-done | bytes 294928 | tf_op jit(solution)/shard_map/reduce_scatter | solution.py:325
  712.9 58.3 %all-reduce.6 = f32[16,136]{1,0:T(8,128)S(1)} all-reduce(f32[16,136]{1,0:T(8,128)S(1)} %pad_maximum_fusion.6), channel_id=5, replica_groups=mesh['shard'=16,'context'=2,'tensor'=4] {'shard'}, use_global_device_ids=true, to_apply=%region_21.22.clone | all-reduce | flops 2176 | bytes 17408
  771.9 27.9 %psum.56 = f32[1,136]{1,0:T(1,128)S(1)} all-reduce(f32[1,136]{1,0:T(1,128)S(1)} %constant_dynamic-slice_fusion), channel_id=1, replica_groups=mesh['shard'=16,'context'=2,'tensor'=4] {'context','tensor'}, use_global_device_ids=true, to_apply=%region_22.23 | all-reduce | flops 136 | bytes 1088 | tf_op jit(solution)/shard_map/psum | solution.py:327
  801.0 65.0 %reduce-scatter.18.cloned.1.call-done = f32[64,512]{1,0:T(8,128)} async-done(((f32[1024,512]{1,0:T(8,128)}), f32[64,512]{1,0:T(8,128)}) %reduce-scatter.18.cloned.1.call-update) | async-done | bytes 131088 | tf_op jit(solution)/shard_map/reduce_scatter | solution.py:320
  866.0 80.2 %reduce-scatter.20.cloned.1.call-done = f32[64,1024]{1,0:T(8,128)} async-done(((f32[1024,1024]{1,0:T(8,128)}), f32[64,1024]{1,0:T(8,128)}) %reduce-scatter.20.cloned.1.call-update) | async-done | bytes 262160 | tf_op jit(solution)/shard_map/reduce_scatter | solution.py:321
  946.2 80.6 %reduce-scatter.14.cloned.1.call-done = f32[64,1024]{1,0:T(8,128)} async-done(((f32[1024,1024]{1,0:T(8,128)}), f32[64,1024]{1,0:T(8,128)}) %reduce-scatter.14.cloned.1.call-update) | async-done | bytes 262160 | tf_op jit(solution)/shard_map/reduce_scatter | solution.py:318
  1027.8 46.0 %all-reduce.15.cloned.1.call-done = (f32[64,1152]{1,0:T(8,128)}, f32[64,1152]{1,0:T(8,128)}, f32[1152,64]{0,1:T(8,128)}) async-done(((f32[64,1152]{1,0:T(8,128)}, f32[64,1152]{1,0:T(8,128)}, f32[1152,64]{0,1:T(8,128)}), (f32[64,1152]{1,0:T(8,128)}, f32[64,1152]{1,0:T(8,128)}, f32[1152,64]{0,1:T(8,128)})) %all-reduce.15.cloned.1.call-update) | async-done | bytes 884752 | tf_op jit(solution)/shard_map/psum | solution.py:330
  1073.8 63.1 %all-reduce.13.cloned.1.call-done = (f32[64,1024]{1,0:T(8,128)}, f32[64,512]{1,0:T(8,128)}, f32[64,512]{1,0:T(8,128)}, f32[64,1024]{1,0:T(8,128)}) async-done(((f32[64,1024]{1,0:T(8,128)}, f32[64,512]{1,0:T(8,128)}, f32[64,512]{1,0:T(8,128)}, f32[64,1024]{1,0:T(8,128)}), (f32[64,1024]{1,0:T(8,128)}, f32[64,512]{1,0:T(8,128)}, f32[64,512]{1,0:T(8,128)}, f32[64,1024]{1,0:T(8,128)})) %all-reduce.13.cloned.1.call-update) | async-done | bytes 786448 | tf_op jit(solution)/shard_map/psum | solution.py:327
  1136.9 1.7 copy.169
  1138.6 1.6 copy.170
  1140.1 1.6 copy.171
  1141.7 1.7 copy.172
  1143.4 1.7 copy.173
  (233 shorter events, 56.9 us)
Async XLA Ops:
  7.2 92.0 %copy-start.2 = (bf16[1,128,1024]{2,1,0:T(8,128)(2,1)S(1)}, bf16[1,128,1024]{2,1,0:T(8,128)(2,1)}, u32[]{:S(2)}) copy-start(bf16[1,128,1024]{2,1,0:T(8,128)(2,1)} %param.25) | copy-start | bytes 786436
  7.2 47.9 %all-gather.15.cloned.1.call-start = ((), (), s32[]{:S(2)}) async-start(), calls=%async_computation.15 | async-start | bytes 1114112 | tf_op jit(solution)/shard_map/all_gather | solution.py:82
  7.9 91.3 %all-gather.13.cloned.1.call-start = ((), (), s32[]{:S(2)}) async-start(), calls=%async_computation.14 | async-start | bytes 1114112 | tf_op jit(solution)/shard_map/all_gather | solution.py:81
  8.7 137.7 %all-gather.11.cloned.1.call-start = ((), (), s32[]{:S(2)}) async-start(), calls=%async_computation.13 | async-start | bytes 2228224 | tf_op jit(solution)/shard_map/all_gather | solution.py:80
  9.4 184.2 %all-gather.17.cloned.1.call-start = ((), (), s32[]{:S(2)}) async-start(), calls=%async_computation.16 | async-start | bytes 2228224 | tf_op jit(solution)/shard_map/all_gather | solution.py:85
  10.0 230.1 %all-gather.21.cloned.1.call-start = ((), (), s32[]{:S(2)}) async-start(), calls=%async_computation.18 | async-start | bytes 2506752 | tf_op jit(solution)/shard_map/all_gather | solution.py:87
  148.4 0.8 copy-start.13
  149.3 0.8 copy-start.6
  149.4 1.8 copy-start.15
  152.0 14.7 %all-to-all-start = ((bf16[1,128,8,256]{1,3,0,2:T(8,128)(2,1)}), bf16[1,128,8,256]{1,3,0,2:T(8,128)(2,1)S(1)}, u32[]{:S(2)}, u32[]{:S(2)}) async-start(bf16[1,128,8,256]{1,3,0,2:T(8,128)(2,1)} %maximum_bitcast_fusion), calls=%async_computation | async-start | bytes 1048576 | tf_op jit(solution)/shard_map/all_to_all | solution.py:149
  166.8 4.2 copy-start.19
  166.8 2.1 copy-start.30
  166.9 2.1 copy-start.32
  170.0 2.1 copy-start
  178.4 11.3 all-to-all-start.1
  183.1 80.5 %all-gather.19.cloned.1.call-start = ((), (), s32[]{:S(2)}) async-start(), calls=%async_computation.17 | async-start | bytes 1310720 | tf_op jit(solution)/shard_map/all_gather | solution.py:184
  193.6 3.9 copy-start.20
  195.8 0.8 copy-start.10
  197.5 112.2 %all-gather.23.cloned.1.call-start = ((), (), s32[]{:S(2)}) async-start(), calls=%async_computation.19 | async-start | bytes 2506752 | tf_op jit(solution)/shard_map/all_gather | solution.py:88
  198.2 134.5 %all-gather.27.cloned.1.call-start = ((), (), s32[]{:S(2)}) async-start(), calls=%async_computation.30 | async-start | bytes 1310720 | tf_op jit(solution)/shard_map/all_gather | solution.py:185
  199.0 179.9 %all-gather.25.cloned.1.call-start = ((), (), s32[]{:S(2)}) async-start(), calls=%async_computation.20 | async-start | bytes 2506752 | tf_op jit(solution)/shard_map/all_gather | solution.py:89
  199.7 229.9 %reduce-scatter.12.cloned.1.call-start = ((), (), s32[]{:S(2)}) async-start(), calls=%async_computation.22 | async-start | bytes 2621440 | tf_op jit(solution)/shard_map/reduce_scatter | solution.py:207
  378.9 6.7 copy-start.37
  385.6 1.6 copy-start.28
  385.6 1.6 copy-start.27
  385.6 2.5 copy-start.38
  391.0 79.3 %reduce-scatter.10.cloned.1.call-start = ((), (), s32[]{:S(2)}) async-start(), calls=%async_computation.21 | async-start | bytes 2621440 | tf_op jit(solution)/shard_map/reduce_scatter | solution.py:192
  396.0 155.3 %reduce-scatter.22.cloned.1.call-start = ((), (), s32[]{:S(2)}) async-start(), calls=%async_computation.27 | async-start | bytes 5013504 | tf_op jit(solution)/shard_map/reduce_scatter | solution.py:323
  401.4 229.7 %reduce-scatter.24.cloned.1.call-start = ((), (), s32[]{:S(2)}) async-start(), calls=%async_computation.28 | async-start | bytes 5013504 | tf_op jit(solution)/shard_map/reduce_scatter | solution.py:324
  407.0 305.1 %reduce-scatter.26.cloned.1.call-start = ((), (), s32[]{:S(2)}) async-start(), calls=%async_computation.29 | async-start | bytes 5013504 | tf_op jit(solution)/shard_map/reduce_scatter | solution.py:325
  412.4 57.8 %copy-start.29 = (bf16[1,128,1024]{2,1,0:T(8,128)(2,1)S(1)}, bf16[1,128,1024]{2,1,0:T(8,128)(2,1)}, u32[]{:S(2)}) copy-start(bf16[1,128,1024]{2,1,0:T(8,128)(2,1)} %param.26) | copy-start | bytes 786436
  470.3 2.5 copy-start.5
  472.7 0.8 copy-start.8
  474.4 10.4 all-to-all-start.2
  478.4 322.6 %reduce-scatter.16.cloned.1.call-start = ((), (), s32[]{:S(2)}) async-start(), calls=%async_computation.24 | async-start | bytes 2228224 | tf_op jit(solution)/shard_map/reduce_scatter | solution.py:319
  494.1 1.0 copy-start.31
  494.1 2.8 copy-start.1
  495.1 3.6 copy-start.3
  525.9 10.6 copy-start.12
  526.3 2.0 copy-start.26
  528.3 337.7 %reduce-scatter.18.cloned.1.call-start = ((), (), s32[]{:S(2)}) async-start(), calls=%async_computation.25 | async-start | bytes 2228224 | tf_op jit(solution)/shard_map/reduce_scatter | solution.py:320
  528.6 1.9 copy-start.24
  528.6 2.0 copy-start.9
  528.6 2.0 copy-start.21
  530.5 415.7 %reduce-scatter.20.cloned.1.call-start = ((), (), s32[]{:S(2)}) async-start(), calls=%async_computation.26 | async-start | bytes 4456448 | tf_op jit(solution)/shard_map/reduce_scatter | solution.py:321
  533.3 1.0 copy-start.7
  533.3 2.1 copy-start.16
  533.4 493.5 %reduce-scatter.14.cloned.1.call-start = ((), (), s32[]{:S(2)}) async-start(), calls=%async_computation.23 | async-start | bytes 4456448 | tf_op jit(solution)/shard_map/reduce_scatter | solution.py:318
  536.9 5.0 copy-start.11
  536.9 3.1 copy-start.14
  538.0 2.1 copy-start.23
  541.9 2.8 copy-start.22
  544.7 3.1 copy-start.4
  544.8 529.0 %all-reduce.15.cloned.1.call-start = ((), (), s32[]{:S(2)}) async-start(), calls=%async_computation.32 | async-start | bytes 1769472 | tf_op jit(solution)/shard_map/psum | solution.py:330
  547.9 1.9 copy-start.18
  549.8 162.4 %copy-start.17 = (bf16[1024,512]{1,0:T(8,128)(2,1)S(1)}, bf16[1024,512]{1,0:T(8,128)(2,1)}, u32[]{:S(2)}) copy-start(bf16[1024,512]{1,0:T(8,128)(2,1)} %all-gather.15.cloned.1.call-done) | copy-start | bytes 3145732
  549.8 162.4 %copy-start.25 = (bf16[1,128,8,64]{1,3,2,0:T(8,128)(2,1)S(1)}, bf16[1,128,8,64]{1,3,2,0:T(8,128)(2,1)}, u32[]{:S(2)}) copy-start(bf16[1,128,8,64]{1,3,2,0:T(8,128)(2,1)} %copy-done.24) | copy-start | bytes 393220
  551.3 161.6 %copy-start.35 = (f32[16,4]{1,0:T(8,128)S(1)}, f32[16,4]{1,0:T(8,128)}, u32[]{:S(2)}) copy-start(f32[16,4]{1,0:T(8,128)} %reshape.900) | copy-start | bytes 772
  551.3 161.6 %copy-start.36 = (f32[16,4]{1,0:T(8,128)S(1)}, f32[16,4]{1,0:T(8,128)}, u32[]{:S(2)}) copy-start(f32[16,4]{1,0:T(8,128)} %reshape.899) | copy-start | bytes 772
  712.1 424.8 %all-reduce.13.cloned.1.call-start = ((), (), s32[]{:S(2)}) async-start(), calls=%async_computation.31 | async-start | bytes 1572864 | tf_op jit(solution)/shard_map/psum | solution.py:327
  1073.8 71.3 %copy-start.34 = (f32[64,1152]{1,0:T(8,128)S(1)}, f32[64,1152]{1,0:T(8,128)}, u32[]{:S(2)}) copy-start(f32[64,1152]{1,0:T(8,128)} %get-tuple-element.141) | copy-start | bytes 884740
  1073.8 72.0 %copy-start.33 = (f32[1152,64]{0,1:T(8,128)S(1)}, f32[1152,64]{0,1:T(8,128)}, u32[]{:S(2)}) copy-start(f32[1152,64]{0,1:T(8,128)} %get-tuple-element.142) | copy-start | bytes 884740
Sparse Core Ops, SparseCore 0:
  10.2 44.8 all-gather.14
  57.2 41.9 all-gather.12
  101.4 44.9 all-gather.10
  148.3 44.5 all-gather.16
  194.9 45.1 all-gather.20
  242.2 21.2 all-gather.18
  265.8 43.9 all-gather.22
  311.4 21.2 all-gather.26
  334.9 43.9 all-gather.24
  391.1 38.4 reduce-scatter.11
  432.5 37.7 reduce-scatter.9
  473.5 76.4 reduce-scatter.21
  553.3 77.7 reduce-scatter.23
  634.2 77.8 reduce-scatter.25
  715.2 73.5 reduce-scatter.15
  792.3 73.6 reduce-scatter.17
  869.2 76.9 reduce-scatter.19
  949.8 77.0 reduce-scatter.13
  1029.5 44.2 all-reduce.14
  1076.1 60.7 all-reduce.12
where the time goes:
time: 1160 us; the launch traced here: 1150 us
  waiting for transfers between devices  834 us (72%)
  blocking collectives  135 us (12%)
  matrix products  79.6 us (7%)
  local copies, waits for them, and re-layouts  43.5 us (4%)
  other arithmetic  28.4 us (2%)
  between operations  17 us (1%)
  starting transfers between devices  16 us (1%)
    unnamed x2, blocking collectives  94.6 us
    reduce_scatter x1, waiting for transfers between devices, on_device(): lax.psum_scatter(down_sum, 'shard', scatter_dimension=1, tiled=True)  81.1 us
    reduce_scatter x1, waiting for transfers between devices, on_device(): lax.psum_scatter(query_sum, 'shard', scatter_dimension=0, tiled=True)  80.6 us
    reduce_scatter x1, waiting for transfers between devices, on_device(): lax.psum_scatter(out_sum, 'shard', scatter_dimension=0, tiled=True)  80.2 us
    reduce_scatter x1, waiting for transfers between devices, on_device(): lax.psum_scatter(up_sum, 'shard', scatter_dimension=0, tiled=True)  79.7 us
    reduce_scatter x1, waiting for transfers between devices, on_device(): lax.psum_scatter(value_sum, 'shard', scatter_dimension=0, tiled=True)  65 us
    psum x1, waiting for transfers between devices, on_device(): lax.psum((query_part, key_part, value_part, out_part, gain_part), ('conte...  63.1 us
    all_gather x1, waiting for transfers between devices, on_device(): lax.all_gather(down_weight, 'shard', axis=1, tiled=True)  46.2 us
  transfers between devices with their start and end apart: 23, of which 20 were waited for; matrix products, arithmetic and copies ran while one was open for 11% of the time, Pallas kernels for 0%

commit v1 on v0

v1 whole, which is shorter than its diff:
```python
import jax
import jax.numpy as jnp
from jax import lax
from jax.sharding import PartitionSpec as P

epsilon = 1e-05
rope_base = 1000000.0
masked_score = -1e30
line = ("context", "tensor")
f32 = jnp.float32
bf16 = jnp.bfloat16


def rope_tables(positions, head_dim):
    exponent = jnp.arange(0, head_dim, 2).astype(f32) / head_dim
    frequency = 1.0 / rope_base**exponent
    angle = positions.astype(f32)[:, None] * frequency[None, :]
    angle = jnp.concatenate([angle, angle], axis=-1)
    return (jnp.cos(angle), jnp.sin(angle))


def rotate(value, cosine, sine):
    half = value.shape[-1] // 2
    turned = jnp.concatenate([-value[..., half:], value[..., :half]], axis=-1)
    return value * cosine + turned * sine


def rotate_back(grad_value, cosine, sine):
    half = grad_value.shape[-1] // 2
    moved = grad_value * sine
    turned = jnp.concatenate([moved[..., half:], -moved[..., :half]], axis=-1)
    return grad_value * cosine + turned


def rms_parts(value):
    inverse = lax.rsqrt(jnp.mean(value * value, axis=-1, keepdims=True) + epsilon)
    return (value * inverse, inverse)


def norm_back(grad_value, normed, inverse, gain):
    scaled = grad_value * gain
    return inverse * (scaled - normed * jnp.mean(scaled * normed, axis=-1, keepdims=True))


def dot(a, b):
    return jnp.dot(a, b, preferred_element_type=f32)


def dot_nt(a, b):
    return lax.dot_general(a, b, (((1,), (1,)), ((), ())), preferred_element_type=f32)


def dot_tn(a, b):
    return lax.dot_general(a, b, (((0,), (0,)), ((), ())), preferred_element_type=f32)


def swap(value, bits):
    return lax.ppermute(value, line, [(i, i ^ bits) for i in range(8)])


def flips():
    tensor = lax.axis_index("tensor")
    return (tensor % 2 == 1, lax.axis_index("context") == 1, tensor // 2 == 1)


def exchange_bits(value):
    for dim, flag in enumerate(flips()):
        value = jnp.where(flag, jnp.flip(value, dim), value)
    return value


def to_places(value):
    n, w = value.shape[-2:]
    value = exchange_bits(value.reshape(2, 2, 2, n, w))
    return jnp.moveaxis(value, 0, 2).reshape(8 * n, w)


def to_partners(value):
    n, w = value.shape[0] // 8, value.shape[1]
    value = jnp.moveaxis(value.reshape(2, 2, 2, n, w), 2, 0)
    return exchange_bits(value).reshape(2, 4, n, w)


def line_gather(block):
    mine = jnp.stack([block, swap(block, 2), swap(block, 4), swap(block, 6)])
    other = swap(mine, 1)
    return jnp.stack([mine, other])


def line_reduce(parts):
    low = parts.astype(bf16)
    summed = parts[0] + swap(low[1], 1).astype(f32)
    sent = summed.astype(bf16)
    total = summed[0]
    for chip in (2, 1, 3):
        total = total + swap(sent[chip], 2 * chip).astype(f32)
    return total


def line_turn(parts):
    got = swap(parts[1], 1)
    both = jnp.stack([parts[0], got], axis=1)
    arrived = [both[0]] + [swap(both[chip], 2 * chip) for chip in (1, 2, 3)]
    return jnp.stack(arrived, axis=1)


def on_device(
    tokens,
    cotangent,
    attention_gain,
    query_weight,
    key_weight,
    value_weight,
    query_gain,
    key_gain,
    out_weight,
    feed_gain,
    gate_weight,
    up_weight,
    down_weight,
):
    _, piece, width = tokens.shape
    shard_count = lax.axis_size("shard")
    rows = query_weight.shape[0]
    head_dim = query_gain.shape[0] * shard_count
    length = piece * 8
    context = lax.axis_index("context")
    place = context * lax.axis_size("tensor") + lax.axis_index("tensor")
    heads_width = query_weight.shape[1] // 8
    half = gate_weight.shape[1] // 2
    scale = head_dim ** (-0.5)

    def my_half(value, axis):
        return lax.dynamic_slice_in_dim(value, context * half, half, axis)

    feed_pack = jnp.concatenate(
        [my_half(gate_weight, 1), my_half(up_weight, 1), my_half(down_weight, 0).T], axis=1
    )
    feed_full = lax.all_gather(feed_pack, "shard", axis=0, tiled=True)

    def mine(value, size):
        return lax.dynamic_slice_in_dim(value, place * size, size, 1)

    extra = jnp.zeros((16, 3 * heads_width), bf16)
    gain_rows = jnp.stack([attention_gain, feed_gain])
    extra = extra.at[:2, :rows].set(gain_rows)
    extra = extra.at[2, : head_dim // shard_count].set(query_gain)
    extra = extra.at[3, : head_dim // shard_count].set(key_gain)
    pack = jnp.concatenate(
        [
            mine(query_weight, heads_width),
            mine(key_weight, head_dim),
            mine(value_weight, head_dim),
            mine(out_weight, heads_width),
        ],
        axis=1,
    )
    pack = jnp.concatenate([pack, extra], axis=0)
    pack_all = lax.all_to_all(
        jnp.broadcast_to(pack[None], (shard_count,) + pack.shape), "shard", 0, 0, tiled=True
    )
    weights = pack_all[:, :rows].reshape(width, 3 * heads_width)
    qkv_weight = weights[:, : 2 * heads_width]
    out_columns = weights[:, 2 * heads_width :]
    gains = pack_all[:, rows:].astype(f32)
    gain_first = gains[:, 0, :rows].reshape(-1)
    gain_second = gains[:, 1, :rows].reshape(-1)
    gain_query = gains[:, 2, : head_dim // shard_count].reshape(-1)
    gain_key = gains[:, 3, : head_dim // shard_count].reshape(-1)

    token_rows = tokens.reshape(piece, width)
    seed_rows = cotangent.reshape(piece, width)
    tokens_all = line_gather(token_rows).reshape(length, width)
    normed_all, _ = rms_parts(tokens_all.astype(f32))
    mixer_input = (normed_all * gain_first).astype(bf16)
    raw = dot(mixer_input, qkv_weight)
    raw = to_places(raw.reshape(2, 4, piece, 2 * heads_width))
    cosine, sine = rope_tables(jnp.arange(length), head_dim)
    query_raw = raw[:, :heads_width].reshape(length, 2, head_dim)
    key_raw = raw[:, heads_width : heads_width + head_dim]
    values = raw[:, heads_width + head_dim :].astype(bf16)
    normed_query, inverse_query = rms_parts(query_raw)
    normed_key, inverse_key = rms_parts(key_raw)
    queries = rotate(normed_query * gain_query, cosine[:, None], sine[:, None]).astype(bf16)
    keys = rotate(normed_key * gain_key, cosine, sine).astype(bf16)
    out_partner = line_gather(out_columns)

    block = 512
    starts = list(range(0, length, block))

    def scores(start):
        stop = start + block
        score = (
            jnp.einsum(
                "qhd,kd->hqk", queries[start:stop], keys[:stop], preferred_element_type=f32
            )
            * scale
        )
        allowed = jnp.arange(stop)[None, :] <= (start + jnp.arange(block))[:, None]
        return jnp.where(allowed, score, masked_score)

    results = []
    log_sums = []
    for start in starts:
        score = scores(start)
        peak = jnp.max(score, axis=-1, keepdims=True)
        raised = jnp.exp(score - peak)
        total = jnp.sum(raised, axis=-1, keepdims=True)
        chance = (raised / total).astype(bf16)
        results.append(
            jnp.einsum(
                "hqk,kd->qhd", chance, values[: start + block], preferred_element_type=f32
            ).astype(bf16)
        )
        log_sums.append(peak + jnp.log(total))
    attended_heads = jnp.concatenate(results, axis=0).reshape(length, heads_width)
    attended_turned = line_turn(to_partners(attended_heads))
    attended = to_places(attended_turned).reshape(8, piece, heads_width)
    attended = jnp.moveaxis(attended, 0, 1).reshape(piece, width)

    out_wide = jnp.moveaxis(out_partner.reshape(8, width, heads_width), 0, 1).reshape(width, width)
    branch = dot(attended, out_wide).reshape(piece, 8, heads_width)
    branch = to_places(jnp.moveaxis(branch, 1, 0).reshape(2, 4, piece, heads_width))
    branch = jnp.moveaxis(branch.reshape(8, piece, heads_width), 0, 1).reshape(piece, width)
    mixed = token_rows.astype(f32) + branch
    normed_second, inverse_second = rms_parts(mixed)
    feed_input = (normed_second * gain_second).astype(bf16)

    seed_all = line_gather(seed_rows).reshape(length, width)
    feed_all = line_gather(feed_input).reshape(length, width)
    gate_full = feed_full[:, :half]
    up_full = feed_full[:, half : 2 * half]
    down_full = feed_full[:, 2 * half :]
    grad_hidden = dot(seed_all, down_full)
    gate = dot(feed_all, gate_full)
    upward = dot(feed_all, up_full)
    squashed = jax.nn.sigmoid(gate)
    activated = gate * squashed
    hidden = (activated * upward).astype(bf16)
    grad_gate = (grad_hidden * upward * squashed * (1.0 + gate * (1.0 - squashed))).astype(bf16)
    grad_up = (grad_hidden * activated).astype(bf16)
    grad_feed = dot_nt(grad_gate, gate_full) + dot_nt(grad_up, up_full)
    grad_feed = line_reduce(grad_feed.reshape(2, 4, piece, width))
    feed_rows = line_reduce(dot_nt(hidden, down_full).reshape(2, 4, piece, width))
    output = (mixed + feed_rows).astype(bf16).reshape(1, piece, width)

    feed_sums = jnp.concatenate(
        [dot_tn(feed_all, grad_gate), dot_tn(feed_all, grad_up), dot_tn(seed_all, hidden)], axis=1
    ).astype(bf16)
    feed_parts = lax.all_to_all(
        feed_sums.reshape(shard_count, rows, 3 * half), "shard", 0, 0, tiled=True
    )
    feed_total = jnp.sum(feed_parts.astype(f32), axis=0)
    feed_other = swap(feed_total.astype(bf16), 4).astype(f32)
    first = jnp.where(context == 0, feed_total, feed_other)
    second = jnp.where(context == 0, feed_other, feed_total)

    def joined(index):
        span = slice(index * half, (index + 1) * half)
        return jnp.concatenate([first[:, span], second[:, span]], axis=1)

    gate_part = joined(0)
    up_part = joined(1)
    down_part = joined(2).T

    grad_mixed = seed_rows.astype(f32) + norm_back(
        grad_feed, normed_second, inverse_second, gain_second
    )
    grad_branch = grad_mixed.astype(bf16)
    branch_all = line_gather(grad_branch).reshape(length, width)
    out_rows = lax.dynamic_slice_in_dim(out_partner, place * heads_width, heads_width, 2)
    out_rows = to_places(out_rows).reshape(8, heads_width, heads_width)
    out_rows = jnp.moveaxis(out_rows, 0, 1).reshape(heads_width, width)
    grad_attended = dot_nt(branch_all, out_rows).astype(bf16)
    attended_partner = to_partners(attended_heads).reshape(length, heads_width)
    out_sum = dot_tn(attended_partner, branch_all).astype(bf16)
    out_sum = jnp.moveaxis(out_sum.reshape(heads_width, 8, heads_width), 1, 0)
    out_turned = line_turn(to_partners(out_sum.reshape(8 * heads_width, heads_width)))
    out_sum = to_places(out_turned)
    grad_heads = to_places(grad_attended.reshape(2, 4, piece, heads_width)).reshape(
        length, 2, head_dim
    )

    key_grad = jnp.zeros((length, head_dim), f32)
    value_grad = jnp.zeros((length, head_dim), f32)
    query_blocks = []
    for index, start in enumerate(starts):
        stop = start + block
        query_block = queries[start:stop]
        grad_block = grad_heads[start:stop]
        chance_full = jnp.exp(scores(start) - log_sums[index])
        grad_chance = jnp.einsum(
            "qhd,kd->hqk", grad_block, values[:stop], preferred_element_type=f32
        )
        inner = jnp.sum(chance_full * grad_chance, axis=-1, keepdims=True)
        grad_score = (chance_full * (grad_chance - inner)).astype(bf16)
        query_blocks.append(
            jnp.einsum("hqk,kd->qhd", grad_score, keys[:stop], preferred_element_type=f32) * scale
        )
        key_grad = key_grad.at[:stop].add(
            jnp.einsum("hqk,qhd->kd", grad_score, query_block, preferred_element_type=f32) * scale
        )
        value_grad = value_grad.at[:stop].add(
            jnp.einsum(
                "hqk,qhd->kd", chance_full.astype(bf16), grad_block, preferred_element_type=f32
            )
        )

    def rounded(value):
        return value.astype(bf16).astype(f32)

    grad_query_normed = rotate_back(
        rounded(jnp.concatenate(query_blocks, axis=0)), cosine[:, None], sine[:, None]
    )
    grad_key_normed = rotate_back(rounded(key_grad), cosine, sine)
    query_gain_sum = jnp.sum(grad_query_normed * normed_query, axis=(0, 1))
    key_gain_sum = jnp.sum(grad_key_normed * normed_key, axis=0)
    grad_raw = jnp.concatenate(
        [
            norm_back(grad_query_normed, normed_query, inverse_query, gain_query).reshape(
                length, heads_width
            ),
            norm_back(grad_key_normed, normed_key, inverse_key, gain_key),
            value_grad,
        ],
        axis=1,
    ).astype(bf16)
    grad_raw = to_partners(grad_raw).reshape(length, 2 * heads_width)
    grad_mixer = line_reduce(dot_nt(grad_raw, qkv_weight).reshape(2, 4, piece, width))
    qkv_sum = dot_tn(mixer_input, grad_raw).astype(bf16)
    normed_first, inverse_first = rms_parts(token_rows.astype(f32))
    input_gradient = (
        (grad_mixed + norm_back(grad_mixer, normed_first, inverse_first, gain_first))
        .astype(bf16)
        .reshape(1, piece, width)
    )

    per_shard = head_dim // shard_count
    last = jnp.zeros((shard_count, 16, 3 * heads_width), bf16)

    def low_pair(value):
        high = value.astype(bf16)
        return jnp.stack([high, (value - high.astype(f32)).astype(bf16)])

    gain_pairs = jnp.concatenate([low_pair(query_gain_sum), low_pair(key_gain_sum)])
    gain_pairs = jnp.moveaxis(gain_pairs.reshape(4, shard_count, per_shard), 0, 1)
    last = last.at[:, :4, :per_shard].set(gain_pairs)
    sums = jnp.concatenate([qkv_sum, out_sum], axis=1).reshape(shard_count, rows, 3 * heads_width)
    sums = jnp.concatenate([sums, last], axis=1)
    parts = lax.all_to_all(sums, "shard", 0, 0, tiled=True)
    total = jnp.sum(parts.astype(f32), axis=0)
    attention_total = total[:rows]
    gain_total = total[rows : rows + 4, :per_shard]
    gain_total = gain_total.reshape(2, 2, per_shard).sum(1)

    def product_sum(weight, grad):
        return jnp.sum(weight.astype(f32) * grad, axis=1)

    first_partial = product_sum(pack[:rows, : 2 * heads_width], attention_total[:, : 2 * heads_width])
    feed_partial = product_sum(feed_pack[:, : 2 * half], feed_total[:, : 2 * half])
    tail = jnp.zeros((16, 3 * heads_width), f32)
    tail = tail.at[0, :rows].set(first_partial).at[1, :rows].set(feed_partial)
    tail = tail.at[2:4, :per_shard].set(gain_total)
    final = jnp.concatenate([attention_total, tail], axis=0)
    final_all = to_places(line_gather(final.astype(bf16))).reshape(8, rows + 16, 3 * heads_width)
    final_all = final_all.astype(f32)

    def columns(low, high):
        return jnp.moveaxis(final_all[:, :rows, low:high], 0, 1).reshape(rows, -1)

    query_part = columns(0, heads_width)
    key_part = columns(heads_width, heads_width + head_dim)
    value_part = columns(heads_width + head_dim, 2 * heads_width)
    out_part = columns(2 * heads_width, 3 * heads_width)
    tails = jnp.sum(final_all[:, rows:], axis=0)
    first_gain_grad = tails[0, :rows] / attention_gain.astype(f32)
    feed_gain_grad = tails[1, :rows] / feed_gain.astype(f32)
    query_gain_grad = tails[2, :per_shard]
    key_gain_grad = tails[3, :per_shard]
    return (
        output,
        input_gradient,
        first_gain_grad,
        query_part,
        key_part,
        value_part,
        query_gain_grad,
        key_gain_grad,
        out_part,
        feed_gain_grad,
        gate_part,
        up_part,
        down_part,
    )


def solution(mesh):
    tokens = P("shard", ("context", "tensor"), None)
    rows = P("shard", None)
    weights = (P("shard"), rows, rows, rows, P("shard"), P("shard"), rows, P("shard")) + (
        P("shard", "tensor"),
        P("shard", "tensor"),
        P("tensor", "shard"),
    )
    placed = (tokens, tokens) + weights
    return jax.shard_map(
        on_device, mesh=mesh, in_specs=placed, out_specs=placed, check_vma=False
    )
```

time: 1160 us -> 433 us (0.37)
  waiting for transfers between devices: 834 us -> 65.6 us
  blocking collectives: 135 us -> 0 us
  local copies, waits for them, and re-layouts: 43.5 us -> 137 us
  starting transfers between devices: 16 us -> 71.3 us
  other arithmetic: 28.4 us -> 77.4 us
  matrix products: 79.6 us -> 56.7 us
    reduce_scatter x9 -> x0, waiting for transfers between devices: 443 us -> none  [the longest x1 81.1 us: on_device(): lax.psum_scatter(down_sum, 'shard', scatter_dimension=1, tiled=True)]
    all_gather x9 -> x1, waiting for transfers between devices: 257 us -> 0.01 us  [on_device(): feed_full = lax.all_gather(feed_pack, 'shard', axis=0, tiled=True)]
    psum x2 -> x0, waiting for transfers between devices: 109 us -> none  [the longest x1 63.1 us: on_device(): lax.psum((query_part, key_part, value_part, out_part, gain_part), ('conte...]
    unnamed x2 -> x0, blocking collectives: 94.6 us -> none
    ppermute x0 -> x45, starting transfers between devices: none -> 52.3 us  [swap(): return lax.ppermute(value, line, [(i, i ^ bits) for i in range(8)])]
    ppermute x0 -> x45, waiting for transfers between devices: none -> 49.8 us  [swap(): return lax.ppermute(value, line, [(i, i ^ bits) for i in range(8)])]
    psum x1 -> x0, blocking collectives: 27.9 us -> none  [on_device(): lax.psum((query_part, key_part, value_part, out_part, gain_part), ('conte...]
    another operation x2 -> x20, other arithmetic: 1.76 us -> 26.4 us  [the longest x11 22.9 us: line_gather(): return jnp.stack([mine, other])]
  transfers between devices with their start and end apart: 23 -> 49, of which waited for: 20 -> 15; matrix products, arithmetic and copies ran while one was open for 11% -> 54% of each run, Pallas kernels for 0% -> 0%
where the time goes in v1:
time: 433 us; the launch traced here: 424 us
  local copies, waits for them, and re-layouts  137 us (32%)
  other arithmetic  77.4 us (18%)
  starting transfers between devices  71.3 us (16%)
  waiting for transfers between devices  65.6 us (15%)
  matrix products  56.7 us (13%)
  between operations  16.4 us (4%)
    ppermute x45, starting transfers between devices, swap(): return lax.ppermute(value, line, [(i, i ^ bits) for i in range(8)])  52.3 us
    ppermute x45, waiting for transfers between devices, swap(): return lax.ppermute(value, line, [(i, i ^ bits) for i in range(8)])  49.8 us
    another operation x11, other arithmetic, line_gather(): return jnp.stack([mine, other])  22.9 us
    unnamed x205, local copies, waits for them, and re-layouts  20.2 us
    another operation x5, local copies, waits for them, and re-layouts, line_gather(): return jnp.stack([mine, other])  15.2 us
    dot_general x5, matrix products, dot(): return jnp.dot(a, b, preferred_element_type=f32)  14.3 us
    squeeze x6, local copies, waits for them, and re-layouts, line_reduce(): summed = parts[0] + swap(low[1], 1).astype(f32)  14 us
    dot_general x5, matrix products, dot_tn(): lax.dot_general(a, b, (((0,), (0,)), ((), ())), preferred_element_type=f32)  12.5 us
  transfers between devices with their start and end apart: 49, of which 15 were waited for; matrix products, arithmetic and copies ran while one was open for 54% of the time, Pallas kernels for 0%

profile of v1, /device:TPU:1, one launch (start us, length us, event | category | flops | bytes accessed | tf_op | source)
XLA Modules:
  0.0 424.3 jit_solution(12564181131142449180)
XLA Ops:
  8.4 3.7 collective-permute-start
  14.7 2.4 collective-permute-start.20
  22.4 7.8 %all-to-all-start = ((bf16[16,80,384]{2,1,0:T(8,128)(2,1)}), bf16[16,80,384]{2,1,0:T(8,128)(2,1)}, u32[]{:S(2)}, u32[]{:S(2)}) async-start(bf16[16,80,384]{2,1,0:T(8,128)(2,1)} %broadcast_in_dim.20), calls=%async_computation | async-start | bytes 1966080 | tf_op jit(solution)/shard_map/all_to_all | solution.py:159
  33.5 2.4 collective-permute-start.3
  38.5 5.9 %all-to-all-done = bf16[16,80,384]{2,1,0:T(8,128)(2,1)} async-done(((bf16[16,80,384]{2,1,0:T(8,128)(2,1)}), bf16[16,80,384]{2,1,0:T(8,128)(2,1)}, u32[]{:S(2)}, u32[]{:S(2)}) %all-to-all-start) | async-done | bytes 983072 | tf_op jit(solution)/shard_map/all_to_all | solution.py:159
  77.3 4.2 collective-permute-start.4
  81.5 2.6 fusion.150
  84.2 2.1 collective-permute-start.5
  87.6 2.6 fusion.148
  92.7 3.1 pad_maximum_fusion
  95.9 3.9 copy.376
  99.8 3.1 fusion.15
  107.9 2.1 collective-permute-start.12
  111.4 5.0 %collective-permute-done.12 = bf16[128,1024]{0,1:T(8,128)(2,1)S(1)} collective-permute-done((bf16[128,1024]{0,1:T(8,128)(2,1)S(1)}, bf16[128,1024]{0,1:T(8,128)(2,1)S(1)}, u32[]{:S(2)}, u32[]{:S(2)}) %collective-permute-start.12) | collective-permute-done | bytes 262176 | tf_op jit(solution)/shard_map/ppermute | solution.py:58
  116.4 6.1 %collective-permute-done.13 = bf16[128,1024]{0,1:T(8,128)(2,1)S(1)} collective-permute-done((bf16[128,1024]{0,1:T(8,128)(2,1)S(1)}, bf16[128,1024]{0,1:T(8,128)(2,1)S(1)}, u32[]{:S(2)}, u32[]{:S(2)}) %collective-permute-start.13) | collective-permute-done | bytes 262176 | tf_op jit(solution)/shard_map/ppermute | solution.py:58
  126.6 3.1 pad_maximum_fusion.3
  129.8 4.4 %copy.390 = bf16[2,4,128,1024]{3,2,1,0:T(8,128)(2,1)} copy(bf16[2,4,128,1024]{2,3,1,0:T(8,128)(2,1)} %pad_maximum_fusion.3) | data formatting | bytes 4194304 | tf_op jit(solution)/shard_map/stack | solution.py:87
  134.2 3.9 copy.430
  140.0 2.0 copy.402
  142.9 2.1 copy.406
  145.0 3.5 fusion.2
  148.5 4.0 copy.416
  156.3 2.8 pad_maximum_fusion.2
  159.1 4.0 copy.385
  163.1 4.2 fusion.44
  168.9 3.6 multiply_convert_fusion.1
  174.3 2.2 convolution_add_fusion
  179.7 2.4 copy.391
  185.9 3.9 copy.429
  189.8 3.2 slice.575
  193.0 2.9 copy.392
  195.9 3.5 fusion.41
  202.6 2.3 copy.386
  205.4 2.4 fusion.154
  208.6 2.3 collective-permute-start.26
  211.7 2.9 convolution_convert_fusion.1
  215.9 7.2 %collective-permute-done.26 = bf16[128,1024]{0,1:T(8,128)(2,1)S(1)} collective-permute-done((bf16[128,1024]{0,1:T(8,128)(2,1)S(1)}, bf16[128,1024]{0,1:T(8,128)(2,1)S(1)}, u32[]{:S(2)}, u32[]{:S(2)}) %collective-permute-start.26) | collective-permute-done | bytes 262176 | tf_op jit(solution)/shard_map/ppermute | solution.py:58
  231.2 2.9 convolution_convert_fusion.2
  235.9 4.0 collective-permute-done.29
  240.0 3.3 collective-permute-done.30
  245.3 2.9 convolution_convert_fusion
  249.6 7.1 %concatenate.166 = bf16[16,64,1728]{2,1,0:T(8,128)(2,1)} concatenate(bf16[16,64,576]{2,1,0:T(8,128)(2,1)} %convolution_convert_fusion.2, bf16[16,64,576]{2,1,0:T(8,128)(2,1)} %convolution_convert_fusion.1, bf16[16,64,576]{2,1,0:T(8,128)(2,1)} %convolution_convert_fusion), dimensions={2} | concatenate | bytes 7077888 | tf_op jit(solution)/shard_map/concatenate | solution.py:247
  256.7 4.5 %all-to-all-start.2 = ((bf16[16,64,1728]{2,1,0:T(8,128)(2,1)}), bf16[16,64,1728]{2,1,0:T(8,128)(2,1)}, u32[]{:S(2)}, u32[]{:S(2)}) async-start(bf16[16,64,1728]{2,1,0:T(8,128)(2,1)} %concatenate.166), calls=%async_computation.2 | async-start | bytes 7340032 | tf_op jit(solution)/shard_map/all_to_all | solution.py:250
  261.2 2.9 copy.387
  264.2 3.5 fusion.155
  269.2 2.7 pad_maximum_fusion.4
  271.9 4.2 copy.393
  276.1 2.3 convolution_convert_fusion.5
  289.2 3.3 fusion.3
  297.1 2.0 copy.403
  302.5 2.4 fusion.143
  307.5 3.8 fusion.50
  324.2 3.3 convolution_convert_fusion.3
  337.0 2.7 convert_reduce_fusion
  341.4 6.6 %all-to-all-start.1 = ((bf16[16,80,384]{2,1,0:T(8,128)(2,1)}), bf16[16,80,384]{2,1,0:T(8,128)(2,1)}, u32[]{:S(2)}, u32[]{:S(2)}) async-start(bf16[16,80,384]{2,1,0:T(8,128)(2,1)} %fusion.64), calls=%async_computation.1 | async-start | bytes 1966080 | tf_op jit(solution)/shard_map/all_to_all | solution.py:350
  351.5 2.5 fusion.152
  354.0 9.9 %all-to-all-done.1 = bf16[16,80,384]{2,1,0:T(8,128)(2,1)} async-done(((bf16[16,80,384]{2,1,0:T(8,128)(2,1)}), bf16[16,80,384]{2,1,0:T(8,128)(2,1)}, u32[]{:S(2)}, u32[]{:S(2)}) %all-to-all-start.1) | async-done | bytes 983072 | tf_op jit(solution)/shard_map/all_to_all | solution.py:350
  372.6 2.8 collective-permute-start.34
  378.1 7.2 %collective-permute-done.41 = bf16[80,384]{1,0:T(8,128)(2,1)S(1)} collective-permute-done((bf16[80,384]{1,0:T(8,128)(2,1)S(1)}, bf16[80,384]{1,0:T(8,128)(2,1)S(1)}, u32[]{:S(2)}, u32[]{:S(2)}) %collective-permute-start.41) | collective-permute-done | bytes 61472 | tf_op jit(solution)/shard_map/ppermute | solution.py:58
  385.5 3.9 collective-permute-done.42
  391.3 4.4 %collective-permute-start.43 = (bf16[4,80,384]{2,1,0:T(8,128)(2,1)}, bf16[4,80,384]{2,1,0:T(8,128)(2,1)}, u32[]{:S(2)}, u32[]{:S(2)}) collective-permute-start(bf16[4,80,384]{2,1,0:T(8,128)(2,1)} %pad_maximum_fusion.19), channel_id=1, source_target_pairs={{0,1},{1,0},{2,3},{3,2},{4,5},{5,4},{6,7},{7,6},{8,9},{9,8},{10,11... | collective-permute-start | bytes 737288 | tf_op jit(solution)/shard_map/ppermute | solution.py:58
  396.6 2.5 collective-permute-done.18
  399.1 4.6 %collective-permute-done.19 = bf16[128,1024]{0,1:T(8,128)(2,1)S(1)} collective-permute-done((bf16[128,1024]{0,1:T(8,128)(2,1)S(1)}, bf16[128,1024]{0,1:T(8,128)(2,1)S(1)}, u32[]{:S(2)}, u32[]{:S(2)}) %collective-permute-start.19) | collective-permute-done | bytes 262176 | tf_op jit(solution)/shard_map/ppermute | solution.py:58
  403.7 2.5 fusion.107
  (488 shorter events, 173.2 us)
Async XLA Ops:
  7.2 23.1 %copy-start = (bf16[1152,64]{0,1:T(8,128)(2,1)S(1)}, bf16[1152,64]{0,1:T(8,128)(2,1)}, u32[]{:S(2)}) copy-start(bf16[1152,64]{0,1:T(8,128)(2,1)} %param.51) | copy-start | bytes 442372
  8.4 22.1 %copy-start.74 = (bf16[64,1152]{1,0:T(8,128)(2,1)S(1)}, bf16[64,1152]{1,0:T(8,128)(2,1)}, u32[]{:S(2)}) copy-start(bf16[64,1152]{1,0:T(8,128)(2,1)} %param.50) | copy-start | bytes 442372
  8.4 22.1 %copy-start.75 = (bf16[64,1152]{1,0:T(8,128)(2,1)S(1)}, bf16[64,1152]{1,0:T(8,128)(2,1)}, u32[]{:S(2)}) copy-start(bf16[64,1152]{1,0:T(8,128)(2,1)} %param.49) | copy-start | bytes 442372
  8.4 24.9 %collective-permute-start = (bf16[128,1024]{0,1:T(8,128)(2,1)S(1)}, bf16[128,1024]{0,1:T(8,128)(2,1)S(1)}, u32[]{:S(2)}, u32[]{:S(2)}) collective-permute-start(bf16[128,1024]{0,1:T(8,128)(2,1)S(1)} %bitcast.437), channel_id=1, source_target_pairs={{0,2},{1,3},{2,0},{3,1},{4,6},{5,7},{6,4},{7,5},{8,10},{9,11},{10,... | collective-permute-start | bytes 786440 | tf_op jit(solution)/shard_map/ppermute | solution.py:58
  12.0 21.3 %collective-permute-start.1 = (bf16[128,1024]{0,1:T(8,128)(2,1)S(1)}, bf16[128,1024]{0,1:T(8,128)(2,1)S(1)}, u32[]{:S(2)}, u32[]{:S(2)}) collective-permute-start(bf16[128,1024]{0,1:T(8,128)(2,1)S(1)} %bitcast.438), channel_id=1, source_target_pairs={{0,4},{1,5},{2,6},{3,7},{4,0},{5,1},{6,2},{7,3},{8,12},{9,13},{10,... | collective-permute-start | bytes 786440 | tf_op jit(solution)/shard_map/ppermute | solution.py:58
  12.3 21.0 %collective-permute-start.2 = (bf16[128,1024]{0,1:T(8,128)(2,1)S(1)}, bf16[128,1024]{0,1:T(8,128)(2,1)S(1)}, u32[]{:S(2)}, u32[]{:S(2)}) collective-permute-start(bf16[128,1024]{0,1:T(8,128)(2,1)S(1)} %bitcast.439), channel_id=1, source_target_pairs={{0,6},{1,7},{2,4},{3,5},{4,2},{5,3},{6,0},{7,1},{8,14},{9,15},{10,... | collective-permute-start | bytes 786440 | tf_op jit(solution)/shard_map/ppermute | solution.py:58
  14.7 71.7 %collective-permute-start.20 = (bf16[128,1024]{0,1:T(8,128)(2,1)}, bf16[128,1024]{0,1:T(8,128)(2,1)}, u32[]{:S(2)}, u32[]{:S(2)}) collective-permute-start(bf16[128,1024]{0,1:T(8,128)(2,1)} %bitcast.79), channel_id=1, source_target_pairs={{0,2},{1,3},{2,0},{3,1},{4,6},{5,7},{6,4},{7,5},{8,10},{9,11},{10,... | collective-permute-start | bytes 786440 | tf_op jit(solution)/shard_map/ppermute | solution.py:58
  17.1 69.6 %collective-permute-start.21 = (bf16[128,1024]{0,1:T(8,128)(2,1)}, bf16[128,1024]{0,1:T(8,128)(2,1)}, u32[]{:S(2)}, u32[]{:S(2)}) collective-permute-start(bf16[128,1024]{0,1:T(8,128)(2,1)} %bitcast.79), channel_id=1, source_target_pairs={{0,4},{1,5},{2,6},{3,7},{4,0},{5,1},{6,2},{7,3},{8,12},{9,13},{10,... | collective-permute-start | bytes 786440 | tf_op jit(solution)/shard_map/ppermute | solution.py:58
  18.8 11.5 %copy-start.64 = (bf16[64,128]{1,0:T(8,128)(2,1)}, bf16[64,128]{1,0:T(8,128)(2,1)S(1)}, u32[]{:S(2)}) copy-start(bf16[64,128]{1,0:T(8,128)(2,1)S(1)} %get-tuple-element.315) | copy-start | bytes 49156
  22.4 21.9 %all-to-all-start = ((bf16[16,80,384]{2,1,0:T(8,128)(2,1)}), bf16[16,80,384]{2,1,0:T(8,128)(2,1)}, u32[]{:S(2)}, u32[]{:S(2)}) async-start(bf16[16,80,384]{2,1,0:T(8,128)(2,1)} %broadcast_in_dim.20), calls=%async_computation | async-start | bytes 1966080 | tf_op jit(solution)/shard_map/all_to_all | solution.py:159
  30.2 132.8 %all-gather.2.cloned.1.call-start = ((), (), s32[]{:S(2)}) async-start(), calls=%async_computation.3 | async-start | bytes 3899392 | tf_op jit(solution)/shard_map/all_gather | solution.py:139
  33.5 23.4 %copy-start.11 = (bf16[1,4,128,1024]{2,3,1,0:T(8,128)(2,1)}, bf16[1,4,128,1024]{2,3,1,0:T(8,128)(2,1)S(1)}, u32[]{:S(2)}) copy-start(bf16[1,4,128,1024]{2,3,1,0:T(8,128)(2,1)S(1)} %get-tuple-element.255) | copy-start | bytes 3145732
  33.5 21.4 %collective-permute-start.3 = (bf16[4,128,1024]{1,2,0:T(8,128)(2,1)S(1)}, bf16[4,128,1024]{1,2,0:T(8,128)(2,1)S(1)}, u32[]{:S(2)}, u32[]{:S(2)}) collective-permute-start(bf16[4,128,1024]{1,2,0:T(8,128)(2,1)S(1)} %get-tuple-element.256), channel_id=1, source_target_pairs={{0,1},{1,0},{2,3},{3,2},{4,5},{5,4},{6,7},{7,6},{8,9},{9,8},{10,11... | collective-permute-start | bytes 3145736 | tf_op jit(solution)/shard_map/ppermute | solution.py:58
  47.3 29.0 %collective-permute-start.8 = (bf16[1024,128]{1,0:T(8,128)(2,1)}, bf16[1024,128]{1,0:T(8,128)(2,1)}, u32[]{:S(2)}, u32[]{:S(2)}) collective-permute-start(bf16[1024,128]{1,0:T(8,128)(2,1)} %get-tuple-element.264), channel_id=1, source_target_pairs={{0,2},{1,3},{2,0},{3,1},{4,6},{5,7},{6,4},{7,5},{8,10},{9,11},{10,... | collective-permute-start | bytes 786440 | tf_op jit(solution)/shard_map/ppermute | solution.py:58
  49.0 28.3 %collective-permute-start.9 = (bf16[1024,128]{1,0:T(8,128)(2,1)}, bf16[1024,128]{1,0:T(8,128)(2,1)}, u32[]{:S(2)}, u32[]{:S(2)}) collective-permute-start(bf16[1024,128]{1,0:T(8,128)(2,1)} %get-tuple-element.264), channel_id=1, source_target_pairs={{0,4},{1,5},{2,6},{3,7},{4,0},{5,1},{6,2},{7,3},{8,12},{9,13},{10,... | collective-permute-start | bytes 786440 | tf_op jit(solution)/shard_map/ppermute | solution.py:58
  54.9 26.6 %collective-permute-start.10 = (bf16[1024,128]{1,0:T(8,128)(2,1)}, bf16[1024,128]{1,0:T(8,128)(2,1)}, u32[]{:S(2)}, u32[]{:S(2)}) collective-permute-start(bf16[1024,128]{1,0:T(8,128)(2,1)} %get-tuple-element.264), channel_id=1, source_target_pairs={{0,6},{1,7},{2,4},{3,5},{4,2},{5,3},{6,0},{7,1},{8,14},{9,15},{10,... | collective-permute-start | bytes 786440 | tf_op jit(solution)/shard_map/ppermute | solution.py:58
  76.4 11.2 %collective-permute-start.22 = (bf16[128,1024]{0,1:T(8,128)(2,1)}, bf16[128,1024]{0,1:T(8,128)(2,1)S(1)}, u32[]{:S(2)}, u32[]{:S(2)}) collective-permute-start(bf16[128,1024]{0,1:T(8,128)(2,1)} %bitcast.79), channel_id=1, source_target_pairs={{0,6},{1,7},{2,4},{3,5},{4,2},{5,3},{6,0},{7,1},{8,14},{9,15},{10,... | collective-permute-start | bytes 786440 | tf_op jit(solution)/shard_map/ppermute | solution.py:58
  77.3 6.9 %collective-permute-start.4 = (bf16[4,128,128]{2,1,0:T(8,128)(2,1)S(1)}, bf16[4,128,128]{2,1,0:T(8,128)(2,1)S(1)}, u32[]{:S(2)}, u32[]{:S(2)}) collective-permute-start(bf16[4,128,128]{2,1,0:T(8,128)(2,1)S(1)} %bitcast.516), channel_id=1, source_target_pairs={{0,1},{1,0},{2,3},{3,2},{4,5},{5,4},{6,7},{7,6},{8,9},{9,8},{10,11... | collective-permute-start | bytes 393224 | tf_op jit(solution)/shard_map/ppermute | solution.py:58
  84.1 8.6 %collective-permute-start.11 = (bf16[4,1024,128]{2,1,0:T(8,128)(2,1)}, bf16[4,1024,128]{2,1,0:T(8,128)(2,1)}, u32[]{:S(2)}, u32[]{:S(2)}) collective-permute-start(bf16[4,1024,128]{2,1,0:T(8,128)(2,1)} %get-tuple-element.254), channel_id=1, source_target_pairs={{0,1},{1,0},{2,3},{3,2},{4,5},{5,4},{6,7},{7,6},{8,9},{9,8},{10,11... | collective-permute-start | bytes 3145736 | tf_op jit(solution)/shard_map/ppermute | solution.py:58
  84.2 8.0 %collective-permute-start.5 = (bf16[2,128,128]{2,1,0:T(8,128)(2,1)S(1)}, bf16[2,128,128]{2,1,0:T(8,128)(2,1)S(1)}, u32[]{:S(2)}, u32[]{:S(2)}) collective-permute-start(bf16[2,128,128]{2,1,0:T(8,128)(2,1)S(1)} %get-tuple-element.290), channel_id=1, source_target_pairs={{0,2},{1,3},{2,0},{3,1},{4,6},{5,7},{6,4},{7,5},{8,10},{9,11},{10,... | collective-permute-start | bytes 196616 | tf_op jit(solution)/shard_map/ppermute | solution.py:58
  86.4 5.9 %collective-permute-start.6 = (bf16[2,128,128]{2,1,0:T(8,128)(2,1)S(1)}, bf16[2,128,128]{2,1,0:T(8,128)(2,1)S(1)}, u32[]{:S(2)}, u32[]{:S(2)}) collective-permute-start(bf16[2,128,128]{2,1,0:T(8,128)(2,1)S(1)} %get-tuple-element.292), channel_id=1, source_target_pairs={{0,4},{1,5},{2,6},{3,7},{4,0},{5,1},{6,2},{7,3},{8,12},{9,13},{10,... | collective-permute-start | bytes 196616 | tf_op jit(solution)/shard_map/ppermute | solution.py:58
  86.7 5.6 %collective-permute-start.7 = (bf16[2,128,128]{2,1,0:T(8,128)(2,1)S(1)}, bf16[2,128,128]{2,1,0:T(8,128)(2,1)S(1)}, u32[]{:S(2)}, u32[]{:S(2)}) collective-permute-start(bf16[2,128,128]{2,1,0:T(8,128)(2,1)S(1)} %get-tuple-element.291), channel_id=1, source_target_pairs={{0,6},{1,7},{2,4},{3,5},{4,2},{5,3},{6,0},{7,1},{8,14},{9,15},{10,... | collective-permute-start | bytes 196616 | tf_op jit(solution)/shard_map/ppermute | solution.py:58
  90.2 36.5 %collective-permute-start.23 = (bf16[4,128,1024]{1,2,0:T(8,128)(2,1)}, bf16[4,128,1024]{1,2,0:T(8,128)(2,1)}, u32[]{:S(2)}, u32[]{:S(2)}) collective-permute-start(bf16[4,128,1024]{1,2,0:T(8,128)(2,1)} %get-tuple-element.247), channel_id=1, source_target_pairs={{0,1},{1,0},{2,3},{3,2},{4,5},{5,4},{6,7},{7,6},{8,9},{9,8},{10,11... | collective-permute-start | bytes 3145736 | tf_op jit(solution)/shard_map/ppermute | solution.py:58
  92.2 19.0 %copy-start.68 = (f32[1024]{0:T(1024)}, f32[1024]{0:T(1024)S(1)}, u32[]{:S(2)}) copy-start(f32[1024]{0:T(1024)S(1)} %mul.466) | copy-start | bytes 12292
  107.7 15.6 %copy-start.85 = (f32[128]{0:T(128)}, f32[128]{0:T(128)S(1)}, u32[]{:S(2)}) copy-start(f32[128]{0:T(128)S(1)} %add_rsqrt_fusion.4) | copy-start | bytes 1540
  107.9 8.5 %collective-permute-start.12 = (bf16[128,1024]{0,1:T(8,128)(2,1)S(1)}, bf16[128,1024]{0,1:T(8,128)(2,1)S(1)}, u32[]{:S(2)}, u32[]{:S(2)}) collective-permute-start(bf16[128,1024]{0,1:T(8,128)(2,1)S(1)} %multiply_convert_fusion.6), channel_id=1, source_target_pairs={{0,2},{1,3},{2,0},{3,1},{4,6},{5,7},{6,4},{7,5},{8,10},{9,11},{10,... | collective-permute-start | bytes 786440 | tf_op jit(solution)/shard_map/ppermute | solution.py:58
  110.0 12.5 %collective-permute-start.13 = (bf16[128,1024]{0,1:T(8,128)(2,1)S(1)}, bf16[128,1024]{0,1:T(8,128)(2,1)S(1)}, u32[]{:S(2)}, u32[]{:S(2)}) collective-permute-start(bf16[128,1024]{0,1:T(8,128)(2,1)S(1)} %multiply_convert_fusion.6), channel_id=1, source_target_pairs={{0,4},{1,5},{2,6},{3,7},{4,0},{5,1},{6,2},{7,3},{8,12},{9,13},{10,... | collective-permute-start | bytes 786440 | tf_op jit(solution)/shard_map/ppermute | solution.py:58
  110.4 13.0 %collective-permute-start.14 = (bf16[128,1024]{0,1:T(8,128)(2,1)S(1)}, bf16[128,1024]{0,1:T(8,128)(2,1)S(1)}, u32[]{:S(2)}, u32[]{:S(2)}) collective-permute-start(bf16[128,1024]{0,1:T(8,128)(2,1)S(1)} %multiply_convert_fusion.6), channel_id=1, source_target_pairs={{0,6},{1,7},{2,4},{3,5},{4,2},{5,3},{6,0},{7,1},{8,14},{9,15},{10,... | collective-permute-start | bytes 786440 | tf_op jit(solution)/shard_map/ppermute | solution.py:58
  124.8 31.4 %collective-permute-start.15 = (bf16[4,128,1024]{1,2,0:T(8,128)(2,1)}, bf16[4,128,1024]{1,2,0:T(8,128)(2,1)}, u32[]{:S(2)}, u32[]{:S(2)}) collective-permute-start(bf16[4,128,1024]{1,2,0:T(8,128)(2,1)} %get-tuple-element.252), channel_id=1, source_target_pairs={{0,1},{1,0},{2,3},{3,2},{4,5},{5,4},{6,7},{7,6},{8,9},{9,8},{10,11... | collective-permute-start | bytes 3145736 | tf_op jit(solution)/shard_map/ppermute | solution.py:58
  182.1 23.3 %collective-permute-start.24 = (bf16[4,128,1024]{1,2,0:T(8,128)(2,1)}, bf16[4,128,1024]{1,2,0:T(8,128)(2,1)}, u32[]{:S(2)}, u32[]{:S(2)}) collective-permute-start(bf16[4,128,1024]{1,2,0:T(8,128)(2,1)} %copy.391), channel_id=1, source_target_pairs={{0,1},{1,0},{2,3},{3,2},{4,5},{5,4},{6,7},{7,6},{8,9},{9,8},{10,11... | collective-permute-start | bytes 3145736 | tf_op jit(solution)/shard_map/ppermute | solution.py:58
  204.9 59.3 %collective-permute-start.16 = (bf16[4,128,1024]{1,2,0:T(8,128)(2,1)}, bf16[4,128,1024]{1,2,0:T(8,128)(2,1)}, u32[]{:S(2)}, u32[]{:S(2)}) collective-permute-start(bf16[4,128,1024]{1,2,0:T(8,128)(2,1)} %copy.386), channel_id=1, source_target_pairs={{0,1},{1,0},{2,3},{3,2},{4,5},{5,4},{6,7},{7,6},{8,9},{9,8},{10,11... | collective-permute-start | bytes 3145736 | tf_op jit(solution)/shard_map/ppermute | solution.py:58
  207.8 8.1 %collective-permute-start.25 = (bf16[128,1024]{0,1:T(8,128)(2,1)S(1)}, bf16[128,1024]{0,1:T(8,128)(2,1)S(1)}, u32[]{:S(2)}, u32[]{:S(2)}) collective-permute-start(bf16[128,1024]{0,1:T(8,128)(2,1)S(1)} %get-tuple-element.243), channel_id=1, source_target_pairs={{0,4},{1,5},{2,6},{3,7},{4,0},{5,1},{6,2},{7,3},{8,12},{9,13},{10,... | collective-permute-start | bytes 786440 | tf_op jit(solution)/shard_map/ppermute | solution.py:58
  208.6 14.5 %collective-permute-start.26 = (bf16[128,1024]{0,1:T(8,128)(2,1)S(1)}, bf16[128,1024]{0,1:T(8,128)(2,1)S(1)}, u32[]{:S(2)}, u32[]{:S(2)}) collective-permute-start(bf16[128,1024]{0,1:T(8,128)(2,1)S(1)} %get-tuple-element.245), channel_id=1, source_target_pairs={{0,2},{1,3},{2,0},{3,1},{4,6},{5,7},{6,4},{7,5},{8,10},{9,11},{10,... | collective-permute-start | bytes 786440 | tf_op jit(solution)/shard_map/ppermute | solution.py:58
  210.9 14.2 %collective-permute-start.27 = (bf16[128,1024]{0,1:T(8,128)(2,1)S(1)}, bf16[128,1024]{0,1:T(8,128)(2,1)S(1)}, u32[]{:S(2)}, u32[]{:S(2)}) collective-permute-start(bf16[128,1024]{0,1:T(8,128)(2,1)S(1)} %get-tuple-element.244), channel_id=1, source_target_pairs={{0,6},{1,7},{2,4},{3,5},{4,2},{5,3},{6,0},{7,1},{8,14},{9,15},{10,... | collective-permute-start | bytes 786440 | tf_op jit(solution)/shard_map/ppermute | solution.py:58
  211.7 13.4 %copy-start.69 = (f32[1024]{0:T(1024)S(1)}, f32[1024]{0:T(1024)}, u32[]{:S(2)}) copy-start(f32[1024]{0:T(1024)} %copy-done.68) | copy-start | bytes 12292
  211.7 13.4 %copy-start.86 = (f32[128]{0:T(128)S(1)}, f32[128]{0:T(128)}, u32[]{:S(2)}) copy-start(f32[128]{0:T(128)} %copy-done.85) | copy-start | bytes 1540
  227.8 8.1 %collective-permute-start.28 = (bf16[128,1024]{0,1:T(8,128)(2,1)S(1)}, bf16[128,1024]{0,1:T(8,128)(2,1)S(1)}, u32[]{:S(2)}, u32[]{:S(2)}) collective-permute-start(bf16[128,1024]{0,1:T(8,128)(2,1)S(1)} %fusion.120), channel_id=1, source_target_pairs={{0,2},{1,3},{2,0},{3,1},{4,6},{5,7},{6,4},{7,5},{8,10},{9,11},{10,... | collective-permute-start | bytes 786440 | tf_op jit(solution)/shard_map/ppermute | solution.py:58
  227.9 12.0 %collective-permute-start.29 = (bf16[128,1024]{0,1:T(8,128)(2,1)S(1)}, bf16[128,1024]{0,1:T(8,128)(2,1)S(1)}, u32[]{:S(2)}, u32[]{:S(2)}) collective-permute-start(bf16[128,1024]{0,1:T(8,128)(2,1)S(1)} %fusion.120), channel_id=1, source_target_pairs={{0,4},{1,5},{2,6},{3,7},{4,0},{5,1},{6,2},{7,3},{8,12},{9,13},{10,... | collective-permute-start | bytes 786440 | tf_op jit(solution)/shard_map/ppermute | solution.py:58
  229.4 13.9 %collective-permute-start.30 = (bf16[128,1024]{0,1:T(8,128)(2,1)S(1)}, bf16[128,1024]{0,1:T(8,128)(2,1)S(1)}, u32[]{:S(2)}, u32[]{:S(2)}) collective-permute-start(bf16[128,1024]{0,1:T(8,128)(2,1)S(1)} %fusion.120), channel_id=1, source_target_pairs={{0,6},{1,7},{2,4},{3,5},{4,2},{5,3},{6,0},{7,1},{8,14},{9,15},{10,... | collective-permute-start | bytes 786440 | tf_op jit(solution)/shard_map/ppermute | solution.py:58
  231.2 14.1 %copy-start.96 = (bf16[1024,576]{0,1:T(8,128)(2,1)S(1)}, bf16[1024,576]{0,1:T(8,128)(2,1)}, u32[]{:S(2)}) copy-start(bf16[1024,576]{0,1:T(8,128)(2,1)} %get-tuple-element.235) | copy-start | bytes 3538948
  244.8 24.4 %collective-permute-start.31 = (bf16[4,128,1024]{1,2,0:T(8,128)(2,1)}, bf16[4,128,1024]{1,2,0:T(8,128)(2,1)}, u32[]{:S(2)}, u32[]{:S(2)}) collective-permute-start(bf16[4,128,1024]{1,2,0:T(8,128)(2,1)} %get-tuple-element.242), channel_id=1, source_target_pairs={{0,1},{1,0},{2,3},{3,2},{4,5},{5,4},{6,7},{7,6},{8,9},{9,8},{10,11... | collective-permute-start | bytes 3145736 | tf_op jit(solution)/shard_map/ppermute | solution.py:58
  256.7 80.3 %all-to-all-start.2 = ((bf16[16,64,1728]{2,1,0:T(8,128)(2,1)}), bf16[16,64,1728]{2,1,0:T(8,128)(2,1)}, u32[]{:S(2)}, u32[]{:S(2)}) async-start(bf16[16,64,1728]{2,1,0:T(8,128)(2,1)} %concatenate.166), calls=%async_computation.2 | async-start | bytes 7340032 | tf_op jit(solution)/shard_map/all_to_all | solution.py:250
  323.5 4.0 collective-permute-start.36
  328.3 8.3 %collective-permute-start.37 = (bf16[2,128,128]{2,1,0:T(8,128)(2,1)S(1)}, bf16[2,128,128]{2,1,0:T(8,128)(2,1)S(1)}, u32[]{:S(2)}, u32[]{:S(2)}) collective-permute-start(bf16[2,128,128]{2,1,0:T(8,128)(2,1)S(1)} %get-tuple-element.280), channel_id=1, source_target_pairs={{0,2},{1,3},{2,0},{3,1},{4,6},{5,7},{6,4},{7,5},{8,10},{9,11},{10,... | collective-permute-start | bytes 196616 | tf_op jit(solution)/shard_map/ppermute | solution.py:58
  328.4 8.2 %collective-permute-start.38 = (bf16[2,128,128]{2,1,0:T(8,128)(2,1)S(1)}, bf16[2,128,128]{2,1,0:T(8,128)(2,1)S(1)}, u32[]{:S(2)}, u32[]{:S(2)}) collective-permute-start(bf16[2,128,128]{2,1,0:T(8,128)(2,1)S(1)} %get-tuple-element.282), channel_id=1, source_target_pairs={{0,4},{1,5},{2,6},{3,7},{4,0},{5,1},{6,2},{7,3},{8,12},{9,13},{10,... | collective-permute-start | bytes 196616 | tf_op jit(solution)/shard_map/ppermute | solution.py:58
  329.9 6.8 %collective-permute-start.39 = (bf16[2,128,128]{2,1,0:T(8,128)(2,1)S(1)}, bf16[2,128,128]{2,1,0:T(8,128)(2,1)S(1)}, u32[]{:S(2)}, u32[]{:S(2)}) collective-permute-start(bf16[2,128,128]{2,1,0:T(8,128)(2,1)S(1)} %get-tuple-element.281), channel_id=1, source_target_pairs={{0,6},{1,7},{2,4},{3,5},{4,2},{5,3},{6,0},{7,1},{8,14},{9,15},{10,... | collective-permute-start | bytes 196616 | tf_op jit(solution)/shard_map/ppermute | solution.py:58
  335.2 16.3 %collective-permute-start.32 = (bf16[4,128,1024]{1,2,0:T(8,128)(2,1)S(1)}, bf16[4,128,1024]{1,2,0:T(8,128)(2,1)}, u32[]{:S(2)}, u32[]{:S(2)}) collective-permute-start(bf16[4,128,1024]{1,2,0:T(8,128)(2,1)S(1)} %copy.414), channel_id=1, source_target_pairs={{0,1},{1,0},{2,3},{3,2},{4,5},{5,4},{6,7},{7,6},{8,9},{9,8},{10,11... | collective-permute-start | bytes 3145736 | tf_op jit(solution)/shard_map/ppermute | solution.py:58
  340.4 8.4 %collective-permute-start.44 = (bf16[64,1728]{1,0:T(8,128)(2,1)}, bf16[64,1728]{1,0:T(8,128)(2,1)S(1)}, u32[]{:S(2)}, u32[]{:S(2)}) collective-permute-start(bf16[64,1728]{1,0:T(8,128)(2,1)} %convert_element_type.403), channel_id=1, source_target_pairs={{0,4},{1,5},{2,6},{3,7},{4,0},{5,1},{6,2},{7,3},{8,12},{9,13},{10,... | collective-permute-start | bytes 663560 | tf_op jit(solution)/shard_map/ppermute | solution.py:58
  341.4 22.5 %all-to-all-start.1 = ((bf16[16,80,384]{2,1,0:T(8,128)(2,1)}), bf16[16,80,384]{2,1,0:T(8,128)(2,1)}, u32[]{:S(2)}, u32[]{:S(2)}) async-start(bf16[16,80,384]{2,1,0:T(8,128)(2,1)} %fusion.64), calls=%async_computation.1 | async-start | bytes 1966080 | tf_op jit(solution)/shard_map/all_to_all | solution.py:350
  351.5 13.8 %copy-start.65 = (bf16[64,128]{1,0:T(8,128)(2,1)S(1)}, bf16[64,128]{1,0:T(8,128)(2,1)}, u32[]{:S(2)}) copy-start(bf16[64,128]{1,0:T(8,128)(2,1)} %copy-done.64) | copy-start | bytes 49156
  354.0 41.7 %copy-start.72 = (f32[1024]{0:T(1024)S(1)}, f32[1024]{0:T(1024)}, u32[]{:S(2)}) copy-start(f32[1024]{0:T(1024)} %copy-done.70) | copy-start | bytes 12292
  365.3 38.4 %copy-start.17 = (f32[128,1024]{0,1:T(8,128)S(1)}, f32[128,1024]{0,1:T(8,128)}, u32[]{:S(2)}) copy-start(f32[128,1024]{0,1:T(8,128)} %copy-done.16) | copy-start | bytes 1572868
  365.3 38.4 %copy-start.87 = (f32[128]{0:T(128)S(1)}, f32[128]{0:T(128)}, u32[]{:S(2)}) copy-start(f32[128]{0:T(128)} %copy-done.85) | copy-start | bytes 1540
  369.8 20.8 %copy-start.63 = (bf16[128,1024]{0,1:T(8,128)(2,1)S(1)}, bf16[128,1024]{0,1:T(8,128)(2,1)}, u32[]{:S(2)}) copy-start(bf16[128,1024]{0,1:T(8,128)(2,1)} %get-tuple-element.249) | copy-start | bytes 786436
  370.6 5.9 %collective-permute-start.40 = (bf16[80,384]{1,0:T(8,128)(2,1)S(1)}, bf16[80,384]{1,0:T(8,128)(2,1)S(1)}, u32[]{:S(2)}, u32[]{:S(2)}) collective-permute-start(bf16[80,384]{1,0:T(8,128)(2,1)S(1)} %pad_maximum_fusion.23), channel_id=1, source_target_pairs={{0,2},{1,3},{2,0},{3,1},{4,6},{5,7},{6,4},{7,5},{8,10},{9,11},{10,... | collective-permute-start | bytes 184328 | tf_op jit(solution)/shard_map/ppermute | solution.py:58
  372.6 18.0 %collective-permute-start.33 = (bf16[128,1024]{0,1:T(8,128)(2,1)S(1)}, bf16[128,1024]{0,1:T(8,128)(2,1)S(1)}, u32[]{:S(2)}, u32[]{:S(2)}) collective-permute-start(bf16[128,1024]{0,1:T(8,128)(2,1)S(1)} %get-tuple-element.238), channel_id=1, source_target_pairs={{0,4},{1,5},{2,6},{3,7},{4,0},{5,1},{6,2},{7,3},{8,12},{9,13},{10,... | collective-permute-start | bytes 786440 | tf_op jit(solution)/shard_map/ppermute | solution.py:58
  372.6 18.6 %collective-permute-start.34 = (bf16[128,1024]{0,1:T(8,128)(2,1)S(1)}, bf16[128,1024]{0,1:T(8,128)(2,1)S(1)}, u32[]{:S(2)}, u32[]{:S(2)}) collective-permute-start(bf16[128,1024]{0,1:T(8,128)(2,1)S(1)} %get-tuple-element.240), channel_id=1, source_target_pairs={{0,2},{1,3},{2,0},{3,1},{4,6},{5,7},{6,4},{7,5},{8,10},{9,11},{10,... | collective-permute-start | bytes 786440 | tf_op jit(solution)/shard_map/ppermute | solution.py:58
  375.4 20.3 %collective-permute-start.35 = (bf16[128,1024]{0,1:T(8,128)(2,1)S(1)}, bf16[128,1024]{0,1:T(8,128)(2,1)S(1)}, u32[]{:S(2)}, u32[]{:S(2)}) collective-permute-start(bf16[128,1024]{0,1:T(8,128)(2,1)S(1)} %get-tuple-element.239), channel_id=1, source_target_pairs={{0,6},{1,7},{2,4},{3,5},{4,2},{5,3},{6,0},{7,1},{8,14},{9,15},{10,... | collective-permute-start | bytes 786440 | tf_op jit(solution)/shard_map/ppermute | solution.py:58
  376.5 8.8 %collective-permute-start.41 = (bf16[80,384]{1,0:T(8,128)(2,1)S(1)}, bf16[80,384]{1,0:T(8,128)(2,1)S(1)}, u32[]{:S(2)}, u32[]{:S(2)}) collective-permute-start(bf16[80,384]{1,0:T(8,128)(2,1)S(1)} %pad_maximum_fusion.23), channel_id=1, source_target_pairs={{0,4},{1,5},{2,6},{3,7},{4,0},{5,1},{6,2},{7,3},{8,12},{9,13},{10,... | collective-permute-start | bytes 184328 | tf_op jit(solution)/shard_map/ppermute | solution.py:58
  376.5 12.9 %collective-permute-start.42 = (bf16[80,384]{1,0:T(8,128)(2,1)S(1)}, bf16[80,384]{1,0:T(8,128)(2,1)S(1)}, u32[]{:S(2)}, u32[]{:S(2)}) collective-permute-start(bf16[80,384]{1,0:T(8,128)(2,1)S(1)} %pad_maximum_fusion.23), channel_id=1, source_target_pairs={{0,6},{1,7},{2,4},{3,5},{4,2},{5,3},{6,0},{7,1},{8,14},{9,15},{10,... | collective-permute-start | bytes 184328 | tf_op jit(solution)/shard_map/ppermute | solution.py:58
  385.3 11.3 %collective-permute-start.17 = (bf16[128,1024]{0,1:T(8,128)(2,1)}, bf16[128,1024]{0,1:T(8,128)(2,1)S(1)}, u32[]{:S(2)}, u32[]{:S(2)}) collective-permute-start(bf16[128,1024]{0,1:T(8,128)(2,1)} %get-tuple-element.248), channel_id=1, source_target_pairs={{0,4},{1,5},{2,6},{3,7},{4,0},{5,1},{6,2},{7,3},{8,12},{9,13},{10,... | collective-permute-start | bytes 786440 | tf_op jit(solution)/shard_map/ppermute | solution.py:58
  389.5 9.6 %collective-permute-start.18 = (bf16[128,1024]{0,1:T(8,128)(2,1)}, bf16[128,1024]{0,1:T(8,128)(2,1)S(1)}, u32[]{:S(2)}, u32[]{:S(2)}) collective-permute-start(bf16[128,1024]{0,1:T(8,128)(2,1)} %get-tuple-element.250), channel_id=1, source_target_pairs={{0,2},{1,3},{2,0},{3,1},{4,6},{5,7},{6,4},{7,5},{8,10},{9,11},{10,... | collective-permute-start | bytes 786440 | tf_op jit(solution)/shard_map/ppermute | solution.py:58
  390.6 13.1 %collective-permute-start.19 = (bf16[128,1024]{0,1:T(8,128)(2,1)S(1)}, bf16[128,1024]{0,1:T(8,128)(2,1)S(1)}, u32[]{:S(2)}, u32[]{:S(2)}) collective-permute-start(bf16[128,1024]{0,1:T(8,128)(2,1)S(1)} %copy-done.63), channel_id=1, source_target_pairs={{0,6},{1,7},{2,4},{3,5},{4,2},{5,3},{6,0},{7,1},{8,14},{9,15},{10,... | collective-permute-start | bytes 786440 | tf_op jit(solution)/shard_map/ppermute | solution.py:58
  391.3 18.5 %collective-permute-start.43 = (bf16[4,80,384]{2,1,0:T(8,128)(2,1)}, bf16[4,80,384]{2,1,0:T(8,128)(2,1)}, u32[]{:S(2)}, u32[]{:S(2)}) collective-permute-start(bf16[4,80,384]{2,1,0:T(8,128)(2,1)} %pad_maximum_fusion.19), channel_id=1, source_target_pairs={{0,1},{1,0},{2,3},{3,2},{4,5},{5,4},{6,7},{7,6},{8,9},{9,8},{10,11... | collective-permute-start | bytes 737288 | tf_op jit(solution)/shard_map/ppermute | solution.py:58
  (85 other events, 279.8 us)
Sparse Core Ops, SparseCore 0:
  33.3 51.6 all-gather.1

commit v2 on v1

v2 whole, which is shorter than its diff:
```python
import jax
import jax.numpy as jnp
import numpy as np
from jax import lax
from jax.experimental import pallas as pl
from jax.experimental.pallas import tpu as pltpu
from jax.sharding import PartitionSpec as P

epsilon = 1e-05
rope_base = 1000000.0
masked_score = -1e30
line = ("context", "tensor")
f32 = jnp.float32
bf16 = jnp.bfloat16
piece = 128
half_head = 64
width = 1024
main = 512
packed = 3 * main + 256


def dot(a, b):
    return jnp.dot(a, b, preferred_element_type=f32)


def dot_nt(a, b):
    return lax.dot_general(a, b, (((1,), (1,)), ((), ())), preferred_element_type=f32)


def dot_tn(a, b):
    return lax.dot_general(a, b, (((0,), (0,)), ((), ())), preferred_element_type=f32)


def shape(dims, dtype):
    return jax.ShapeDtypeStruct(dims, dtype)


def estimate(micros):
    return pl.CostEstimate(flops=int(micros * 10**9), bytes_accessed=2**20, transcendentals=0)


room = {"attention_forward": 16, "attention_backward": 18, "feed_forward": 14, "pack": 60, "feed_pack": 60}


def big(value):
    return value.shape[0] > 1024


def call(body, outs, *args, micros=2, scratch=(), name=None, fetch=(), store=()):
    smem = pl.BlockSpec(memory_space=pltpu.SMEM)
    vmem = pl.BlockSpec(memory_space=pltpu.VMEM)
    anywhere = pl.BlockSpec(memory_space=pltpu.HBM)
    arrays = [i for i, a in enumerate(args) if a.dtype != jnp.int32]
    moved_in = arrays if fetch is True else list(fetch)
    moved_out = list(range(len(outs))) if store is True else list(store)
    buffers = [pltpu.VMEM(args[i].shape, args[i].dtype) for i in moved_in]
    buffers += [pltpu.VMEM(outs[i].shape, outs[i].dtype) for i in moved_out]
    count = len(buffers)
    if count:
        buffers.append(pltpu.SemaphoreType.DMA((count,)))

    def run(*refs):
        if not count:
            return body(*refs)
        refs = list(refs)
        first = len(args) + len(outs)
        held, sems = refs[first : first + count], refs[first + count]
        shown = refs[:first] + refs[first + count + 1 :]
        copies = []
        for slot, index in enumerate(moved_in):
            copy = pltpu.make_async_copy(refs[index], held[slot], sems.at[slot])
            copy.start()
            copies.append(copy)
            shown[index] = held[slot]
        for slot, index in enumerate(moved_out):
            shown[len(args) + index] = held[len(moved_in) + slot]
        for copy in copies:
            copy.wait()
        body(*shown)
        copies = []
        for slot, index in enumerate(moved_out):
            slot += len(moved_in)
            copy = pltpu.make_async_copy(held[slot], refs[len(args) + index], sems.at[slot])
            copy.start()
            copies.append(copy)
        for copy in copies:
            copy.wait()

    return pl.pallas_call(
        run,
        out_shape=tuple(outs),
        in_specs=[
            smem if i not in arrays else (anywhere if i in moved_in or big(args[i]) else vmem)
            for i in range(len(args))
        ],
        out_specs=tuple(anywhere if i in moved_out or big(o) else vmem for i, o in enumerate(outs)),
        scratch_shapes=buffers + list(scratch),
        compiler_params=pltpu.CompilerParams(vmem_limit_bytes=room.get(name, 12) * 2**20),
        cost_estimate=estimate(micros),
        name=name,
    )(*args)


def lanes(rows=1):
    return lax.broadcasted_iota(jnp.int32, (rows, piece), 1)


def mean_square_factor(value):
    return lax.rsqrt(jnp.mean(value * value, axis=-1, keepdims=True) + epsilon)


def halves_sum(value, low):
    first = jnp.sum(jnp.where(low, value, 0.0), axis=-1, keepdims=True)
    second = jnp.sum(jnp.where(low, 0.0, value), axis=-1, keepdims=True)
    return jnp.where(low, first, second)


def swapped_halves(value):
    return pltpu.roll(value, half_head, 1)


def turned(value, early):
    return jnp.where(early, pltpu.roll(value, 96, 1), pltpu.roll(value, 32, 1))


def place_of(me, core, chip):
    return me ^ (2 * chip + core)


def slot_of(me, place):
    partner = place ^ me
    return (partner % 2) * 4 + partner // 2


def feed_pack_kernel(info, gate, up, down, feed_out):
    context = info[2]
    low = lanes() < half_head
    late = context == 1
    start = pl.multiple_of(context * main, main)
    made = [ref[:, pl.ds(start, main)] for ref in (gate, up, down)]

    def rest(ref):
        tile = ref[:, 2 * main : 2 * main + piece].astype(f32)
        return jnp.where(late, swapped_halves(tile), tile)

    tail = jnp.where(low, rest(gate), swapped_halves(rest(up)))
    made.append(tail.astype(bf16))
    made.append(jnp.where(low, rest(down), 0.0).astype(bf16))
    block = jnp.concatenate(made, axis=1)
    for index in range(16):
        feed_out[index] = block


def pack_kernel(info, small, query, key, value, out, pack_out):
    shard, me = info[0], info[1]
    low = lanes() < half_head
    odd = me % 2 == 1

    def pair(ref):
        tile = ref[:, pl.ds(pl.multiple_of((me // 2) * piece, piece), piece)].astype(f32)
        return jnp.where(odd, swapped_halves(tile), tile)

    start = pl.multiple_of(me * piece, piece)
    keys = pair(key)
    values = swapped_halves(pair(value))
    pack = jnp.concatenate(
        [
            query[:, pl.ds(start, piece)],
            jnp.where(low, keys, values).astype(bf16),
            out[:, pl.ds(start, piece)],
        ],
        axis=1,
    )
    row = lax.broadcasted_iota(jnp.int32, (16, piece), 0)
    lane = lanes(16)
    ours = lane // half_head == shard % 2
    both = small[0:1, :]
    other = swapped_halves(both)
    gains = jnp.where(ours & (row == shard // 2), jnp.where(low, both, other), 0.0)
    gains = gains + jnp.where(ours & (row == 8 + shard // 2), jnp.where(low, other, both), 0.0)
    spot = (lane % half_head) // 4 == shard
    head_gains = jnp.zeros((16, piece), f32)
    for entry in range(4):
        here = spot & (lane % 4 == entry)
        query_gain = small[1:2, entry : entry + 1]
        key_gain = small[1:2, 4 + entry : 5 + entry]
        head_gains = head_gains + jnp.where(here & (row == 0), query_gain, 0.0)
        head_gains = head_gains + jnp.where(here & (row == 1), key_gain, 0.0)
    extra = jnp.concatenate([gains, head_gains, jnp.zeros((16, piece), f32)], axis=1)
    pack = jnp.concatenate([pack, extra.astype(bf16)], axis=0)
    for index in range(16):
        pack_out[index] = pack


def gathered_gains(pack):
    gains = pack[0, half_head:, :].astype(f32)
    for index in range(1, 16):
        gains = gains + pack[index, half_head:, :].astype(f32)
    return gains


def wide_gain(gains, first):
    return jnp.concatenate([gains[first + i : first + i + 1, :piece] for i in range(8)], axis=1)


def qkv_weight(pack):
    return pack[:, :half_head, : 2 * piece].reshape(width, 2 * piece)


def rounded(value):
    return value.astype(bf16).astype(f32)


def block_queries(ref, block, masks):
    both = ref[2 * block : 2 * block + 2].reshape(2 * piece, piece).astype(bf16)
    return jnp.concatenate([both * masks[0], both * masks[1]], axis=0)


def head_masks():
    low = (lanes() < half_head).astype(f32)
    return (low.astype(bf16), (1.0 - low).astype(bf16))


def block_scores(keys, stacked, count):
    score = dot_nt(keys, stacked) * (half_head**-0.5)
    span = 2 * piece
    row = lax.broadcasted_iota(jnp.int32, (span, 2 * span), 0)
    column = lax.broadcasted_iota(jnp.int32, (span, 2 * span), 1) % span
    own = jnp.where(row <= column, score[count - span :], masked_score)
    if count == span:
        return own
    return jnp.concatenate([score[: count - span], own], axis=0)


def pick_heads(wide):
    span = 2 * piece
    both = jnp.concatenate([wide[:half_head, :span], wide[half_head:, span:]], axis=0)
    return both.T


def angle_tables(table, place):
    start_cos, start_sin = table[pl.ds(place, 1), :], table[pl.ds(8 + place, 1), :]
    cos, sin = table[16 : 16 + piece, :], table[16 + piece :, :]
    return start_cos * cos - start_sin * sin, start_sin * cos + start_cos * sin


def forward_kernel(info, pack, mine, other, table, attended, mixer, log_out, gain_out, kept, raw, held, sem):
    me = info[1]
    query_out, key_out, value_out, query_normed, key_normed, query_factor, key_factor = [
        held.at[pl.ds(8 * i, 8)] for i in range(7)
    ]
    gains = gathered_gains(pack)
    gain_out[...] = gains
    gain = wide_gain(gains, 0)
    gain_query = gains[0:1, piece : 2 * piece]
    gain_key = gains[1:2, piece : 2 * piece]
    low = lanes() < half_head
    early = lanes() % half_head < half_head // 2
    for core, ref in enumerate((mine, other)):

        def prepare(chip, carry, ref=ref, core=core):
            x = ref[chip].astype(f32)
            mixer[core, chip] = (x * mean_square_factor(x) * gain).astype(bf16)
            return carry

        lax.fori_loop(0, 4, prepare, 0)
        raw[core] = dot(mixer[core].reshape(4 * piece, width), qkv_weight(pack)).reshape(
            4, piece, 2 * piece
        )

    def shape_heads(slot, carry):
        core, chip = slot // 4, slot % 4
        place = place_of(me, core, chip)
        block = raw[core, chip]
        query = block[:, :piece]
        both = block[:, piece:]
        other_way = swapped_halves(both)
        key = jnp.where(low, both, other_way)
        value_out[place] = rounded(jnp.where(low, other_way, both))
        factor = lax.rsqrt(halves_sum(query * query, low) / half_head + epsilon)
        normed = query * factor
        scaled = normed * gain_query
        cos, sin = angle_tables(table, place)
        sin = jnp.where(early, -sin, sin)
        query_out[place] = rounded(scaled * cos + turned(scaled, early) * sin)
        query_normed[place] = normed
        query_factor[place] = factor
        factor = jnp.broadcast_to(mean_square_factor(key), key.shape)
        normed = key * factor
        scaled = normed * gain_key
        key_out[place] = rounded(scaled * cos + turned(scaled, early) * sin)
        key_normed[place] = normed
        key_factor[place] = factor
        return carry

    lax.fori_loop(0, 8, shape_heads, 0)
    copy = pltpu.make_async_copy(held, kept.at[pl.ds(0, 56)], sem)
    copy.start()
    masks = head_masks()
    values_across = value_out[...].reshape(width, piece).T.astype(bf16)
    for block in range(4):
        count = 2 * piece * (block + 1)
        keys = key_out[: 2 * block + 2].reshape(count, piece).astype(bf16)
        score = block_scores(keys, block_queries(query_out, block, masks), count)
        peak = jnp.max(score, axis=0, keepdims=True)
        raised = jnp.exp(score - peak)
        total = jnp.sum(raised, axis=0, keepdims=True)
        chance = (raised * (1.0 / total)).astype(bf16)
        log_out[block] = peak + jnp.log(total)
        result = pick_heads(dot(values_across[:, :count], chance)).astype(bf16)
        for index in range(2):
            attended[slot_of(me, 2 * block + index)] = result[index * piece : (index + 1) * piece]
    copy.wait()


def branch_kernel(info, own, far, near, next_, mine, other, tokens, gains, mixed_out, feed_out, out_rows, attended):
    me = info[1]
    for chip, ref in enumerate((own, far, near, next_)):
        for core in range(2):
            start = pl.multiple_of(place_of(me, core, chip) * piece, piece)
            attended[:, pl.ds(start, piece)] = ref[core]
    rows = attended[...]
    own = pl.ds(pl.multiple_of(me * piece, piece), piece)
    for core, ref in enumerate((mine, other)):
        for chip in range(4):
            start = pl.multiple_of(place_of(me, core, chip) * piece, piece)
            mixed_out[:, pl.ds(start, piece)] = dot(rows, ref[chip])
            out_rows[:, pl.ds(start, piece)] = ref[chip, own, :]
    mixed = tokens[...].astype(f32) + mixed_out[...]
    mixed_out[...] = mixed
    gain = wide_gain(gains, 8)
    feed_out[...] = (mixed * mean_square_factor(mixed) * gain).astype(bf16)


def squash(value):
    return 1.0 / (1.0 + jnp.exp(-value))


def feed_kernel(feed_mine, feed_other, seed_mine, seed_other, weight, state, keep, give):
    low = lanes() < half_head

    def grads(gate, up, grad):
        squashed = squash(gate)
        activated = gate * squashed
        return (
            grad * up * squashed * (1.0 + gate * (1.0 - squashed)),
            grad * activated,
            activated * up,
        )

    starts = [0, main, 2 * main, 3 * main, 3 * main + piece, packed]

    def step(chip, carry):
        feed = jnp.concatenate([feed_mine[chip], feed_other[chip]], axis=0)
        seed = jnp.concatenate([seed_mine[chip], seed_other[chip]], axis=0)
        first = grads(
            dot(feed, weight[:, :main]),
            dot(feed, weight[:, main : 2 * main]),
            dot(seed, weight[:, 2 * main : 3 * main]),
        )
        pair = dot(feed, weight[:, 3 * main : 3 * main + piece])
        rest = grads(pair, swapped_halves(pair), dot(seed, weight[:, 3 * main + piece :]))
        made = [value.astype(bf16) for value in first]
        made.append(jnp.where(low, rest[0], swapped_halves(rest[1])).astype(bf16))
        made.append(jnp.where(low, rest[2], 0.0).astype(bf16))
        for index, value in enumerate(made):
            state[0, chip, :, starts[index] : starts[index + 1]] = value[:piece]
            state[1, chip, :, starts[index] : starts[index + 1]] = value[piece:]
        result = dot_nt(made[0], weight[:, :main]) + dot_nt(made[1], weight[:, main : 2 * main])
        result = result + dot_nt(made[3], weight[:, 3 * main : 3 * main + piece])
        result = result.astype(bf16)
        keep[chip] = result[:piece]
        give[chip] = result[piece:]
        return carry

    lax.fori_loop(0, 4, step, 0)


def feed_sums_kernel(feed_mine, feed_other, seed_mine, seed_other, state, sums):
    rows = 4 * piece

    def step(block, carry):
        columns = pl.ds(pl.multiple_of(block * 2 * piece, 2 * piece), 2 * piece)

        def both(mine, other, low, high):
            total = dot_tn(
                mine[:, :, columns].reshape(rows, 2 * piece),
                state[0, :, :, low:high].reshape(rows, high - low),
            )
            total = total + dot_tn(
                other[:, :, columns].reshape(rows, 2 * piece),
                state[1, :, :, low:high].reshape(rows, high - low),
            )
            sums[columns, low:high] = total.astype(bf16)

        both(feed_mine, feed_other, 0, 2 * main)
        both(seed_mine, seed_other, 2 * main, 3 * main)
        both(feed_mine, feed_other, 3 * main, 3 * main + piece)
        both(seed_mine, seed_other, 3 * main + piece, packed)
        return carry

    lax.fori_loop(0, 4, step, 0)


def feed_out_kernel(state, weight, keep, give):
    rows = 4 * piece
    for core, ref in ((1, give), (0, keep)):
        hidden = state[core, :, :, 2 * main : 3 * main].reshape(rows, main)
        result = dot_nt(hidden, weight[:, 2 * main : 3 * main])
        hidden = state[core, :, :, 3 * main + piece :].reshape(rows, piece)
        result = result + dot_nt(hidden, weight[:, 3 * main + piece :])
        ref[...] = result.astype(bf16).reshape(4, piece, width)


def meet_kernel(keep, got, own, far, near, next_):
    for chip, out in enumerate((own, far, near, next_)):
        out[...] = (keep[chip].astype(f32) + got[chip].astype(f32)).astype(bf16)


def grad_mixed_kernel(own, far, near, next_, mixed, seed, gains, grad_out, low_out):
    grad = own[...].astype(f32) + far[...].astype(f32) + near[...].astype(f32) + next_[...].astype(f32)
    x = mixed[...]
    factor = mean_square_factor(x)
    normed = x * factor
    scaled = grad * wide_gain(gains, 8)
    back = factor * (scaled - normed * jnp.mean(scaled * normed, axis=-1, keepdims=True))
    result = seed[...].astype(f32) + back
    grad_out[...] = result
    low_out[...] = result.astype(bf16)


def output_kernel(own, far, near, next_, mixed, out):
    total = own[...].astype(f32) + far[...].astype(f32) + near[...].astype(f32) + next_[...].astype(f32)
    out[...] = (mixed[...] + total).astype(bf16)


def input_kernel(own, far, near, next_, tokens, grad_mixed, gains, out):
    grad = own[...].astype(f32) + far[...].astype(f32) + near[...].astype(f32) + next_[...].astype(f32)
    x = tokens[...].astype(f32)
    factor = mean_square_factor(x)
    normed = x * factor
    scaled = grad * wide_gain(gains, 0)
    back = factor * (scaled - normed * jnp.mean(scaled * normed, axis=-1, keepdims=True))
    out[...] = (grad_mixed[...] + back).astype(bf16)


def backward_kernel(
    info, pack, gains, branch_mine, branch_other, out_rows, table, log_sum, kept,
    keep, give, raw_out, gain_out,
    grads, query_grad, key_grad, value_grad, held, sem,
):
    copy = pltpu.make_async_copy(kept.at[pl.ds(0, 56)], held, sem)
    copy.start()
    queries, keys, values, query_normed, key_normed, query_factor, key_factor = [
        held.at[pl.ds(8 * i, 8)] for i in range(7)
    ]
    me = info[1]
    low = lanes() < half_head
    early = lanes() % half_head < half_head // 2
    gain_query = gains[0:1, piece : 2 * piece]
    gain_key = gains[1:2, piece : 2 * piece]
    for core, ref in enumerate((branch_mine, branch_other)):
        grad = dot_nt(ref[...].reshape(4 * piece, width), out_rows[...]).astype(bf16)
        for chip in range(4):
            grads[place_of(me, core, chip)] = grad[chip * piece : (chip + 1) * piece]
    masks = head_masks()
    copy.wait()
    keys_across = keys[...].reshape(width, piece).T.astype(bf16)
    key_grad[...] = jnp.zeros_like(key_grad)
    value_grad[...] = jnp.zeros_like(value_grad)
    scale = half_head**-0.5
    for block in range(4):
        count = 2 * piece * (block + 1)
        some = 2 * block + 2
        key = keys[:some].reshape(count, piece).astype(bf16)
        value = values[:some].reshape(count, piece).astype(bf16)
        stacked = block_queries(queries, block, masks)
        grad = block_queries(grads, block, masks)
        chance = jnp.exp(block_scores(key, stacked, count) - log_sum[block])
        grad_chance = dot_nt(value, grad)
        inner = jnp.sum(chance * grad_chance, axis=0, keepdims=True)
        grad_score = (chance * (grad_chance - inner)).astype(bf16)
        value_grad[:some] += dot(chance.astype(bf16), grad).reshape(some, piece, piece)
        key_grad[:some] += dot(grad_score, stacked).reshape(some, piece, piece)
        result = pick_heads(dot(keys_across[:, :count], grad_score))
        query_grad[2 * block] = result[:piece]
        query_grad[2 * block + 1] = result[piece:]

    def finish(place, sums):
        cos, sin = angle_tables(table, place)
        sin = jnp.where(early, sin, -sin)

        def turn_back(value):
            return value * cos + turned(value, early) * sin

        grad = turn_back(rounded(query_grad[place] * scale))
        normed = query_normed[place]
        query_sum = sums[0] + jnp.sum(grad * normed, axis=0, keepdims=True)
        scaled = grad * gain_query
        mean = halves_sum(scaled * normed, low) / half_head
        raw_query = query_factor[place] * (scaled - normed * mean)
        both = key_grad[place]
        grad = turn_back(rounded((both + swapped_halves(both)) * scale))
        normed = key_normed[place]
        key_sum = sums[1] + jnp.sum(grad * normed, axis=0, keepdims=True)
        scaled = grad * gain_key
        mean = jnp.mean(scaled * normed, axis=-1, keepdims=True)
        raw_key = key_factor[place] * (scaled - normed * mean)
        both = value_grad[place]
        raw_value = both + swapped_halves(both)
        partner = place ^ me
        core, chip = partner % 2, partner // 2
        raw_out[core, chip, :, :piece] = raw_query.astype(bf16)
        raw_out[core, chip, :, piece:] = jnp.where(low, raw_key, raw_value).astype(bf16)
        return (query_sum, key_sum)

    zero = jnp.zeros((1, piece), f32)
    query_sum, key_sum = lax.fori_loop(0, 8, finish, (zero, zero))
    query_sum = query_sum + swapped_halves(query_sum)
    gain_out[...] = jnp.concatenate([query_sum, key_sum, jnp.zeros((6, piece), f32)], axis=0)
    for core, ref in ((1, give), (0, keep)):
        ref[...] = (
            dot_nt(raw_out[core].reshape(4 * piece, 2 * piece), qkv_weight(pack))
            .astype(bf16)
            .reshape(4, piece, width)
        )


def out_sums_kernel(info, attended, branch_mine, branch_other, sums):
    me = info[1]
    rows = 4 * piece
    total = dot_tn(attended[:4].reshape(rows, piece), branch_mine[...].reshape(rows, width))
    total = total + dot_tn(attended[4:].reshape(rows, piece), branch_other[...].reshape(rows, width))
    total = total.astype(bf16)
    for place in range(8):
        sums[slot_of(me, place)] = total[:, place * piece : (place + 1) * piece]


def pair_kernel(parts, got, own, far, near, next_):
    for chip, out in enumerate((own, far, near, next_)):
        out[0] = parts[chip]
        out[1] = got[chip]


def attention_sums_kernel(info, mixer, raw, own, far, near, next_, gain_sums, sums):
    total = dot_tn(mixer[...].reshape(width, width), raw[...].reshape(width, 2 * piece))
    sums[:, :half_head, : 2 * piece] = total.astype(bf16).reshape(16, half_head, 2 * piece)
    me = info[1]
    for chip, ref in enumerate((own, far, near, next_)):
        for core in range(2):
            place = place_of(me, core, chip)
            for index in range(2):
                block = ref[core, index * half_head : (index + 1) * half_head, :]
                sums[2 * place + index, :half_head, 2 * piece :] = block
    value = gain_sums[...]
    high = value.astype(bf16).astype(f32)
    tail = jnp.concatenate([high, value - high], axis=0)
    tail = jnp.concatenate([tail, jnp.zeros((16, 2 * piece), f32)], axis=1).astype(bf16)
    for index in range(16):
        sums[index, half_head:, :] = tail


def feed_total_kernel(parts, total, low):
    value = parts[0].astype(f32)
    for index in range(1, 16):
        value = value + parts[index].astype(f32)
    total[...] = value
    low[...] = value.astype(bf16)


def feed_outputs_kernel(info, own, other, gate, up, down):
    context = info[2]
    late = context == 1
    low = lanes() < half_head
    here = pl.multiple_of(context * main, main)
    there = pl.multiple_of((1 - context) * main, main)
    for index, ref in enumerate((gate, up, down)):
        span = slice(index * main, (index + 1) * main)
        ref[:, pl.ds(here, main)] = own[:, span].astype(f32)
        ref[:, pl.ds(there, main)] = other[:, span].astype(f32)
    span = slice(3 * main, 3 * main + piece)
    mine, far = own[:, span].astype(f32), other[:, span].astype(f32)
    first, second = jnp.where(late, far, mine), jnp.where(late, mine, far)
    gate[:, 2 * main :] = jnp.where(low, first, swapped_halves(second))
    up[:, 2 * main :] = jnp.where(low, swapped_halves(first), second)
    span = slice(3 * main + piece, packed)
    mine, far = own[:, span].astype(f32), other[:, span].astype(f32)
    first, second = jnp.where(late, far, mine), jnp.where(late, mine, far)
    down[:, 2 * main :] = jnp.where(low, first, swapped_halves(second))


def attention_total_kernel(parts, pack, feed_pack, feed_total, final):
    value = parts[0].astype(f32)
    for index in range(1, 16):
        value = value + parts[index].astype(f32)
    weights = value[:half_head]
    tail = value[half_head : half_head + 8, :piece] + value[half_head + 8 :, :piece]
    first = jnp.sum(
        pack[0, :half_head, : 2 * piece].astype(f32) * weights[:, : 2 * piece],
        axis=1,
        keepdims=True,
    )
    feed = jnp.sum(
        feed_pack[0, :, : 2 * main].astype(f32) * feed_total[:, : 2 * main].astype(f32), axis=1, keepdims=True
    )
    span = slice(3 * main, 3 * main + piece)
    feed = feed + jnp.sum(
        feed_pack[0, :, span].astype(f32) * feed_total[:, span].astype(f32), axis=1, keepdims=True
    )
    lane = lanes(half_head)
    spread = jnp.where(lane == 0, first, jnp.where(lane == 1, feed, 0.0))
    spread = jnp.concatenate([spread, jnp.zeros_like(spread)], axis=0).T
    rows = jnp.concatenate([spread[:8], tail], axis=0)
    rows = jnp.concatenate([rows, jnp.zeros((16, 2 * piece), f32)], axis=1)
    result = jnp.concatenate([weights, rows], axis=0).astype(bf16)
    for index in range(8):
        final[index] = result


def attention_outputs_kernel(small, final, query, key, value, out, gains):
    low = lanes() < half_head
    for place in range(8):
        span = slice(place * piece, (place + 1) * piece)
        query[:, span] = final[place, :half_head, :piece].astype(f32)
        out[:, span] = final[place, :half_head, 2 * piece :].astype(f32)
    for pair in range(4):
        span = slice(pair * piece, (pair + 1) * piece)
        first = final[2 * pair, :half_head, piece : 2 * piece].astype(f32)
        second = final[2 * pair + 1, :half_head, piece : 2 * piece].astype(f32)
        key[:, span] = jnp.where(low, first, swapped_halves(second))
        value[:, span] = jnp.where(low, swapped_halves(first), second)
    tail = final[0, half_head:, :piece].astype(f32)
    for place in range(1, 8):
        tail = tail + final[place, half_head:, :piece].astype(f32)
    both = small[0:1, :]
    gains[0:1] = tail[0:1] / both
    gains[1:2] = tail[1:2] / swapped_halves(both)
    gains[2:4] = tail[8:10]


def swap(value, bits):
    return lax.ppermute(value, line, [(i, i ^ bits) for i in range(8)])


def line_gather(block, *others):
    far, near, next_ = swap(block, 2), swap(block, 4), swap(block, 6)
    mine = jnp.stack([after(block, *others), far, near, next_])
    return mine, swap(mine, 1)


def line_reduce(keep, give, *others):
    got = swap(give, 1)
    keep = after(keep, *others)
    sent = call(meet_kernel, [shape((piece, width), bf16)] * 4, keep, got, micros=2, name="meet")
    return sent[0], swap(sent[1], 2), swap(sent[2], 4), swap(sent[3], 6)


def line_turn(parts):
    got = swap(parts[4:], 1)
    pair = shape((2,) + parts.shape[1:], parts.dtype)
    sent = call(pair_kernel, [pair] * 4, parts, got, micros=1, name="pair")
    return sent[0], swap(sent[1], 2), swap(sent[2], 4), swap(sent[3], 6)


def after(value, *others):
    return lax.optimization_barrier((value,) + others)[0]


def across(value):
    return lax.all_to_all(value, "shard", 0, 0, tiled=True)


def rope_table():
    frequency = rope_base ** (-np.arange(0, half_head, 2) / half_head)
    frequency = np.concatenate([frequency] * 4)[None, :]
    starts = np.arange(8)[:, None] * piece * frequency
    steps = np.arange(piece)[:, None] * frequency
    rows = [np.cos(starts), np.sin(starts), np.cos(steps), np.sin(steps)]
    return jnp.asarray(np.concatenate(rows), f32)


def on_device(
    tokens,
    cotangent,
    attention_gain,
    query_weight,
    key_weight,
    value_weight,
    query_gain,
    key_gain,
    out_weight,
    feed_gain,
    gate_weight,
    up_weight,
    down_weight,
):
    shard = lax.axis_index("shard")
    context = lax.axis_index("context")
    place = context * 4 + lax.axis_index("tensor")
    info = jnp.stack([shard, place, context]).astype(jnp.int32)
    token_rows = tokens.reshape(piece, width)
    seed_rows = cotangent.reshape(piece, width)
    small = jnp.concatenate(
        [attention_gain, feed_gain, query_gain, key_gain, jnp.zeros((120,), bf16)]
    )
    small = small.astype(f32).reshape(2, piece)
    (own_pack,) = call(
        pack_kernel,
        [shape((16, 80, 3 * piece), bf16)],
        info, small, query_weight, key_weight, value_weight, out_weight,
        micros=6,
        name="pack",
        fetch=True,
    )
    (feed_pack,) = call(
        feed_pack_kernel,
        [shape((16, half_head, packed), bf16)],
        info, gate_weight, up_weight, down_weight.T,
        micros=12,
        name="feed_pack",
        fetch=True,
    )
    pack = after(across(own_pack), feed_pack)
    feed_full = across(after(feed_pack, pack)).reshape(width, packed)
    out_columns = pack[:, :half_head, 2 * piece :].reshape(width, piece)
    tokens_mine, tokens_other = line_gather(token_rows, own_pack)
    seed_mine, seed_other = line_gather(after(seed_rows, tokens_mine))
    table = rope_table()
    cube = (8, piece, piece)
    attended_heads, mixer, log_sum, gains, kept = call(
        forward_kernel,
        [
            shape(cube, bf16), shape((2, 4, piece, width), bf16), shape((4, 1, 4 * piece), f32),
            shape((16, 3 * piece), f32), shape((1100, piece, piece), f32),
        ],
        info, pack, after(tokens_mine, seed_mine), tokens_other, table,
        micros=36,
        scratch=[
            pltpu.VMEM((2, 4, piece, 2 * piece), f32),
            pltpu.VMEM((56, piece, piece), f32),
            pltpu.SemaphoreType.DMA,
        ],
        name="attention_forward",
    )
    out_mine, out_other = line_gather(out_columns)
    attended = line_turn(attended_heads)
    mixed, feed_input, out_rows = call(
        branch_kernel,
        [shape((piece, width), f32), shape((piece, width), bf16), shape((piece, width), bf16)],
        info, *attended, out_mine, out_other, token_rows, gains,
        micros=2,
        scratch=[pltpu.VMEM((piece, width), bf16)],
        name="branch",
    )
    feed_mine, feed_other = line_gather(feed_input, feed_full)
    rows = (feed_mine, feed_other, seed_mine, seed_other)
    line_shape = shape((4, piece, width), bf16)
    state, grad_keep, grad_give = call(
        feed_kernel,
        [shape((2, 4, piece, packed), bf16), line_shape, line_shape],
        *rows, feed_full,
        micros=11,
        name="feed_forward",
    )
    grad_feed = line_reduce(grad_keep, grad_give)
    (sums,) = call(
        feed_sums_kernel,
        [shape((width, packed), bf16)],
        *rows, state,
        micros=8,
        name="feed_sums",
    )
    feed_parts = across(sums.reshape(16, half_head, packed))
    feed_total, feed_low = call(
        feed_total_kernel,
        [shape((half_head, packed), f32), shape((half_head, packed), bf16)],
        feed_parts,
        name="feed_total",
    )
    grad_mixed, grad_branch = call(
        grad_mixed_kernel,
        [shape((piece, width), f32), shape((piece, width), bf16)],
        after(grad_feed[0], sums), *grad_feed[1:], mixed, seed_rows, gains,
        name="grad_mixed",
    )
    (out_keep, out_give) = call(
        feed_out_kernel,
        [line_shape, line_shape],
        after(state, grad_branch), feed_full,
        micros=4,
        name="feed_out",
    )
    branch_mine, branch_other = line_gather(grad_branch, out_keep)
    (out_sums,) = call(
        out_sums_kernel,
        [shape(cube, bf16)],
        info, attended_heads, branch_mine, branch_other,
        micros=1,
        name="out_sums",
    )
    out_sums = line_turn(out_sums)
    cube_f32 = pltpu.VMEM(cube, f32)
    mixer_keep, mixer_give, raw, gain_sums = call(
        backward_kernel,
        [
            shape((4, piece, width), bf16),
            shape((4, piece, width), bf16),
            shape((2, 4, piece, 2 * piece), bf16),
            shape((8, piece), f32),
        ],
        info, pack, gains, branch_mine, branch_other, out_rows, table, log_sum, kept,
        micros=11,
        scratch=[
            pltpu.VMEM(cube, bf16), cube_f32, cube_f32, cube_f32,
            pltpu.VMEM((56, piece, piece), f32), pltpu.SemaphoreType.DMA,
        ],
        name="attention_backward",
    )
    (attention_sums,) = call(
        attention_sums_kernel,
        [shape((16, 80, 3 * piece), bf16)],
        info, after(mixer, feed_low), raw, *out_sums, gain_sums,
        micros=4,
        name="attention_sums",
    )
    grad_mixer = line_reduce(mixer_keep, mixer_give)
    attention_parts = across(after(attention_sums, grad_mixer[0]))
    (input_gradient,) = call(
        input_kernel,
        [shape((piece, width), bf16)],
        *grad_mixer, token_rows, grad_mixed, gains,
        name="input_gradient",
        store=True,
    )
    (output,) = call(
        output_kernel,
        [shape((piece, width), bf16)],
        *line_reduce(out_keep, after(out_give, raw)), mixed,
        name="output",
        store=True,
    )
    feed_far = swap(feed_low, 4)
    long = shape((half_head, 2 * main + piece), f32)
    gate_part, up_part, down_part = call(
        feed_outputs_kernel, [long, long, long], info, feed_total, feed_far, name="feed_outputs", store=True
    )
    (final,) = call(
        attention_total_kernel,
        [shape((8, 80, 3 * piece), bf16)],
        attention_parts, own_pack, feed_pack, feed_total,
        name="attention_total",
    )
    final = lax.all_to_all(final, line, 0, 0, tiled=True)
    query_part, key_part, value_part, out_part, gain_parts = call(
        attention_outputs_kernel,
        [
            shape((half_head, width), f32), shape((half_head, main), f32),
            shape((half_head, main), f32), shape((half_head, width), f32), shape((4, piece), f32),
        ],
        small, final,
        name="attention_outputs", store=True,
    )
    head_gains = lax.dynamic_slice(gain_parts, (2, 4 * shard), (2, 4))
    return (
        output.reshape(1, piece, width),
        input_gradient.reshape(1, piece, width),
        gain_parts[0, :half_head],
        query_part,
        key_part,
        value_part,
        head_gains[0],
        head_gains[1],
        out_part,
        gain_parts[1, :half_head],
        gate_part,
        up_part,
        down_part.T,
    )


def solution(mesh):
    tokens = P("shard", ("context", "tensor"), None)
    rows = P("shard", None)
    weights = (P("shard"), rows, rows, rows, P("shard"), P("shard"), rows, P("shard")) + (
        P("shard", "tensor"),
        P("shard", "tensor"),
        P("tensor", "shard"),
    )
    placed = (tokens, tokens) + weights
    return jax.shard_map(
        on_device, mesh=mesh, in_specs=placed, out_specs=placed, check_vma=False
    )
```

time: 433 us -> 239 us (0.55); the launches traced: 424 us -> 238 us
  local copies, waits for them, and re-layouts: 137 us -> 19 us
  other arithmetic: 77.4 us -> 5.22 us
  Pallas kernels: 0 us -> 70.5 us
  matrix products: 56.7 us -> 0 us
  starting transfers between devices: 71.3 us -> 93.4 us
  waiting for transfers between devices: 65.6 us -> 48.4 us
  between operations: 16.4 us -> 1.31 us
    pallas_call x0 -> x22, Pallas kernels: none -> 70.5 us  [call(): pl.pallas_call(run, out_shape=tuple(outs), in_specs=[smem if i not in arr...]
    dot_general x27 -> x0, matrix products: 56.7 us -> none  [the longest x5 14.3 us: dot(): return jnp.dot(a, b, preferred_element_type=f32)]
    another operation x20 -> x6, other arithmetic: 26.4 us -> 4.65 us  [the longest x5 4.06 us: line_gather(): mine = jnp.stack([after(block, *others), far, near, next_])]
    another operation x11 -> x0, local copies, waits for them, and re-layouts: 20 us -> none  [the longest x5 15.2 us: line_gather(): return jnp.stack([mine, other])]
    ppermute x45 -> x41, waiting for transfers between devices: 49.8 us -> 31.2 us  [swap(): return lax.ppermute(value, line, [(i, i ^ bits) for i in range(8)])]
    slice x24 -> x3, local copies, waits for them, and re-layouts: 18.4 us -> 0.79 us  [the longest x1 0.77 us: on_device(): out_columns = pack[:, :half_head, 2 * piece:].reshape(width, piece)]
    convert_element_type x16 -> x1, other arithmetic: 17.2 us -> 0.57 us  [on_device(): small = small.astype(f32).reshape(2, piece)]
    all_to_all x3 -> x5, starting transfers between devices: 18.9 us -> 35.5 us  [the longest x4 25.6 us: across(): return lax.all_to_all(value, 'shard', 0, 0, tiled=True)]
  transfers between devices with their start and end apart: 49 -> 46, of which waited for: 15 -> 17; matrix products, arithmetic and copies ran while one was open for 54% -> 4% of each run, Pallas kernels for 0% -> 24%
where the time goes in v2:
time: 239 us; the launch traced here: 238 us
  starting transfers between devices  93.4 us (39%)
  Pallas kernels  70.5 us (29%)
  waiting for transfers between devices  48.4 us (20%)
  local copies, waits for them, and re-layouts  19 us (8%)
  other arithmetic  5.22 us (2%)
    pallas_call x22, Pallas kernels, call(): pl.pallas_call(run, out_shape=tuple(outs), in_specs=[smem if i not in arr...  70.5 us
    ppermute x41, starting transfers between devices, swap(): return lax.ppermute(value, line, [(i, i ^ bits) for i in range(8)])  58 us
    ppermute x41, waiting for transfers between devices, swap(): return lax.ppermute(value, line, [(i, i ^ bits) for i in range(8)])  31.2 us
    all_to_all x4, starting transfers between devices, across(): return lax.all_to_all(value, 'shard', 0, 0, tiled=True)  25.6 us
    all_to_all x4, waiting for transfers between devices, across(): return lax.all_to_all(value, 'shard', 0, 0, tiled=True)  17.2 us
    unnamed x82, local copies, waits for them, and re-layouts  14.4 us
    all_to_all x1, starting transfers between devices, on_device(): final = lax.all_to_all(final, line, 0, 0, tiled=True)  9.9 us
  transfers between devices with their start and end apart: 46, of which 17 were waited for; matrix products, arithmetic and copies ran while one was open for 4% of the time, Pallas kernels for 24%

profile of v2, /device:TPU:1, one launch (start us, length us, event | category | flops | bytes accessed | tf_op | source)
XLA Modules:
  0.0 237.9 jit_solution(4594075225666425719)
XLA Ops:
  0.6 3.4 %collective-permute-start.2 = (bf16[128,1024]{1,0:T(8,128)(2,1)}, bf16[128,1024]{1,0:T(8,128)(2,1)S(1)}, u32[]{:S(2)}, u32[]{:S(2)}) collective-permute-start(bf16[128,1024]{1,0:T(8,128)(2,1)} %bitcast.48), channel_id=1, source_target_pairs={{0,6},{1,7},{2,4},{3,5},{4,2},{5,3},{6,0},{7,1},{8,14},{9,15},{10,... | collective-permute-start | bytes 786440 | tf_op jit(solution)/shard_map/ppermute | solution.py:642
  4.0 1.3 collective-permute-start
  5.3 2.8 %concatenate.3 = bf16[256]{0:T(256)(128)(2,1)S(1)} concatenate(bf16[64]{0:T(256)(128)(2,1)} %param.16, bf16[64]{0:T(256)(128)(2,1)} %param.23, bf16[4]{0:T(256)(128)(2,1)} %param.20, bf16[4]{0:T(256)(128)(2,1)} %param.21, bf16[120]{0:T(256)(128)(2,1)S(1)} %broadcast_in_dim.3), dimensions={0} | concatenate | bytes 1024 | tf_op jit(solution)/shard_map/concatenate | solution.py:703
  9.2 3.0 %pack.1.refs_1_ = bf16[16,80,384]{2,1,0:T(8,128)(2,1)} custom-call(s32[3]{0:T(128)} %pad_add_fusion.refs_0_, f32[2,128]{1,0:T(2,128)} %bitcast_convert_fusion.refs_1_.refs_0_, bf16[64,1024]{1,0:T(8,128)(2,1)} %refs_2_.2, bf16[64,512]{1,0:T(8,128)(2,1)} %refs_3_.1, bf16[64,512]{1,0:T(8,128)(2,1)} %refs_4_.2, bf16[64,1024]{1,0:T(8,128)(2,1)} %refs_5_.1), custom_call_target="tpu_custom_call" | custom-call | flops 6000000000 | bytes 1048576 | tf_op jit(solution)/shard_map/pack/pallas_call | solution.py:89
  12.3 8.0 %all-to-all-start = ((bf16[16,80,384]{2,1,0:T(8,128)(2,1)}), bf16[16,80,384]{2,1,0:T(8,128)(2,1)S(1)}, u32[]{:S(2)}, u32[]{:S(2)}) async-start(bf16[16,80,384]{2,1,0:T(8,128)(2,1)} %pack.1.refs_1_), calls=%async_computation | async-start | bytes 1966080 | tf_op jit(solution)/shard_map/all_to_all | solution.py:670
  20.5 2.6 %collective-permute-start.5 = (bf16[128,1024]{1,0:T(8,128)(2,1)S(1)}, bf16[128,1024]{1,0:T(8,128)(2,1)S(1)}, u32[]{:S(2)}, u32[]{:S(2)}) collective-permute-start(bf16[128,1024]{1,0:T(8,128)(2,1)S(1)} %bitcast.44), channel_id=1, source_target_pairs={{0,6},{1,7},{2,4},{3,5},{4,2},{5,3},{6,0},{7,1},{8,14},{9,15},{10,... | collective-permute-start | bytes 786440 | tf_op jit(solution)/shard_map/ppermute | solution.py:642
  23.0 1.4 collective-permute-start.3
  24.4 2.6 %collective-permute-start.6 = (bf16[4,128,1024]{2,1,0:T(8,128)(2,1)S(1)}, bf16[4,128,1024]{2,1,0:T(8,128)(2,1)}, u32[]{:S(2)}, u32[]{:S(2)}) collective-permute-start(bf16[4,128,1024]{2,1,0:T(8,128)(2,1)S(1)} %pad_maximum_fusion.refs_2_), channel_id=1, source_target_pairs={{0,1},{1,0},{2,3},{3,2},{4,5},{5,4},{6,7},{7,6},{8,9},{9,8},{10,11... | collective-permute-start | bytes 3145736 | tf_op jit(solution)/shard_map/ppermute | solution.py:642
  27.1 3.8 %feed_pack.1.refs_2_ = bf16[16,64,1792]{2,1,0:T(8,128)(2,1)} custom-call(s32[3]{0:T(128)} %pad_add_fusion.refs_0_, bf16[64,1152]{1,0:T(8,128)(2,1)} %refs_1_.1, bf16[64,1152]{1,0:T(8,128)(2,1)} %refs_2_.3, bf16[64,1152]{1,0:T(8,128)(2,1)} %bitcast.64), custom_call_target="tpu_custom_call" | custom-call | flops 12000000000 | bytes 1048576 | tf_op jit(solution)/shard_map/feed_pack/pallas_call | solution.py:89
  30.9 3.8 %all-to-all-done.refs_1_ = bf16[16,80,384]{2,1,0:T(8,128)(2,1)S(1)} async-done(((bf16[16,80,384]{2,1,0:T(8,128)(2,1)}), bf16[16,80,384]{2,1,0:T(8,128)(2,1)S(1)}, u32[]{:S(2)}, u32[]{:S(2)}) %all-to-all-start) | async-done | bytes 983072 | tf_op jit(solution)/shard_map/all_to_all | solution.py:670
  35.5 2.5 %collective-permute-start.13 = (bf16[1024,128]{1,0:T(8,128)(2,1)}, bf16[1024,128]{1,0:T(8,128)(2,1)}, u32[]{:S(2)}, u32[]{:S(2)}) collective-permute-start(bf16[1024,128]{1,0:T(8,128)(2,1)} %bitcast.15), channel_id=1, source_target_pairs={{0,6},{1,7},{2,4},{3,5},{4,2},{5,3},{6,0},{7,1},{8,14},{9,15},{10,... | collective-permute-start | bytes 786440 | tf_op jit(solution)/shard_map/ppermute | solution.py:642
  38.0 1.4 collective-permute-start.11
  41.3 4.6 %all-to-all-start.1 = ((bf16[16,64,1792]{2,1,0:T(8,128)(2,1)}), bf16[16,64,1792]{2,1,0:T(8,128)(2,1)}, u32[]{:S(2)}, u32[]{:S(2)}) async-start(bf16[16,64,1792]{2,1,0:T(8,128)(2,1)} %feed_pack.1.refs_2_), calls=%async_computation.1 | async-start | bytes 7340032 | tf_op jit(solution)/shard_map/all_to_all | solution.py:670
  46.0 2.1 collective-permute-done.11
  48.1 1.3 pad_maximum_fusion.2.refs_5_
  49.4 4.5 %collective-permute-start.14 = (bf16[4,1024,128]{2,1,0:T(8,128)(2,1)S(1)}, bf16[4,1024,128]{2,1,0:T(8,128)(2,1)S(1)}, u32[]{:S(2)}, u32[]{:S(2)}) collective-permute-start(bf16[4,1024,128]{2,1,0:T(8,128)(2,1)S(1)} %pad_maximum_fusion.2.refs_5_), channel_id=1, source_target_pairs={{0,1},{1,0},{2,3},{3,2},{4,5},{5,4},{6,7},{7,6},{8,9},{9,8},{10,11... | collective-permute-start | bytes 3145736 | tf_op jit(solution)/shard_map/ppermute | solution.py:642
  54.0 11.3 %attention_forward.1 = (bf16[8,128,128]{2,1,0:T(8,128)(2,1)S(1)}, bf16[2,4,128,1024]{3,2,1,0:T(8,128)(2,1)S(1)}, f32[4,1,512]{2,1,0:T(1,128)S(1)}, f32[16,384]{1,0:T(8,128)S(1)}, f32[1100,128,128]{2,1,0:T(8,128)}) custom-call(s32[3]{0:T(128)S(1)} %copy-done.10, bf16[16,80,384]{2,1,0:T(8,128)(2,1)S(1)} %all-to-all-done.refs_1_, ...), custom_call_target="tpu_custom_call" | custom-call | flops 35999997952 | bytes 1048576 | tf_op jit(solution)/shard_map/attention_forward/pallas_call | solution.py:89
  65.4 1.3 collective-permute-done.7.refs_1_
  66.7 1.7 collective-permute-start.8
  68.4 1.5 collective-permute-start.9
  70.1 1.9 collective-permute-done.8.refs_2_
  72.0 1.5 collective-permute-done.9.refs_3_
  74.6 1.5 branch.1
  76.2 1.5 collective-permute-start.17
  77.6 2.5 %collective-permute-start.15 = (bf16[128,1024]{1,0:T(8,128)(2,1)S(1)}, bf16[128,1024]{1,0:T(8,128)(2,1)}, u32[]{:S(2)}, u32[]{:S(2)}) collective-permute-start(bf16[128,1024]{1,0:T(8,128)(2,1)S(1)} %get-tuple-element.86), channel_id=1, source_target_pairs={{0,2},{1,3},{2,0},{3,1},{4,6},{5,7},{6,4},{7,5},{8,10},{9,11},{10,... | collective-permute-start | bytes 786440 | tf_op jit(solution)/shard_map/ppermute | solution.py:642
  80.1 2.3 collective-permute-start.19
  82.4 4.2 %all-to-all-done.1 = bf16[16,64,1792]{2,1,0:T(8,128)(2,1)} async-done(((bf16[16,64,1792]{2,1,0:T(8,128)(2,1)}), bf16[16,64,1792]{2,1,0:T(8,128)(2,1)}, u32[]{:S(2)}, u32[]{:S(2)}) %all-to-all-start.1) | async-done | bytes 3670048 | tf_op jit(solution)/shard_map/all_to_all | solution.py:670
  86.6 3.8 %collective-permute-done.15 = bf16[128,1024]{1,0:T(8,128)(2,1)} collective-permute-done((bf16[128,1024]{1,0:T(8,128)(2,1)S(1)}, bf16[128,1024]{1,0:T(8,128)(2,1)}, u32[]{:S(2)}, u32[]{:S(2)}) %collective-permute-start.15) | collective-permute-done | bytes 262176 | tf_op jit(solution)/shard_map/ppermute | solution.py:642
  91.7 4.3 %collective-permute-start.18 = (bf16[4,128,1024]{2,1,0:T(8,128)(2,1)S(1)}, bf16[4,128,1024]{2,1,0:T(8,128)(2,1)S(1)}, u32[]{:S(2)}, u32[]{:S(2)}) collective-permute-start(bf16[4,128,1024]{2,1,0:T(8,128)(2,1)S(1)} %pad_maximum_fusion.3.refs_0_), channel_id=1, source_target_pairs={{0,1},{1,0},{2,3},{3,2},{4,5},{5,4},{6,7},{7,6},{8,9},{9,8},{10,11... | collective-permute-start | bytes 3145736 | tf_op jit(solution)/shard_map/ppermute | solution.py:642
  95.9 2.3 collective-permute-done.18.refs_1_
  98.2 10.5 %feed_forward.1 = (bf16[2,4,128,1792]{3,2,1,0:T(8,128)(2,1)S(1)}, bf16[4,128,1024]{2,1,0:T(8,128)(2,1)S(1)}, bf16[4,128,1024]{2,1,0:T(8,128)(2,1)S(1)}) custom-call(bf16[4,128,1024]{2,1,0:T(8,128)(2,1)S(1)} %pad_maximum_fusion.3.refs_0_, bf16[4,128,1024]{2,1,0:T(8,128)(2,1)S(1)} %collective-permute-done.18.refs_1_, ...), custom_call_target="tpu_custom_call" | custom-call | flops 11000000512 | bytes 1048576 | tf_op jit(solution)/shard_map/feed_forward/pallas_call | solution.py:89
  109.2 2.3 collective-permute-done.20.refs_1_
  112.5 2.0 collective-permute-start.21
  115.7 6.4 %feed_sums.1 = bf16[1024,1792]{1,0:T(8,128)(2,1)S(1)} custom-call(bf16[4,128,1024]{2,1,0:T(8,128)(2,1)S(1)} %pad_maximum_fusion.3.refs_0_, bf16[4,128,1024]{2,1,0:T(8,128)(2,1)S(1)} %collective-permute-done.18.refs_1_, bf16[4,128,1024]{2,1,0:T(8,128)(2,1)S(1)} %pad_maximum_fusion.1.refs_2_, bf16[4,128,1024]{2,1,0:T(8,128)(2,1)} %collective-permute-done.19.refs_3_, ...), custom_call_target="tpu_custom_call" | custom-call | flops 8000000000 | bytes 1048576 | tf_op jit(solution)/shard_map/feed_sums/pallas_call | solution.py:89
  122.2 1.8 copy-done.1
  124.0 6.0 %all-to-all-start.2 = ((bf16[16,64,1792]{2,1,0:T(8,128)(2,1)}), bf16[16,64,1792]{2,1,0:T(8,128)(2,1)}, u32[]{:S(2)}, u32[]{:S(2)}) async-start(bf16[16,64,1792]{2,1,0:T(8,128)(2,1)} %bitcast.43), calls=%async_computation.2 | async-start | bytes 7340032 | tf_op jit(solution)/shard_map/all_to_all | solution.py:670
  130.1 1.4 grad_mixed.1
  132.3 2.5 %collective-permute-start.26 = (bf16[128,1024]{1,0:T(8,128)(2,1)S(1)}, bf16[128,1024]{1,0:T(8,128)(2,1)S(1)}, u32[]{:S(2)}, u32[]{:S(2)}) collective-permute-start(bf16[128,1024]{1,0:T(8,128)(2,1)S(1)} %get-tuple-element.100), channel_id=1, source_target_pairs={{0,6},{1,7},{2,4},{3,5},{4,2},{5,3},{6,0},{7,1},{8,14},{9,15},{10,... | collective-permute-start | bytes 786440 | tf_op jit(solution)/shard_map/ppermute | solution.py:642
  134.8 1.4 collective-permute-start.24
  136.2 4.0 %feed_out.1 = (bf16[4,128,1024]{2,1,0:T(8,128)(2,1)S(1)}, bf16[4,128,1024]{2,1,0:T(8,128)(2,1)}) custom-call(bf16[2,4,128,1792]{3,2,1,0:T(8,128)(2,1)S(1)} %copy-done.22, bf16[1024,1792]{1,0:T(8,128)(2,1)} %bitcast.20.refs_4_.refs_1_), custom_call_target="tpu_custom_call" | custom-call | flops 4000000000 | bytes 1048576 | tf_op jit(solution)/shard_map/feed_out/pallas_call | solution.py:89
  141.1 5.3 %collective-permute-done.24 = bf16[128,1024]{1,0:T(8,128)(2,1)S(1)} collective-permute-done((bf16[128,1024]{1,0:T(8,128)(2,1)S(1)}, bf16[128,1024]{1,0:T(8,128)(2,1)S(1)}, u32[]{:S(2)}, u32[]{:S(2)}) %collective-permute-start.24) | collective-permute-done | bytes 262176 | tf_op jit(solution)/shard_map/ppermute | solution.py:642
  146.6 2.9 %collective-permute-start.27 = (bf16[4,128,1024]{2,1,0:T(8,128)(2,1)S(1)}, bf16[4,128,1024]{2,1,0:T(8,128)(2,1)S(1)}, u32[]{:S(2)}, u32[]{:S(2)}) collective-permute-start(bf16[4,128,1024]{2,1,0:T(8,128)(2,1)S(1)} %pad_maximum_fusion.4.refs_3_.refs_2_), channel_id=1, source_target_pairs={{0,1},{1,0},{2,3},{3,2},{4,5},{5,4},{6,7},{7,6},{8,9},{9,8},{10,11... | collective-permute-start | bytes 3145736 | tf_op jit(solution)/shard_map/ppermute | solution.py:642
  149.5 2.3 collective-permute-done.27.refs_4_.refs_3_
  151.8 9.8 %attention_backward.1 = (bf16[4,128,1024]{2,1,0:T(8,128)(2,1)S(1)}, bf16[4,128,1024]{2,1,0:T(8,128)(2,1)S(1)}, bf16[2,4,128,256]{3,2,1,0:T(8,128)(2,1)S(1)}, f32[8,128]{1,0:T(8,128)S(1)}) custom-call(s32[3]{0:T(128)S(1)} %copy-done.10, bf16[16,80,384]{2,1,0:T(8,128)(2,1)S(1)} %all-to-all-done.refs_1_, ...), custom_call_target="tpu_custom_call" | custom-call | flops 11000000512 | bytes 1048576 | tf_op jit(solution)/shard_map/attention_backward/pallas_call | solution.py:89
  164.6 1.7 collective-permute-start.37
  166.2 1.5 collective-permute-start.38
  167.9 8.2 %all-to-all-done.2.refs_0_ = bf16[16,64,1792]{2,1,0:T(8,128)(2,1)} async-done(((bf16[16,64,1792]{2,1,0:T(8,128)(2,1)}), bf16[16,64,1792]{2,1,0:T(8,128)(2,1)}, u32[]{:S(2)}, u32[]{:S(2)}) %all-to-all-start.2) | async-done | bytes 3670048 | tf_op jit(solution)/shard_map/all_to_all | solution.py:670
  176.1 3.3 %feed_total.1 = (f32[64,1792]{1,0:T(8,128)S(1)}, bf16[64,1792]{1,0:T(8,128)(2,1)}) custom-call(bf16[16,64,1792]{2,1,0:T(8,128)(2,1)} %all-to-all-done.2.refs_0_), custom_call_target="tpu_custom_call" | custom-call | flops 2000000000 | bytes 1048576 | tf_op jit(solution)/shard_map/feed_total/pallas_call | solution.py:89
  181.3 2.4 %attention_sums.1 = bf16[16,80,384]{2,1,0:T(8,128)(2,1)} custom-call(s32[3]{0:T(128)S(1)} %copy-done.10, bf16[2,4,128,1024]{3,2,1,0:T(8,128)(2,1)S(1)} %copy-done.31, bf16[2,4,128,256]{3,2,1,0:T(8,128)(2,1)S(1)} %copy-done.12, bf16[2,128,128]{2,1,0:T(8,128)(2,1)S(1)} %get-tuple-element.120.refs_3_, bf16[2,128,128]{2,1,0:T(8,128)(2,1)S(1)} %collective-permute-done.37.refs_4_, ...), custom_call_target="tpu_custom_call" | custom-call | flops 4000000000 | bytes 1048576 | tf_op jit(solution)/shard_map/attention_sums/pallas_call | solution.py:89
  183.7 1.5 meet.5
  185.9 6.9 %all-to-all-start.3 = ((bf16[16,80,384]{2,1,0:T(8,128)(2,1)}), bf16[16,80,384]{2,1,0:T(8,128)(2,1)S(1)}, u32[]{:S(2)}, u32[]{:S(2)}) async-start(bf16[16,80,384]{2,1,0:T(8,128)(2,1)} %attention_sums.1), calls=%async_computation.3 | async-start | bytes 1966080 | tf_op jit(solution)/shard_map/all_to_all | solution.py:670
  192.8 1.3 copy-done.24
  194.1 1.5 meet.4
  197.0 2.3 collective-permute-start.29
  201.9 1.5 collective-permute-start.33
  204.4 2.0 copy-done
  208.4 9.9 %all-to-all-start.4 = ((bf16[8,80,384]{2,1,0:T(8,128)(2,1)}), bf16[8,80,384]{2,1,0:T(8,128)(2,1)S(1)}, u32[]{:S(2)}, u32[]{:S(2)}) async-start(bf16[8,80,384]{2,1,0:T(8,128)(2,1)} %attention_total.1), calls=%async_computation.4 | async-start | bytes 983040 | tf_op jit(solution)/shard_map/all_to_all | solution.py:853
  218.3 1.4 collective-permute-start.34
  220.4 1.8 collective-permute-start.35
  223.2 2.0 feed_outputs.1
  225.4 2.0 output.1
  227.4 4.8 %collective-permute-done.34.refs_2_ = bf16[128,1024]{1,0:T(8,128)(2,1)S(1)} collective-permute-done((bf16[128,1024]{1,0:T(8,128)(2,1)S(1)}, bf16[128,1024]{1,0:T(8,128)(2,1)S(1)}, u32[]{:S(2)}, u32[]{:S(2)}) %collective-permute-start.34) | collective-permute-done | bytes 262176 | tf_op jit(solution)/shard_map/ppermute | solution.py:642
  232.1 1.7 collective-permute-done.35.refs_3_
  233.8 2.0 input_gradient.1
  (147 shorter events, 27.9 us)
Async XLA Ops:
  0.6 19.6 %collective-permute-start.2 = (bf16[128,1024]{1,0:T(8,128)(2,1)}, bf16[128,1024]{1,0:T(8,128)(2,1)S(1)}, u32[]{:S(2)}, u32[]{:S(2)}) collective-permute-start(bf16[128,1024]{1,0:T(8,128)(2,1)} %bitcast.48), channel_id=1, source_target_pairs={{0,6},{1,7},{2,4},{3,5},{4,2},{5,3},{6,0},{7,1},{8,14},{9,15},{10,... | collective-permute-start | bytes 786440 | tf_op jit(solution)/shard_map/ppermute | solution.py:642
  4.0 16.3 %collective-permute-start.1 = (bf16[128,1024]{1,0:T(8,128)(2,1)}, bf16[128,1024]{1,0:T(8,128)(2,1)S(1)}, u32[]{:S(2)}, u32[]{:S(2)}) collective-permute-start(bf16[128,1024]{1,0:T(8,128)(2,1)} %bitcast.49), channel_id=1, source_target_pairs={{0,4},{1,5},{2,6},{3,7},{4,0},{5,1},{6,2},{7,3},{8,12},{9,13},{10,... | collective-permute-start | bytes 786440 | tf_op jit(solution)/shard_map/ppermute | solution.py:642
  4.0 16.3 %collective-permute-start = (bf16[128,1024]{1,0:T(8,128)(2,1)}, bf16[128,1024]{1,0:T(8,128)(2,1)S(1)}, u32[]{:S(2)}, u32[]{:S(2)}) collective-permute-start(bf16[128,1024]{1,0:T(8,128)(2,1)} %bitcast.50), channel_id=1, source_target_pairs={{0,2},{1,3},{2,0},{3,1},{4,6},{5,7},{6,4},{7,5},{8,10},{9,11},{10,... | collective-permute-start | bytes 786440 | tf_op jit(solution)/shard_map/ppermute | solution.py:642
  9.2 11.1 %copy-start.4 = (bf16[1,128,1024]{2,1,0:T(8,128)(2,1)S(1)}, bf16[1,128,1024]{2,1,0:T(8,128)(2,1)}, u32[]{:S(2)}) copy-start(bf16[1,128,1024]{2,1,0:T(8,128)(2,1)} %param.14) | copy-start | bytes 786436
  12.2 8.2 %copy-start.3 = (bf16[1,128,1024]{2,1,0:T(8,128)(2,1)S(1)}, bf16[1,128,1024]{2,1,0:T(8,128)(2,1)}, u32[]{:S(2)}) copy-start(bf16[1,128,1024]{2,1,0:T(8,128)(2,1)} %param.15) | copy-start | bytes 786436
  12.3 22.4 %all-to-all-start = ((bf16[16,80,384]{2,1,0:T(8,128)(2,1)}), bf16[16,80,384]{2,1,0:T(8,128)(2,1)S(1)}, u32[]{:S(2)}, u32[]{:S(2)}) async-start(bf16[16,80,384]{2,1,0:T(8,128)(2,1)} %pack.1.refs_1_), calls=%async_computation | async-start | bytes 1966080 | tf_op jit(solution)/shard_map/all_to_all | solution.py:670
  20.5 17.5 %collective-permute-start.5 = (bf16[128,1024]{1,0:T(8,128)(2,1)S(1)}, bf16[128,1024]{1,0:T(8,128)(2,1)S(1)}, u32[]{:S(2)}, u32[]{:S(2)}) collective-permute-start(bf16[128,1024]{1,0:T(8,128)(2,1)S(1)} %bitcast.44), channel_id=1, source_target_pairs={{0,6},{1,7},{2,4},{3,5},{4,2},{5,3},{6,0},{7,1},{8,14},{9,15},{10,... | collective-permute-start | bytes 786440 | tf_op jit(solution)/shard_map/ppermute | solution.py:642
  23.0 14.9 %collective-permute-start.4 = (bf16[128,1024]{1,0:T(8,128)(2,1)S(1)}, bf16[128,1024]{1,0:T(8,128)(2,1)S(1)}, u32[]{:S(2)}, u32[]{:S(2)}) collective-permute-start(bf16[128,1024]{1,0:T(8,128)(2,1)S(1)} %bitcast.45), channel_id=1, source_target_pairs={{0,4},{1,5},{2,6},{3,7},{4,0},{5,1},{6,2},{7,3},{8,12},{9,13},{10,... | collective-permute-start | bytes 786440 | tf_op jit(solution)/shard_map/ppermute | solution.py:642
  23.0 16.3 %collective-permute-start.3 = (bf16[128,1024]{1,0:T(8,128)(2,1)S(1)}, bf16[128,1024]{1,0:T(8,128)(2,1)S(1)}, u32[]{:S(2)}, u32[]{:S(2)}) collective-permute-start(bf16[128,1024]{1,0:T(8,128)(2,1)S(1)} %bitcast.46), channel_id=1, source_target_pairs={{0,2},{1,3},{2,0},{3,1},{4,6},{5,7},{6,4},{7,5},{8,10},{9,11},{10,... | collective-permute-start | bytes 786440 | tf_op jit(solution)/shard_map/ppermute | solution.py:642
  24.4 29.5 %collective-permute-start.6 = (bf16[4,128,1024]{2,1,0:T(8,128)(2,1)S(1)}, bf16[4,128,1024]{2,1,0:T(8,128)(2,1)}, u32[]{:S(2)}, u32[]{:S(2)}) collective-permute-start(bf16[4,128,1024]{2,1,0:T(8,128)(2,1)S(1)} %pad_maximum_fusion.refs_2_), channel_id=1, source_target_pairs={{0,1},{1,0},{2,3},{3,2},{4,5},{5,4},{6,7},{7,6},{8,9},{9,8},{10,11... | collective-permute-start | bytes 3145736 | tf_op jit(solution)/shard_map/ppermute | solution.py:642
  35.5 10.5 %collective-permute-start.13 = (bf16[1024,128]{1,0:T(8,128)(2,1)}, bf16[1024,128]{1,0:T(8,128)(2,1)}, u32[]{:S(2)}, u32[]{:S(2)}) collective-permute-start(bf16[1024,128]{1,0:T(8,128)(2,1)} %bitcast.15), channel_id=1, source_target_pairs={{0,6},{1,7},{2,4},{3,5},{4,2},{5,3},{6,0},{7,1},{8,14},{9,15},{10,... | collective-permute-start | bytes 786440 | tf_op jit(solution)/shard_map/ppermute | solution.py:642
  37.9 8.0 %collective-permute-start.12 = (bf16[1024,128]{1,0:T(8,128)(2,1)}, bf16[1024,128]{1,0:T(8,128)(2,1)}, u32[]{:S(2)}, u32[]{:S(2)}) collective-permute-start(bf16[1024,128]{1,0:T(8,128)(2,1)} %bitcast.15), channel_id=1, source_target_pairs={{0,4},{1,5},{2,6},{3,7},{4,0},{5,1},{6,2},{7,3},{8,12},{9,13},{10,... | collective-permute-start | bytes 786440 | tf_op jit(solution)/shard_map/ppermute | solution.py:642
  38.0 10.1 %collective-permute-start.11 = (bf16[1024,128]{1,0:T(8,128)(2,1)}, bf16[1024,128]{1,0:T(8,128)(2,1)}, u32[]{:S(2)}, u32[]{:S(2)}) collective-permute-start(bf16[1024,128]{1,0:T(8,128)(2,1)} %bitcast.15), channel_id=1, source_target_pairs={{0,2},{1,3},{2,0},{3,1},{4,6},{5,7},{6,4},{7,5},{8,10},{9,11},{10,... | collective-permute-start | bytes 786440 | tf_op jit(solution)/shard_map/ppermute | solution.py:642
  41.3 12.7 %copy-start.7 = (f32[272,128]{1,0:T(8,128)S(1)}, f32[272,128]{1,0:T(8,128)}, u32[]{:S(2)}) copy-start(f32[272,128]{1,0:T(8,128)} %constant.26.clone.refs_4_.refs_6_) | copy-start | bytes 417796
  41.3 12.7 %copy-start.10 = (s32[3]{0:T(128)S(1)}, s32[3]{0:T(128)}, u32[]{:S(2)}) copy-start(s32[3]{0:T(128)} %pad_add_fusion.refs_0_) | copy-start | bytes 40
  41.3 45.3 %all-to-all-start.1 = ((bf16[16,64,1792]{2,1,0:T(8,128)(2,1)}), bf16[16,64,1792]{2,1,0:T(8,128)(2,1)}, u32[]{:S(2)}, u32[]{:S(2)}) async-start(bf16[16,64,1792]{2,1,0:T(8,128)(2,1)} %feed_pack.1.refs_2_), calls=%async_computation.1 | async-start | bytes 7340032 | tf_op jit(solution)/shard_map/all_to_all | solution.py:670
  49.4 25.2 %collective-permute-start.14 = (bf16[4,1024,128]{2,1,0:T(8,128)(2,1)S(1)}, bf16[4,1024,128]{2,1,0:T(8,128)(2,1)S(1)}, u32[]{:S(2)}, u32[]{:S(2)}) collective-permute-start(bf16[4,1024,128]{2,1,0:T(8,128)(2,1)S(1)} %pad_maximum_fusion.2.refs_5_), channel_id=1, source_target_pairs={{0,1},{1,0},{2,3},{3,2},{4,5},{5,4},{6,7},{7,6},{8,9},{9,8},{10,11... | collective-permute-start | bytes 3145736 | tf_op jit(solution)/shard_map/ppermute | solution.py:642
  65.2 10.9 %copy-start.8 = (bf16[8,128,128]{2,1,0:T(8,128)(2,1)}, bf16[8,128,128]{2,1,0:T(8,128)(2,1)S(1)}, u32[]{:S(2)}) copy-start(bf16[8,128,128]{2,1,0:T(8,128)(2,1)S(1)} %get-tuple-element.78.refs_0_.refs_1_) | copy-start | bytes 786436
  65.3 10.9 %copy-start.30 = (bf16[2,4,128,1024]{3,2,1,0:T(8,128)(2,1)}, bf16[2,4,128,1024]{3,2,1,0:T(8,128)(2,1)S(1)}, u32[]{:S(2)}) copy-start(bf16[2,4,128,1024]{3,2,1,0:T(8,128)(2,1)S(1)} %get-tuple-element.119.refs_1_) | copy-start | bytes 6291460
  65.3 9.4 %copy-start.5 = (bf16[1,128,1024]{2,1,0:T(8,128)(2,1)S(1)}, bf16[1,128,1024]{2,1,0:T(8,128)(2,1)}, u32[]{:S(2)}) copy-start(bf16[1,128,1024]{2,1,0:T(8,128)(2,1)} %param.14) | copy-start | bytes 786436
  65.3 1.4 collective-permute-start.7
  66.7 5.2 %collective-permute-start.8 = (bf16[2,128,128]{2,1,0:T(8,128)(2,1)S(1)}, bf16[2,128,128]{2,1,0:T(8,128)(2,1)S(1)}, u32[]{:S(2)}, u32[]{:S(2)}) collective-permute-start(bf16[2,128,128]{2,1,0:T(8,128)(2,1)S(1)} %get-tuple-element.80), channel_id=1, source_target_pairs={{0,2},{1,3},{2,0},{3,1},{4,6},{5,7},{6,4},{7,5},{8,10},{9,11},{10,... | collective-permute-start | bytes 196616 | tf_op jit(solution)/shard_map/ppermute | solution.py:642
  68.4 5.1 %collective-permute-start.9 = (bf16[2,128,128]{2,1,0:T(8,128)(2,1)S(1)}, bf16[2,128,128]{2,1,0:T(8,128)(2,1)S(1)}, u32[]{:S(2)}, u32[]{:S(2)}) collective-permute-start(bf16[2,128,128]{2,1,0:T(8,128)(2,1)S(1)} %get-tuple-element.81), channel_id=1, source_target_pairs={{0,4},{1,5},{2,6},{3,7},{4,0},{5,1},{6,2},{7,3},{8,12},{9,13},{10,... | collective-permute-start | bytes 196616 | tf_op jit(solution)/shard_map/ppermute | solution.py:642
  69.9 4.7 %collective-permute-start.10 = (bf16[2,128,128]{2,1,0:T(8,128)(2,1)S(1)}, bf16[2,128,128]{2,1,0:T(8,128)(2,1)S(1)}, u32[]{:S(2)}, u32[]{:S(2)}) collective-permute-start(bf16[2,128,128]{2,1,0:T(8,128)(2,1)S(1)} %get-tuple-element.82), channel_id=1, source_target_pairs={{0,6},{1,7},{2,4},{3,5},{4,2},{5,3},{6,0},{7,1},{8,14},{9,15},{10,... | collective-permute-start | bytes 196616 | tf_op jit(solution)/shard_map/ppermute | solution.py:642
  76.2 32.6 %copy-start.25 = (f32[128,1024]{1,0:T(8,128)}, f32[128,1024]{1,0:T(8,128)S(1)}, u32[]{:S(2)}) copy-start(f32[128,1024]{1,0:T(8,128)S(1)} %get-tuple-element.95.refs_4_) | copy-start | bytes 1572868
  76.2 10.5 %collective-permute-start.17 = (bf16[128,1024]{1,0:T(8,128)(2,1)S(1)}, bf16[128,1024]{1,0:T(8,128)(2,1)}, u32[]{:S(2)}, u32[]{:S(2)}) collective-permute-start(bf16[128,1024]{1,0:T(8,128)(2,1)S(1)} %get-tuple-element.86), channel_id=1, source_target_pairs={{0,6},{1,7},{2,4},{3,5},{4,2},{5,3},{6,0},{7,1},{8,14},{9,15},{10,... | collective-permute-start | bytes 786440 | tf_op jit(solution)/shard_map/ppermute | solution.py:642
  77.6 9.0 %collective-permute-start.16 = (bf16[128,1024]{1,0:T(8,128)(2,1)S(1)}, bf16[128,1024]{1,0:T(8,128)(2,1)}, u32[]{:S(2)}, u32[]{:S(2)}) collective-permute-start(bf16[128,1024]{1,0:T(8,128)(2,1)S(1)} %get-tuple-element.86), channel_id=1, source_target_pairs={{0,4},{1,5},{2,6},{3,7},{4,0},{5,1},{6,2},{7,3},{8,12},{9,13},{10,... | collective-permute-start | bytes 786440 | tf_op jit(solution)/shard_map/ppermute | solution.py:642
  77.6 12.8 %collective-permute-start.15 = (bf16[128,1024]{1,0:T(8,128)(2,1)S(1)}, bf16[128,1024]{1,0:T(8,128)(2,1)}, u32[]{:S(2)}, u32[]{:S(2)}) collective-permute-start(bf16[128,1024]{1,0:T(8,128)(2,1)S(1)} %get-tuple-element.86), channel_id=1, source_target_pairs={{0,2},{1,3},{2,0},{3,1},{4,6},{5,7},{6,4},{7,5},{8,10},{9,11},{10,... | collective-permute-start | bytes 786440 | tf_op jit(solution)/shard_map/ppermute | solution.py:642
  80.1 15.8 %collective-permute-start.19 = (bf16[4,128,1024]{2,1,0:T(8,128)(2,1)S(1)}, bf16[4,128,1024]{2,1,0:T(8,128)(2,1)}, u32[]{:S(2)}, u32[]{:S(2)}) collective-permute-start(bf16[4,128,1024]{2,1,0:T(8,128)(2,1)S(1)} %pad_maximum_fusion.1.refs_2_), channel_id=1, source_target_pairs={{0,1},{1,0},{2,3},{3,2},{4,5},{5,4},{6,7},{7,6},{8,9},{9,8},{10,11... | collective-permute-start | bytes 3145736 | tf_op jit(solution)/shard_map/ppermute | solution.py:642
  91.7 6.6 %collective-permute-start.18 = (bf16[4,128,1024]{2,1,0:T(8,128)(2,1)S(1)}, bf16[4,128,1024]{2,1,0:T(8,128)(2,1)S(1)}, u32[]{:S(2)}, u32[]{:S(2)}) collective-permute-start(bf16[4,128,1024]{2,1,0:T(8,128)(2,1)S(1)} %pad_maximum_fusion.3.refs_0_), channel_id=1, source_target_pairs={{0,1},{1,0},{2,3},{3,2},{4,5},{5,4},{6,7},{7,6},{8,9},{9,8},{10,11... | collective-permute-start | bytes 3145736 | tf_op jit(solution)/shard_map/ppermute | solution.py:642
  108.7 7.0 %copy-start.21 = (bf16[2,4,128,1792]{3,2,1,0:T(8,128)(2,1)}, bf16[2,4,128,1792]{3,2,1,0:T(8,128)(2,1)S(1)}, u32[]{:S(2)}) copy-start(bf16[2,4,128,1792]{3,2,1,0:T(8,128)(2,1)S(1)} %get-tuple-element.97.refs_4_.refs_0_) | copy-start | bytes 11010052
  108.8 2.7 %collective-permute-start.20 = (bf16[4,128,1024]{2,1,0:T(8,128)(2,1)S(1)}, bf16[4,128,1024]{2,1,0:T(8,128)(2,1)S(1)}, u32[]{:S(2)}, u32[]{:S(2)}) collective-permute-start(bf16[4,128,1024]{2,1,0:T(8,128)(2,1)S(1)} %get-tuple-element.89), channel_id=1, source_target_pairs={{0,1},{1,0},{2,3},{3,2},{4,5},{5,4},{6,7},{7,6},{8,9},{9,8},{10,11... | collective-permute-start | bytes 3145736 | tf_op jit(solution)/shard_map/ppermute | solution.py:642
  112.4 9.7 %copy-start.36 = (bf16[128,1024]{1,0:T(8,128)(2,1)}, bf16[128,1024]{1,0:T(8,128)(2,1)S(1)}, u32[]{:S(2)}) copy-start(bf16[128,1024]{1,0:T(8,128)(2,1)S(1)} %get-tuple-element.91.refs_0_) | copy-start | bytes 786436
  112.5 17.6 %collective-permute-start.21 = (bf16[128,1024]{1,0:T(8,128)(2,1)}, bf16[128,1024]{1,0:T(8,128)(2,1)S(1)}, u32[]{:S(2)}, u32[]{:S(2)}) collective-permute-start(bf16[128,1024]{1,0:T(8,128)(2,1)} %get-tuple-element.92), channel_id=1, source_target_pairs={{0,2},{1,3},{2,0},{3,1},{4,6},{5,7},{6,4},{7,5},{8,10},{9,11},{10,... | collective-permute-start | bytes 786440 | tf_op jit(solution)/shard_map/ppermute | solution.py:642
  114.5 15.6 %collective-permute-start.22 = (bf16[128,1024]{1,0:T(8,128)(2,1)}, bf16[128,1024]{1,0:T(8,128)(2,1)S(1)}, u32[]{:S(2)}, u32[]{:S(2)}) collective-permute-start(bf16[128,1024]{1,0:T(8,128)(2,1)} %get-tuple-element.93), channel_id=1, source_target_pairs={{0,4},{1,5},{2,6},{3,7},{4,0},{5,1},{6,2},{7,3},{8,12},{9,13},{10,... | collective-permute-start | bytes 786440 | tf_op jit(solution)/shard_map/ppermute | solution.py:642
  115.5 14.5 %collective-permute-start.23 = (bf16[128,1024]{1,0:T(8,128)(2,1)S(1)}, bf16[128,1024]{1,0:T(8,128)(2,1)}, u32[]{:S(2)}, u32[]{:S(2)}) collective-permute-start(bf16[128,1024]{1,0:T(8,128)(2,1)S(1)} %get-tuple-element.94), channel_id=1, source_target_pairs={{0,6},{1,7},{2,4},{3,5},{4,2},{5,3},{6,0},{7,1},{8,14},{9,15},{10,... | collective-permute-start | bytes 786440 | tf_op jit(solution)/shard_map/ppermute | solution.py:642
  124.0 6.0 %copy-start.37 = (bf16[128,1024]{1,0:T(8,128)(2,1)S(1)}, bf16[128,1024]{1,0:T(8,128)(2,1)}, u32[]{:S(2)}) copy-start(bf16[128,1024]{1,0:T(8,128)(2,1)} %copy-done.36) | copy-start | bytes 786436
  124.0 52.1 %all-to-all-start.2 = ((bf16[16,64,1792]{2,1,0:T(8,128)(2,1)}), bf16[16,64,1792]{2,1,0:T(8,128)(2,1)}, u32[]{:S(2)}, u32[]{:S(2)}) async-start(bf16[16,64,1792]{2,1,0:T(8,128)(2,1)} %bitcast.43), calls=%async_computation.2 | async-start | bytes 7340032 | tf_op jit(solution)/shard_map/all_to_all | solution.py:670
  130.1 6.1 %copy-start.22 = (bf16[2,4,128,1792]{3,2,1,0:T(8,128)(2,1)S(1)}, bf16[2,4,128,1792]{3,2,1,0:T(8,128)(2,1)}, u32[]{:S(2)}) copy-start(bf16[2,4,128,1792]{3,2,1,0:T(8,128)(2,1)} %copy-done.21) | copy-start | bytes 11010052
  132.3 8.8 %collective-permute-start.26 = (bf16[128,1024]{1,0:T(8,128)(2,1)S(1)}, bf16[128,1024]{1,0:T(8,128)(2,1)S(1)}, u32[]{:S(2)}, u32[]{:S(2)}) collective-permute-start(bf16[128,1024]{1,0:T(8,128)(2,1)S(1)} %get-tuple-element.100), channel_id=1, source_target_pairs={{0,6},{1,7},{2,4},{3,5},{4,2},{5,3},{6,0},{7,1},{8,14},{9,15},{10,... | collective-permute-start | bytes 786440 | tf_op jit(solution)/shard_map/ppermute | solution.py:642
  134.8 6.4 %collective-permute-start.25 = (bf16[128,1024]{1,0:T(8,128)(2,1)S(1)}, bf16[128,1024]{1,0:T(8,128)(2,1)S(1)}, u32[]{:S(2)}, u32[]{:S(2)}) collective-permute-start(bf16[128,1024]{1,0:T(8,128)(2,1)S(1)} %get-tuple-element.100), channel_id=1, source_target_pairs={{0,4},{1,5},{2,6},{3,7},{4,0},{5,1},{6,2},{7,3},{8,12},{9,13},{10,... | collective-permute-start | bytes 786440 | tf_op jit(solution)/shard_map/ppermute | solution.py:642
  134.8 11.7 %collective-permute-start.24 = (bf16[128,1024]{1,0:T(8,128)(2,1)S(1)}, bf16[128,1024]{1,0:T(8,128)(2,1)S(1)}, u32[]{:S(2)}, u32[]{:S(2)}) collective-permute-start(bf16[128,1024]{1,0:T(8,128)(2,1)S(1)} %get-tuple-element.100), channel_id=1, source_target_pairs={{0,2},{1,3},{2,0},{3,1},{4,6},{5,7},{6,4},{7,5},{8,10},{9,11},{10,... | collective-permute-start | bytes 786440 | tf_op jit(solution)/shard_map/ppermute | solution.py:642
  146.6 5.2 %collective-permute-start.27 = (bf16[4,128,1024]{2,1,0:T(8,128)(2,1)S(1)}, bf16[4,128,1024]{2,1,0:T(8,128)(2,1)S(1)}, u32[]{:S(2)}, u32[]{:S(2)}) collective-permute-start(bf16[4,128,1024]{2,1,0:T(8,128)(2,1)S(1)} %pad_maximum_fusion.4.refs_3_.refs_2_), channel_id=1, source_target_pairs={{0,1},{1,0},{2,3},{3,2},{4,5},{5,4},{6,7},{7,6},{8,9},{9,8},{10,11... | collective-permute-start | bytes 3145736 | tf_op jit(solution)/shard_map/ppermute | solution.py:642
  151.8 10.3 %copy-start.9 = (bf16[8,128,128]{2,1,0:T(8,128)(2,1)S(1)}, bf16[8,128,128]{2,1,0:T(8,128)(2,1)}, u32[]{:S(2)}) copy-start(bf16[8,128,128]{2,1,0:T(8,128)(2,1)} %copy-done.8) | copy-start | bytes 786436
  161.6 22.1 %collective-permute-start.32 = (bf16[4,128,1024]{2,1,0:T(8,128)(2,1)S(1)}, bf16[4,128,1024]{2,1,0:T(8,128)(2,1)}, u32[]{:S(2)}, u32[]{:S(2)}) collective-permute-start(bf16[4,128,1024]{2,1,0:T(8,128)(2,1)S(1)} %get-tuple-element.111), channel_id=1, source_target_pairs={{0,1},{1,0},{2,3},{3,2},{4,5},{5,4},{6,7},{7,6},{8,9},{9,8},{10,11... | collective-permute-start | bytes 3145736 | tf_op jit(solution)/shard_map/ppermute | solution.py:642
  163.1 1.4 collective-permute-start.36
  163.3 29.5 %collective-permute-start.28 = (bf16[4,128,1024]{2,1,0:T(8,128)(2,1)}, bf16[4,128,1024]{2,1,0:T(8,128)(2,1)}, u32[]{:S(2)}, u32[]{:S(2)}) collective-permute-start(bf16[4,128,1024]{2,1,0:T(8,128)(2,1)} %get-tuple-element.105), channel_id=1, source_target_pairs={{0,1},{1,0},{2,3},{3,2},{4,5},{5,4},{6,7},{7,6},{8,9},{9,8},{10,11... | collective-permute-start | bytes 3145736 | tf_op jit(solution)/shard_map/ppermute | solution.py:642
  164.6 15.7 %collective-permute-start.37 = (bf16[2,128,128]{2,1,0:T(8,128)(2,1)S(1)}, bf16[2,128,128]{2,1,0:T(8,128)(2,1)S(1)}, u32[]{:S(2)}, u32[]{:S(2)}) collective-permute-start(bf16[2,128,128]{2,1,0:T(8,128)(2,1)S(1)} %get-tuple-element.121), channel_id=1, source_target_pairs={{0,2},{1,3},{2,0},{3,1},{4,6},{5,7},{6,4},{7,5},{8,10},{9,11},{10,... | collective-permute-start | bytes 196616 | tf_op jit(solution)/shard_map/ppermute | solution.py:642
  166.2 14.0 %collective-permute-start.38 = (bf16[2,128,128]{2,1,0:T(8,128)(2,1)S(1)}, bf16[2,128,128]{2,1,0:T(8,128)(2,1)S(1)}, u32[]{:S(2)}, u32[]{:S(2)}) collective-permute-start(bf16[2,128,128]{2,1,0:T(8,128)(2,1)S(1)} %get-tuple-element.122), channel_id=1, source_target_pairs={{0,4},{1,5},{2,6},{3,7},{4,0},{5,1},{6,2},{7,3},{8,12},{9,13},{10,... | collective-permute-start | bytes 196616 | tf_op jit(solution)/shard_map/ppermute | solution.py:642
  167.7 12.5 %collective-permute-start.39 = (bf16[2,128,128]{2,1,0:T(8,128)(2,1)S(1)}, bf16[2,128,128]{2,1,0:T(8,128)(2,1)S(1)}, u32[]{:S(2)}, u32[]{:S(2)}) collective-permute-start(bf16[2,128,128]{2,1,0:T(8,128)(2,1)S(1)} %get-tuple-element.123), channel_id=1, source_target_pairs={{0,6},{1,7},{2,4},{3,5},{4,2},{5,3},{6,0},{7,1},{8,14},{9,15},{10,... | collective-permute-start | bytes 196616 | tf_op jit(solution)/shard_map/ppermute | solution.py:642
  185.2 7.6 %copy-start.32 = (bf16[128,1024]{1,0:T(8,128)(2,1)}, bf16[128,1024]{1,0:T(8,128)(2,1)S(1)}, u32[]{:S(2)}) copy-start(bf16[128,1024]{1,0:T(8,128)(2,1)S(1)} %get-tuple-element.112.refs_0_) | copy-start | bytes 786436
  185.9 18.5 %all-to-all-start.3 = ((bf16[16,80,384]{2,1,0:T(8,128)(2,1)}), bf16[16,80,384]{2,1,0:T(8,128)(2,1)S(1)}, u32[]{:S(2)}, u32[]{:S(2)}) async-start(bf16[16,80,384]{2,1,0:T(8,128)(2,1)} %attention_sums.1), calls=%async_computation.3 | async-start | bytes 1966080 | tf_op jit(solution)/shard_map/all_to_all | solution.py:670
  192.8 11.5 %copy-start.2 = (bf16[16,80,384]{2,1,0:T(8,128)(2,1)S(1)}, bf16[16,80,384]{2,1,0:T(8,128)(2,1)}, u32[]{:S(2)}) copy-start(bf16[16,80,384]{2,1,0:T(8,128)(2,1)} %pack.1.refs_1_) | copy-start | bytes 2949124
  197.0 22.7 %collective-permute-start.29 = (bf16[128,1024]{1,0:T(8,128)(2,1)S(1)}, bf16[128,1024]{1,0:T(8,128)(2,1)S(1)}, u32[]{:S(2)}, u32[]{:S(2)}) collective-permute-start(bf16[128,1024]{1,0:T(8,128)(2,1)S(1)} %get-tuple-element.107), channel_id=1, source_target_pairs={{0,2},{1,3},{2,0},{3,1},{4,6},{5,7},{6,4},{7,5},{8,10},{9,11},{10,... | collective-permute-start | bytes 786440 | tf_op jit(solution)/shard_map/ppermute | solution.py:642
  199.3 19.0 %collective-permute-start.40 = (bf16[64,1792]{1,0:T(8,128)(2,1)}, bf16[64,1792]{1,0:T(8,128)(2,1)}, u32[]{:S(2)}, u32[]{:S(2)}) collective-permute-start(bf16[64,1792]{1,0:T(8,128)(2,1)} %get-tuple-element.118), channel_id=1, source_target_pairs={{0,4},{1,5},{2,6},{3,7},{4,0},{5,1},{6,2},{7,3},{8,12},{9,13},{10,... | collective-permute-start | bytes 688136 | tf_op jit(solution)/shard_map/ppermute | solution.py:642
  200.1 25.2 %collective-permute-start.30 = (bf16[128,1024]{1,0:T(8,128)(2,1)S(1)}, bf16[128,1024]{1,0:T(8,128)(2,1)}, u32[]{:S(2)}, u32[]{:S(2)}) collective-permute-start(bf16[128,1024]{1,0:T(8,128)(2,1)S(1)} %get-tuple-element.108), channel_id=1, source_target_pairs={{0,4},{1,5},{2,6},{3,7},{4,0},{5,1},{6,2},{7,3},{8,12},{9,13},{10,... | collective-permute-start | bytes 786440 | tf_op jit(solution)/shard_map/ppermute | solution.py:642
  200.8 24.5 %collective-permute-start.31 = (bf16[128,1024]{1,0:T(8,128)(2,1)}, bf16[128,1024]{1,0:T(8,128)(2,1)}, u32[]{:S(2)}, u32[]{:S(2)}) collective-permute-start(bf16[128,1024]{1,0:T(8,128)(2,1)} %copy-done.14), channel_id=1, source_target_pairs={{0,6},{1,7},{2,4},{3,5},{4,2},{5,3},{6,0},{7,1},{8,14},{9,15},{10,... | collective-permute-start | bytes 786440 | tf_op jit(solution)/shard_map/ppermute | solution.py:642
  201.9 25.4 %collective-permute-start.33 = (bf16[128,1024]{1,0:T(8,128)(2,1)}, bf16[128,1024]{1,0:T(8,128)(2,1)}, u32[]{:S(2)}, u32[]{:S(2)}) collective-permute-start(bf16[128,1024]{1,0:T(8,128)(2,1)} %copy-done.13), channel_id=1, source_target_pairs={{0,2},{1,3},{2,0},{3,1},{4,6},{5,7},{6,4},{7,5},{8,10},{9,11},{10,... | collective-permute-start | bytes 786440 | tf_op jit(solution)/shard_map/ppermute | solution.py:642
  208.4 27.4 %all-to-all-start.4 = ((bf16[8,80,384]{2,1,0:T(8,128)(2,1)}), bf16[8,80,384]{2,1,0:T(8,128)(2,1)S(1)}, u32[]{:S(2)}, u32[]{:S(2)}) async-start(bf16[8,80,384]{2,1,0:T(8,128)(2,1)} %attention_total.1), calls=%async_computation.4 | async-start | bytes 983040 | tf_op jit(solution)/shard_map/all_to_all | solution.py:853
  218.3 13.8 %collective-permute-start.34 = (bf16[128,1024]{1,0:T(8,128)(2,1)S(1)}, bf16[128,1024]{1,0:T(8,128)(2,1)S(1)}, u32[]{:S(2)}, u32[]{:S(2)}) collective-permute-start(bf16[128,1024]{1,0:T(8,128)(2,1)S(1)} %get-tuple-element.114), channel_id=1, source_target_pairs={{0,4},{1,5},{2,6},{3,7},{4,0},{5,1},{6,2},{7,3},{8,12},{9,13},{10,... | collective-permute-start | bytes 786440 | tf_op jit(solution)/shard_map/ppermute | solution.py:642
  220.4 13.4 %collective-permute-start.35 = (bf16[128,1024]{1,0:T(8,128)(2,1)S(1)}, bf16[128,1024]{1,0:T(8,128)(2,1)S(1)}, u32[]{:S(2)}, u32[]{:S(2)}) collective-permute-start(bf16[128,1024]{1,0:T(8,128)(2,1)S(1)} %get-tuple-element.115), channel_id=1, source_target_pairs={{0,6},{1,7},{2,4},{3,5},{4,2},{5,3},{6,0},{7,1},{8,14},{9,15},{10,... | collective-permute-start | bytes 786440 | tf_op jit(solution)/shard_map/ppermute | solution.py:642
  225.3 8.5 %copy-start.6 = (bf16[1,128,1024]{2,1,0:T(8,128)(2,1)S(1)}, bf16[1,128,1024]{2,1,0:T(8,128)(2,1)}, u32[]{:S(2)}) copy-start(bf16[1,128,1024]{2,1,0:T(8,128)(2,1)} %param.14) | copy-start | bytes 786436
  225.3 8.5 %copy-start.29 = (f32[128,1024]{1,0:T(8,128)S(1)}, f32[128,1024]{1,0:T(8,128)}, u32[]{:S(2)}) copy-start(f32[128,1024]{1,0:T(8,128)} %copy-done.28) | copy-start | bytes 1572868
  225.4 8.4 %copy-start.33 = (bf16[128,1024]{1,0:T(8,128)(2,1)S(1)}, bf16[128,1024]{1,0:T(8,128)(2,1)}, u32[]{:S(2)}) copy-start(bf16[128,1024]{1,0:T(8,128)(2,1)} %copy-done.32) | copy-start | bytes 786436
  (23 other events, 41.3 us)

commit v3 on v2

--- a/solution.py
+++ b/solution.py
@@ -132,7 +132,7 @@
     return (partner % 2) * 4 + partner // 2
 
 
-def feed_pack_kernel(info, gate, up, down, feed_out):
+def feed_pack_kernel(info, gate, up, down, feed_out, own_out):
     context = info[2]
     low = lanes() < half_head
     late = context == 1
@@ -147,11 +147,15 @@
     made.append(tail.astype(bf16))
     made.append(jnp.where(low, rest(down), 0.0).astype(bf16))
     block = jnp.concatenate(made, axis=1)
+    own_out[...] = block
     for index in range(16):
         feed_out[index] = block
 
 
-def pack_kernel(info, small, query, key, value, out, pack_out):
+def pack_kernel(
+    info, first_gain, second_gain, query_gain, key_gain, query, key, value, out,
+    pack_out, own_out, gain_out,
+):
     shard, me = info[0], info[1]
     low = lanes() < half_head
     odd = me % 2 == 1
@@ -174,7 +178,8 @@
     row = lax.broadcasted_iota(jnp.int32, (16, piece), 0)
     lane = lanes(16)
     ours = lane // half_head == shard % 2
-    both = small[0:1, :]
+    both = jnp.concatenate([first_gain[...], second_gain[...]], axis=1).astype(f32)
+    gain_out[...] = jnp.broadcast_to(both, gain_out.shape)
     other = swapped_halves(both)
     gains = jnp.where(ours & (row == shard // 2), jnp.where(low, both, other), 0.0)
     gains = gains + jnp.where(ours & (row == 8 + shard // 2), jnp.where(low, other, both), 0.0)
@@ -182,10 +187,11 @@
     head_gains = jnp.zeros((16, piece), f32)
     for entry in range(4):
         here = spot & (lane % 4 == entry)
-        query_gain = small[1:2, entry : entry + 1]
-        key_gain = small[1:2, 4 + entry : 5 + entry]
-        head_gains = head_gains + jnp.where(here & (row == 0), query_gain, 0.0)
-        head_gains = head_gains + jnp.where(here & (row == 1), key_gain, 0.0)
+        value_query = query_gain[:, entry : entry + 1].astype(f32)
+        value_key = key_gain[:, entry : entry + 1].astype(f32)
+        head_gains = head_gains + jnp.where(here & (row == 0), value_query, 0.0)
+        head_gains = head_gains + jnp.where(here & (row == 1), value_key, 0.0)
+    own_out[...] = pack[:, : 2 * piece]
     extra = jnp.concatenate([gains, head_gains, jnp.zeros((16, piece), f32)], axis=1)
     pack = jnp.concatenate([pack, extra.astype(bf16)], axis=0)
     for index in range(16):
@@ -596,16 +602,16 @@
     weights = value[:half_head]
     tail = value[half_head : half_head + 8, :piece] + value[half_head + 8 :, :piece]
     first = jnp.sum(
-        pack[0, :half_head, : 2 * piece].astype(f32) * weights[:, : 2 * piece],
+        pack[...].astype(f32) * weights[:, : 2 * piece],
         axis=1,
         keepdims=True,
     )
     feed = jnp.sum(
-        feed_pack[0, :, : 2 * main].astype(f32) * feed_total[:, : 2 * main].astype(f32), axis=1, keepdims=True
+        feed_pack[:, : 2 * main].astype(f32) * feed_total[:, : 2 * main].astype(f32), axis=1, keepdims=True
     )
     span = slice(3 * main, 3 * main + piece)
     feed = feed + jnp.sum(
-        feed_pack[0, :, span].astype(f32) * feed_total[:, span].astype(f32), axis=1, keepdims=True
+        feed_pack[:, span].astype(f32) * feed_total[:, span].astype(f32), axis=1, keepdims=True
     )
     lane = lanes(half_head)
     spread = jnp.where(lane == 0, first, jnp.where(lane == 1, feed, 0.0))
@@ -700,27 +706,28 @@
     info = jnp.stack([shard, place, context]).astype(jnp.int32)
     token_rows = tokens.reshape(piece, width)
     seed_rows = cotangent.reshape(piece, width)
-    small = jnp.concatenate(
-        [attention_gain, feed_gain, query_gain, key_gain, jnp.zeros((120,), bf16)]
-    )
-    small = small.astype(f32).reshape(2, piece)
-    (own_pack,) = call(
+    gains = [value.reshape(1, -1) for value in (attention_gain, feed_gain, query_gain, key_gain)]
+    pack, own_pack, small = call(
         pack_kernel,
-        [shape((16, 80, 3 * piece), bf16)],
-        info, small, query_weight, key_weight, value_weight, out_weight,
+        [
+            shape((16, 80, 3 * piece), bf16),
+            shape((half_head, 2 * piece), bf16),
+            shape((8, piece), f32),
+        ],
+        info, *gains, query_weight, key_weight, value_weight, out_weight,
         micros=6,
         name="pack",
         fetch=True,
     )
-    (feed_pack,) = call(
+    feed_pack, own_feed = call(
         feed_pack_kernel,
-        [shape((16, half_head, packed), bf16)],
+        [shape((16, half_head, packed), bf16), shape((half_head, packed), bf16)],
         info, gate_weight, up_weight, down_weight.T,
         micros=12,
         name="feed_pack",
         fetch=True,
     )
-    pack = after(across(own_pack), feed_pack)
+    pack = after(across(pack), feed_pack)
     feed_full = across(after(feed_pack, pack)).reshape(width, packed)
     out_columns = pack[:, :half_head, 2 * piece :].reshape(width, piece)
     tokens_mine, tokens_other = line_gather(token_rows, own_pack)
@@ -742,7 +749,7 @@
         ],
         name="attention_forward",
     )
-    out_mine, out_other = line_gather(out_columns)
+    out_mine, out_other = line_gather(out_columns, attended_heads)
     attended = line_turn(attended_heads)
     mixed, feed_input, out_rows = call(
         branch_kernel,
@@ -771,12 +778,6 @@
         name="feed_sums",
     )
     feed_parts = across(sums.reshape(16, half_head, packed))
-    feed_total, feed_low = call(
-        feed_total_kernel,
-        [shape((half_head, packed), f32), shape((half_head, packed), bf16)],
-        feed_parts,
-        name="feed_total",
-    )
     grad_mixed, grad_branch = call(
         grad_mixed_kernel,
         [shape((piece, width), f32), shape((piece, width), bf16)],
@@ -791,14 +792,14 @@
         name="feed_out",
     )
     branch_mine, branch_other = line_gather(grad_branch, out_keep)
-    (out_sums,) = call(
+    (out_parts,) = call(
         out_sums_kernel,
         [shape(cube, bf16)],
         info, attended_heads, branch_mine, branch_other,
         micros=1,
         name="out_sums",
     )
-    out_sums = line_turn(out_sums)
+    out_sums = line_turn(out_parts)
     cube_f32 = pltpu.VMEM(cube, f32)
     mixer_keep, mixer_give, raw, gain_sums = call(
         backward_kernel,
@@ -808,8 +809,8 @@
             shape((2, 4, piece, 2 * piece), bf16),
             shape((8, piece), f32),
         ],
-        info, pack, gains, branch_mine, branch_other, out_rows, table, log_sum, kept,
-        micros=11,
+        info, pack, gains, branch_mine, branch_other, after(out_rows, out_parts), table, log_sum, kept,
+        micros=6,
         scratch=[
             pltpu.VMEM(cube, bf16), cube_f32, cube_f32, cube_f32,
             pltpu.VMEM((56, piece, piece), f32), pltpu.SemaphoreType.DMA,
@@ -819,12 +820,18 @@
     (attention_sums,) = call(
         attention_sums_kernel,
         [shape((16, 80, 3 * piece), bf16)],
-        info, after(mixer, feed_low), raw, *out_sums, gain_sums,
-        micros=4,
+        info, mixer, raw, *out_sums, gain_sums,
+        micros=2,
         name="attention_sums",
     )
     grad_mixer = line_reduce(mixer_keep, mixer_give)
-    attention_parts = across(after(attention_sums, grad_mixer[0]))
+    attention_parts = across(after(attention_sums, *grad_mixer[1:]))
+    feed_total, feed_low = call(
+        feed_total_kernel,
+        [shape((half_head, packed), f32), shape((half_head, packed), bf16)],
+        after(feed_parts, attention_sums),
+        name="feed_total",
+    )
     (input_gradient,) = call(
         input_kernel,
         [shape((piece, width), bf16)],
@@ -847,7 +854,7 @@
     (final,) = call(
         attention_total_kernel,
         [shape((8, 80, 3 * piece), bf16)],
-        attention_parts, own_pack, feed_pack, feed_total,
+        attention_parts, own_pack, own_feed, feed_total,
         name="attention_total",
     )
     final = lax.all_to_all(final, line, 0, 0, tiled=True)

time: 239 us -> 231 us (0.967)
  local copies, waits for them, and re-layouts: 19 us -> 11.8 us
  waiting for transfers between devices: 48.4 us -> 53.7 us
  starting transfers between devices: 93.4 us -> 89.6 us
    ppermute x41, waiting for transfers between devices: 31.2 us -> 41.9 us  [swap(): return lax.ppermute(value, line, [(i, i ^ bits) for i in range(8)])]
    all_to_all x4, waiting for transfers between devices: 17.2 us -> 9.41 us  [across(): return lax.all_to_all(value, 'shard', 0, 0, tiled=True)]
    unnamed x82 -> x66, local copies, waits for them, and re-layouts: 14.4 us -> 9.9 us
    ppermute x41, starting transfers between devices: 58 us -> 54.5 us  [swap(): return lax.ppermute(value, line, [(i, i ^ bits) for i in range(8)])]
    all_to_all x1, starting transfers between devices: 9.9 us -> 6.67 us  [on_device(): final = lax.all_to_all(final, line, 0, 0, tiled=True)]
    all_to_all x4, starting transfers between devices: 25.6 us -> 28.5 us  [across(): return lax.all_to_all(value, 'shard', 0, 0, tiled=True)]
    concatenate x1 -> x0, local copies, waits for them, and re-layouts: 2.76 us -> none  [on_device(): jnp.concatenate([attention_gain, feed_gain, query_gain, key_gain, jnp.zer...]
  transfers between devices with their start and end apart: 46 -> 46, of which waited for: 17 -> 17; matrix products, arithmetic and copies ran while one was open for 4% -> 2% of each run, Pallas kernels for 24% -> 24%
where the time goes in v3:
time: 231 us; the launch traced here: 230 us
  starting transfers between devices  89.6 us (39%)
  Pallas kernels  68.6 us (30%)
  waiting for transfers between devices  53.7 us (23%)
  local copies, waits for them, and re-layouts  11.8 us (5%)
  other arithmetic  4.52 us (2%)
    pallas_call x22, Pallas kernels, call(): pl.pallas_call(run, out_shape=tuple(outs), in_specs=[smem if i not in arr...  68.6 us
    ppermute x41, starting transfers between devices, swap(): return lax.ppermute(value, line, [(i, i ^ bits) for i in range(8)])  54.5 us
    ppermute x41, waiting for transfers between devices, swap(): return lax.ppermute(value, line, [(i, i ^ bits) for i in range(8)])  41.9 us
    all_to_all x4, starting transfers between devices, across(): return lax.all_to_all(value, 'shard', 0, 0, tiled=True)  28.5 us
    unnamed x66, local copies, waits for them, and re-layouts  9.9 us
    all_to_all x4, waiting for transfers between devices, across(): return lax.all_to_all(value, 'shard', 0, 0, tiled=True)  9.41 us
    all_to_all x1, starting transfers between devices, on_device(): final = lax.all_to_all(final, line, 0, 0, tiled=True)  6.67 us
  transfers between devices with their start and end apart: 46, of which 17 were waited for; matrix products, arithmetic and copies ran while one was open for 2% of the time, Pallas kernels for 24%

profile of v3, /device:TPU:1, one launch (start us, length us, event | category | flops | bytes accessed | tf_op | source)
XLA Modules:
  0.0 229.5 jit_solution(9093694240341675224)
XLA Ops:
  0.6 3.4 %collective-permute-start.2 = (bf16[128,1024]{1,0:T(8,128)(2,1)}, bf16[128,1024]{1,0:T(8,128)(2,1)S(1)}, u32[]{:S(2)}, u32[]{:S(2)}) collective-permute-start(bf16[128,1024]{1,0:T(8,128)(2,1)} %bitcast.49), channel_id=1, source_target_pairs={{0,6},{1,7},{2,4},{3,5},{4,2},{5,3},{6,0},{7,1},{8,14},{9,15},{10,... | collective-permute-start | bytes 786440 | tf_op jit(solution)/shard_map/ppermute | solution.py:648
  4.0 1.3 collective-permute-start
  5.9 3.1 %pack.1 = (bf16[16,80,384]{2,1,0:T(8,128)(2,1)}, bf16[64,256]{1,0:T(8,128)(2,1)}, f32[8,128]{1,0:T(8,128)}) custom-call(s32[3]{0:T(128)} %pad_add_fusion.refs_0_, bf16[1,64]{1,0:T(2,128)(2,1)} %bitcast.66, bf16[1,64]{1,0:T(2,128)(2,1)} %bitcast.67, bf16[1,4]{1,0:T(2,128)(2,1)} %bitcast.68, bf16[1,4]{1,0:T(2,128)(2,1)} %bitcast.69, bf16[64,1024]{1,0:T(8,128)(2,1)} %refs_5_.1, ...), custom_call_target="tpu_custom_call" | custom-call | flops 6000000000 | bytes 1048576 | tf_op jit(solution)/shard_map/pack/pallas_call | solution.py:89
  9.0 8.0 %all-to-all-start = ((bf16[16,80,384]{2,1,0:T(8,128)(2,1)}), bf16[16,80,384]{2,1,0:T(8,128)(2,1)S(1)}, u32[]{:S(2)}, u32[]{:S(2)}) async-start(bf16[16,80,384]{2,1,0:T(8,128)(2,1)} %get-tuple-element.81), calls=%async_computation | async-start | bytes 1966080 | tf_op jit(solution)/shard_map/all_to_all | solution.py:676
  17.2 2.6 %collective-permute-start.5 = (bf16[128,1024]{1,0:T(8,128)(2,1)S(1)}, bf16[128,1024]{1,0:T(8,128)(2,1)S(1)}, u32[]{:S(2)}, u32[]{:S(2)}) collective-permute-start(bf16[128,1024]{1,0:T(8,128)(2,1)S(1)} %bitcast.45), channel_id=1, source_target_pairs={{0,6},{1,7},{2,4},{3,5},{4,2},{5,3},{6,0},{7,1},{8,14},{9,15},{10,... | collective-permute-start | bytes 786440 | tf_op jit(solution)/shard_map/ppermute | solution.py:648
  19.8 1.4 collective-permute-start.3
  21.2 2.6 %collective-permute-start.6 = (bf16[4,128,1024]{2,1,0:T(8,128)(2,1)S(1)}, bf16[4,128,1024]{2,1,0:T(8,128)(2,1)}, u32[]{:S(2)}, u32[]{:S(2)}) collective-permute-start(bf16[4,128,1024]{2,1,0:T(8,128)(2,1)S(1)} %pad_maximum_fusion.refs_2_), channel_id=1, source_target_pairs={{0,1},{1,0},{2,3},{3,2},{4,5},{5,4},{6,7},{7,6},{8,9},{9,8},{10,11... | collective-permute-start | bytes 3145736 | tf_op jit(solution)/shard_map/ppermute | solution.py:648
  23.8 4.1 %feed_pack.1 = (bf16[16,64,1792]{2,1,0:T(8,128)(2,1)}, bf16[64,1792]{1,0:T(8,128)(2,1)}) custom-call(s32[3]{0:T(128)} %pad_add_fusion.refs_0_, bf16[64,1152]{1,0:T(8,128)(2,1)} %refs_1_.1, bf16[64,1152]{1,0:T(8,128)(2,1)} %refs_2_.1, bf16[64,1152]{1,0:T(8,128)(2,1)} %bitcast.65), custom_call_target="tpu_custom_call" | custom-call | flops 12000000000 | bytes 1048576 | tf_op jit(solution)/shard_map/feed_pack/pallas_call | solution.py:89
  27.9 3.2 %collective-permute-done.3 = bf16[128,1024]{1,0:T(8,128)(2,1)} collective-permute-done((bf16[128,1024]{1,0:T(8,128)(2,1)S(1)}, bf16[128,1024]{1,0:T(8,128)(2,1)}, u32[]{:S(2)}, u32[]{:S(2)}) %collective-permute-start.3) | collective-permute-done | bytes 262176 | tf_op jit(solution)/shard_map/ppermute | solution.py:648
  31.2 1.1 pad_maximum_fusion.1.refs_2_
  33.0 2.5 %collective-permute-start.13 = (bf16[1024,128]{1,0:T(8,128)(2,1)}, bf16[1024,128]{1,0:T(8,128)(2,1)}, u32[]{:S(2)}, u32[]{:S(2)}) collective-permute-start(bf16[1024,128]{1,0:T(8,128)(2,1)} %bitcast.18), channel_id=1, source_target_pairs={{0,6},{1,7},{2,4},{3,5},{4,2},{5,3},{6,0},{7,1},{8,14},{9,15},{10,... | collective-permute-start | bytes 786440 | tf_op jit(solution)/shard_map/ppermute | solution.py:648
  35.5 1.4 collective-permute-start.11
  36.9 7.3 %all-to-all-start.1 = ((bf16[16,64,1792]{2,1,0:T(8,128)(2,1)}), bf16[16,64,1792]{2,1,0:T(8,128)(2,1)}, u32[]{:S(2)}, u32[]{:S(2)}) async-start(bf16[16,64,1792]{2,1,0:T(8,128)(2,1)} %get-tuple-element.96), calls=%async_computation.1 | async-start | bytes 7340032 | tf_op jit(solution)/shard_map/all_to_all | solution.py:676
  44.2 11.3 %attention_forward.1 = (bf16[8,128,128]{2,1,0:T(8,128)(2,1)S(1)}, bf16[2,4,128,1024]{3,2,1,0:T(8,128)(2,1)S(1)}, f32[4,1,512]{2,1,0:T(1,128)S(1)}, f32[16,384]{1,0:T(8,128)S(1)}, f32[1100,128,128]{2,1,0:T(8,128)}) custom-call(s32[3]{0:T(128)S(1)} %copy-done.7, bf16[16,80,384]{2,1,0:T(8,128)(2,1)S(1)} %all-to-all-done.refs_1_, ...), custom_call_target="tpu_custom_call" | custom-call | flops 35999997952 | bytes 1048576 | tf_op jit(solution)/shard_map/attention_forward/pallas_call | solution.py:89
  55.5 1.3 copy-done.10
  56.9 1.4 pad_maximum_fusion.2.refs_5_
  58.3 4.3 %collective-permute-start.14 = (bf16[4,1024,128]{2,1,0:T(8,128)(2,1)S(1)}, bf16[4,1024,128]{2,1,0:T(8,128)(2,1)S(1)}, u32[]{:S(2)}, u32[]{:S(2)}) collective-permute-start(bf16[4,1024,128]{2,1,0:T(8,128)(2,1)S(1)} %pad_maximum_fusion.2.refs_5_), channel_id=1, source_target_pairs={{0,1},{1,0},{2,3},{3,2},{4,5},{5,4},{6,7},{7,6},{8,9},{9,8},{10,11... | collective-permute-start | bytes 3145736 | tf_op jit(solution)/shard_map/ppermute | solution.py:648
  62.7 2.4 %collective-permute-done.7.refs_1_ = bf16[4,128,128]{2,1,0:T(8,128)(2,1)S(1)} collective-permute-done((bf16[4,128,128]{2,1,0:T(8,128)(2,1)S(1)}, bf16[4,128,128]{2,1,0:T(8,128)(2,1)S(1)}, u32[]{:S(2)}, u32[]{:S(2)}) %collective-permute-start.7) | collective-permute-done | bytes 131104 | tf_op jit(solution)/shard_map/ppermute | solution.py:648
  65.1 1.4 collective-permute-start.8
  66.4 1.7 collective-permute-start.9
  68.4 1.8 collective-permute-done.8.refs_2_
  70.2 1.4 collective-permute-done.9.refs_3_
  71.5 1.4 collective-permute-done.10.refs_4_
  72.9 1.5 branch.1
  75.3 1.1 collective-permute-start.17
  76.3 2.8 %collective-permute-start.15 = (bf16[128,1024]{1,0:T(8,128)(2,1)S(1)}, bf16[128,1024]{1,0:T(8,128)(2,1)}, u32[]{:S(2)}, u32[]{:S(2)}) collective-permute-start(bf16[128,1024]{1,0:T(8,128)(2,1)S(1)} %get-tuple-element.97), channel_id=1, source_target_pairs={{0,2},{1,3},{2,0},{3,1},{4,6},{5,7},{6,4},{7,5},{8,10},{9,11},{10,... | collective-permute-start | bytes 786440 | tf_op jit(solution)/shard_map/ppermute | solution.py:648
  79.1 2.5 %collective-permute-start.19 = (bf16[4,128,1024]{2,1,0:T(8,128)(2,1)S(1)}, bf16[4,128,1024]{2,1,0:T(8,128)(2,1)}, u32[]{:S(2)}, u32[]{:S(2)}) collective-permute-start(bf16[4,128,1024]{2,1,0:T(8,128)(2,1)S(1)} %pad_maximum_fusion.1.refs_2_), channel_id=1, source_target_pairs={{0,1},{1,0},{2,3},{3,2},{4,5},{5,4},{6,7},{7,6},{8,9},{9,8},{10,11... | collective-permute-start | bytes 3145736 | tf_op jit(solution)/shard_map/ppermute | solution.py:648
  81.6 4.1 %all-to-all-done.1 = bf16[16,64,1792]{2,1,0:T(8,128)(2,1)} async-done(((bf16[16,64,1792]{2,1,0:T(8,128)(2,1)}), bf16[16,64,1792]{2,1,0:T(8,128)(2,1)}, u32[]{:S(2)}, u32[]{:S(2)}) %all-to-all-start.1) | async-done | bytes 3670048 | tf_op jit(solution)/shard_map/all_to_all | solution.py:676
  85.7 3.5 %collective-permute-done.15 = bf16[128,1024]{1,0:T(8,128)(2,1)} collective-permute-done((bf16[128,1024]{1,0:T(8,128)(2,1)S(1)}, bf16[128,1024]{1,0:T(8,128)(2,1)}, u32[]{:S(2)}, u32[]{:S(2)}) %collective-permute-start.15) | collective-permute-done | bytes 262176 | tf_op jit(solution)/shard_map/ppermute | solution.py:648
  89.2 1.2 pad_maximum_fusion.3.refs_0_
  90.4 3.5 %collective-permute-start.18 = (bf16[4,128,1024]{2,1,0:T(8,128)(2,1)S(1)}, bf16[4,128,1024]{2,1,0:T(8,128)(2,1)S(1)}, u32[]{:S(2)}, u32[]{:S(2)}) collective-permute-start(bf16[4,128,1024]{2,1,0:T(8,128)(2,1)S(1)} %pad_maximum_fusion.3.refs_0_), channel_id=1, source_target_pairs={{0,1},{1,0},{2,3},{3,2},{4,5},{5,4},{6,7},{7,6},{8,9},{9,8},{10,11... | collective-permute-start | bytes 3145736 | tf_op jit(solution)/shard_map/ppermute | solution.py:648
  93.9 2.3 collective-permute-done.18.refs_1_
  96.2 10.5 %feed_forward.1 = (bf16[2,4,128,1792]{3,2,1,0:T(8,128)(2,1)S(1)}, bf16[4,128,1024]{2,1,0:T(8,128)(2,1)S(1)}, bf16[4,128,1024]{2,1,0:T(8,128)(2,1)S(1)}) custom-call(bf16[4,128,1024]{2,1,0:T(8,128)(2,1)S(1)} %pad_maximum_fusion.3.refs_0_, bf16[4,128,1024]{2,1,0:T(8,128)(2,1)S(1)} %collective-permute-done.18.refs_1_, ...), custom_call_target="tpu_custom_call" | custom-call | flops 11000000512 | bytes 1048576 | tf_op jit(solution)/shard_map/feed_forward/pallas_call | solution.py:89
  107.1 2.3 collective-permute-done.20.refs_1_
  111.1 1.8 collective-permute-start.21
  112.9 1.3 collective-permute-start.22
  114.3 6.5 %feed_sums.1 = bf16[1024,1792]{1,0:T(8,128)(2,1)S(1)} custom-call(bf16[4,128,1024]{2,1,0:T(8,128)(2,1)S(1)} %pad_maximum_fusion.3.refs_0_, bf16[4,128,1024]{2,1,0:T(8,128)(2,1)S(1)} %collective-permute-done.18.refs_1_, bf16[4,128,1024]{2,1,0:T(8,128)(2,1)S(1)} %pad_maximum_fusion.1.refs_2_, bf16[4,128,1024]{2,1,0:T(8,128)(2,1)} %collective-permute-done.19.refs_3_, ...), custom_call_target="tpu_custom_call" | custom-call | flops 8000000000 | bytes 1048576 | tf_op jit(solution)/shard_map/feed_sums/pallas_call | solution.py:89
  120.8 1.8 copy-done
  122.6 6.6 %all-to-all-start.3 = ((bf16[16,64,1792]{2,1,0:T(8,128)(2,1)}), bf16[16,64,1792]{2,1,0:T(8,128)(2,1)}, u32[]{:S(2)}, u32[]{:S(2)}) async-start(bf16[16,64,1792]{2,1,0:T(8,128)(2,1)} %bitcast.44), calls=%async_computation.3 | async-start | bytes 7340032 | tf_op jit(solution)/shard_map/all_to_all | solution.py:676
  130.2 1.5 grad_mixed.1
  132.5 2.1 collective-permute-start.26
  134.6 1.8 collective-permute-start.24
  136.3 3.8 %feed_out.1 = (bf16[4,128,1024]{2,1,0:T(8,128)(2,1)S(1)}, bf16[4,128,1024]{2,1,0:T(8,128)(2,1)S(1)}) custom-call(bf16[2,4,128,1792]{3,2,1,0:T(8,128)(2,1)S(1)} %copy-done.13, bf16[1024,1792]{1,0:T(8,128)(2,1)} %bitcast.23.refs_4_.refs_1_), custom_call_target="tpu_custom_call" | custom-call | flops 4000000000 | bytes 1048576 | tf_op jit(solution)/shard_map/feed_out/pallas_call | solution.py:89
  140.7 5.9 %collective-permute-done.24 = bf16[128,1024]{1,0:T(8,128)(2,1)S(1)} collective-permute-done((bf16[128,1024]{1,0:T(8,128)(2,1)S(1)}, bf16[128,1024]{1,0:T(8,128)(2,1)S(1)}, u32[]{:S(2)}, u32[]{:S(2)}) %collective-permute-start.24) | collective-permute-done | bytes 262176 | tf_op jit(solution)/shard_map/ppermute | solution.py:648
  146.7 2.9 %collective-permute-start.27 = (bf16[4,128,1024]{2,1,0:T(8,128)(2,1)S(1)}, bf16[4,128,1024]{2,1,0:T(8,128)(2,1)S(1)}, u32[]{:S(2)}, u32[]{:S(2)}) collective-permute-start(bf16[4,128,1024]{2,1,0:T(8,128)(2,1)S(1)} %pad_maximum_fusion.4.refs_2_.refs_3_), channel_id=1, source_target_pairs={{0,1},{1,0},{2,3},{3,2},{4,5},{5,4},{6,7},{7,6},{8,9},{9,8},{10,11... | collective-permute-start | bytes 3145736 | tf_op jit(solution)/shard_map/ppermute | solution.py:648
  149.6 2.3 collective-permute-done.27.refs_3_.refs_4_
  152.9 9.8 %attention_backward.1 = (bf16[4,128,1024]{2,1,0:T(8,128)(2,1)S(1)}, bf16[4,128,1024]{2,1,0:T(8,128)(2,1)S(1)}, bf16[2,4,128,256]{3,2,1,0:T(8,128)(2,1)S(1)}, f32[8,128]{1,0:T(8,128)S(1)}) custom-call(s32[3]{0:T(128)S(1)} %copy-done.7, bf16[16,80,384]{2,1,0:T(8,128)(2,1)S(1)} %all-to-all-done.refs_1_, ...), custom_call_target="tpu_custom_call" | custom-call | flops 6000000000 | bytes 1048576 | tf_op jit(solution)/shard_map/attention_backward/pallas_call | solution.py:89
  163.9 2.1 collective-permute-done.36.refs_1_
  165.9 1.3 collective-permute-start.37
  167.2 1.5 collective-permute-start.38
  171.0 2.1 collective-permute-start.35
  173.7 12.1 %collective-permute-done.39.refs_6_ = bf16[2,128,128]{2,1,0:T(8,128)(2,1)S(1)} collective-permute-done((bf16[2,128,128]{2,1,0:T(8,128)(2,1)S(1)}, bf16[2,128,128]{2,1,0:T(8,128)(2,1)S(1)}, u32[]{:S(2)}, u32[]{:S(2)}) %collective-permute-start.39) | collective-permute-done | bytes 65568 | tf_op jit(solution)/shard_map/ppermute | solution.py:648
  185.8 2.4 %attention_sums.1 = bf16[16,80,384]{2,1,0:T(8,128)(2,1)} custom-call(s32[3]{0:T(128)S(1)} %copy-done.7, bf16[2,4,128,1024]{3,2,1,0:T(8,128)(2,1)S(1)} %copy-done.11, bf16[2,4,128,256]{3,2,1,0:T(8,128)(2,1)S(1)} %get-tuple-element.116.refs_2_, bf16[2,128,128]{2,1,0:T(8,128)(2,1)S(1)} %get-tuple-element.131.refs_3_, ...), custom_call_target="tpu_custom_call" | custom-call | flops 2000000000 | bytes 1048576 | tf_op jit(solution)/shard_map/attention_sums/pallas_call | solution.py:89
  188.9 6.6 %all-to-all-start.2 = ((bf16[16,80,384]{2,1,0:T(8,128)(2,1)}), bf16[16,80,384]{2,1,0:T(8,128)(2,1)S(1)}, u32[]{:S(2)}, u32[]{:S(2)}) async-start(bf16[16,80,384]{2,1,0:T(8,128)(2,1)} %attention_sums.1), calls=%async_computation.2 | async-start | bytes 1966080 | tf_op jit(solution)/shard_map/all_to_all | solution.py:676
  195.6 3.3 %feed_total.1 = (f32[64,1792]{1,0:T(8,128)S(1)}, bf16[64,1792]{1,0:T(8,128)(2,1)}) custom-call(bf16[16,64,1792]{2,1,0:T(8,128)(2,1)} %all-to-all-done.3.refs_0_), custom_call_target="tpu_custom_call" | custom-call | flops 2000000000 | bytes 1048576 | tf_op jit(solution)/shard_map/feed_total/pallas_call | solution.py:89
  198.9 1.7 meet.4
  201.3 2.8 %collective-permute-start.29 = (bf16[128,1024]{1,0:T(8,128)(2,1)S(1)}, bf16[128,1024]{1,0:T(8,128)(2,1)S(1)}, u32[]{:S(2)}, u32[]{:S(2)}) collective-permute-start(bf16[128,1024]{1,0:T(8,128)(2,1)S(1)} %get-tuple-element.119), channel_id=1, source_target_pairs={{0,2},{1,3},{2,0},{3,1},{4,6},{5,7},{6,4},{7,5},{8,10},{9,11},{10,... | collective-permute-start | bytes 786440 | tf_op jit(solution)/shard_map/ppermute | solution.py:648
  204.9 5.3 %all-to-all-done.2.refs_0_ = bf16[16,80,384]{2,1,0:T(8,128)(2,1)S(1)} async-done(((bf16[16,80,384]{2,1,0:T(8,128)(2,1)}), bf16[16,80,384]{2,1,0:T(8,128)(2,1)S(1)}, u32[]{:S(2)}, u32[]{:S(2)}) %all-to-all-start.2) | async-done | bytes 983072 | tf_op jit(solution)/shard_map/all_to_all | solution.py:676
  212.3 6.7 %all-to-all-start.4 = ((bf16[8,80,384]{2,1,0:T(8,128)(2,1)}), bf16[8,80,384]{2,1,0:T(8,128)(2,1)S(1)}, u32[]{:S(2)}, u32[]{:S(2)}) async-start(bf16[8,80,384]{2,1,0:T(8,128)(2,1)} %attention_total.1), calls=%async_computation.4 | async-start | bytes 983040 | tf_op jit(solution)/shard_map/all_to_all | solution.py:860
  219.0 1.1 copy-done.18
  220.0 2.0 feed_outputs.1
  222.1 1.0 input_gradient.1
  223.3 1.8 output.1
  225.1 2.4 %all-to-all-done.4.refs_1_ = bf16[8,80,384]{2,1,0:T(8,128)(2,1)S(1)} async-done(((bf16[8,80,384]{2,1,0:T(8,128)(2,1)}), bf16[8,80,384]{2,1,0:T(8,128)(2,1)S(1)}, u32[]{:S(2)}, u32[]{:S(2)}) %all-to-all-start.4) | async-done | bytes 491552 | tf_op jit(solution)/shard_map/all_to_all | solution.py:860
  (128 shorter events, 18.8 us)
Async XLA Ops:
  0.6 16.4 %collective-permute-start.2 = (bf16[128,1024]{1,0:T(8,128)(2,1)}, bf16[128,1024]{1,0:T(8,128)(2,1)S(1)}, u32[]{:S(2)}, u32[]{:S(2)}) collective-permute-start(bf16[128,1024]{1,0:T(8,128)(2,1)} %bitcast.49), channel_id=1, source_target_pairs={{0,6},{1,7},{2,4},{3,5},{4,2},{5,3},{6,0},{7,1},{8,14},{9,15},{10,... | collective-permute-start | bytes 786440 | tf_op jit(solution)/shard_map/ppermute | solution.py:648
  4.0 13.0 %collective-permute-start.1 = (bf16[128,1024]{1,0:T(8,128)(2,1)}, bf16[128,1024]{1,0:T(8,128)(2,1)S(1)}, u32[]{:S(2)}, u32[]{:S(2)}) collective-permute-start(bf16[128,1024]{1,0:T(8,128)(2,1)} %bitcast.50), channel_id=1, source_target_pairs={{0,4},{1,5},{2,6},{3,7},{4,0},{5,1},{6,2},{7,3},{8,12},{9,13},{10,... | collective-permute-start | bytes 786440 | tf_op jit(solution)/shard_map/ppermute | solution.py:648
  4.0 13.0 %collective-permute-start = (bf16[128,1024]{1,0:T(8,128)(2,1)}, bf16[128,1024]{1,0:T(8,128)(2,1)S(1)}, u32[]{:S(2)}, u32[]{:S(2)}) collective-permute-start(bf16[128,1024]{1,0:T(8,128)(2,1)} %bitcast.51), channel_id=1, source_target_pairs={{0,2},{1,3},{2,0},{3,1},{4,6},{5,7},{6,4},{7,5},{8,10},{9,11},{10,... | collective-permute-start | bytes 786440 | tf_op jit(solution)/shard_map/ppermute | solution.py:648
  5.9 11.2 %copy-start.2 = (bf16[1,128,1024]{2,1,0:T(8,128)(2,1)S(1)}, bf16[1,128,1024]{2,1,0:T(8,128)(2,1)}, u32[]{:S(2)}) copy-start(bf16[1,128,1024]{2,1,0:T(8,128)(2,1)} %param.14) | copy-start | bytes 786436
  9.0 8.2 %copy-start.1 = (bf16[1,128,1024]{2,1,0:T(8,128)(2,1)S(1)}, bf16[1,128,1024]{2,1,0:T(8,128)(2,1)}, u32[]{:S(2)}) copy-start(bf16[1,128,1024]{2,1,0:T(8,128)(2,1)} %param.15) | copy-start | bytes 786436
  9.0 23.2 %all-to-all-start = ((bf16[16,80,384]{2,1,0:T(8,128)(2,1)}), bf16[16,80,384]{2,1,0:T(8,128)(2,1)S(1)}, u32[]{:S(2)}, u32[]{:S(2)}) async-start(bf16[16,80,384]{2,1,0:T(8,128)(2,1)} %get-tuple-element.81), calls=%async_computation | async-start | bytes 1966080 | tf_op jit(solution)/shard_map/all_to_all | solution.py:676
  17.2 10.7 %collective-permute-start.5 = (bf16[128,1024]{1,0:T(8,128)(2,1)S(1)}, bf16[128,1024]{1,0:T(8,128)(2,1)S(1)}, u32[]{:S(2)}, u32[]{:S(2)}) collective-permute-start(bf16[128,1024]{1,0:T(8,128)(2,1)S(1)} %bitcast.45), channel_id=1, source_target_pairs={{0,6},{1,7},{2,4},{3,5},{4,2},{5,3},{6,0},{7,1},{8,14},{9,15},{10,... | collective-permute-start | bytes 786440 | tf_op jit(solution)/shard_map/ppermute | solution.py:648
  19.8 8.1 %collective-permute-start.4 = (bf16[128,1024]{1,0:T(8,128)(2,1)S(1)}, bf16[128,1024]{1,0:T(8,128)(2,1)S(1)}, u32[]{:S(2)}, u32[]{:S(2)}) collective-permute-start(bf16[128,1024]{1,0:T(8,128)(2,1)S(1)} %bitcast.46), channel_id=1, source_target_pairs={{0,4},{1,5},{2,6},{3,7},{4,0},{5,1},{6,2},{7,3},{8,12},{9,13},{10,... | collective-permute-start | bytes 786440 | tf_op jit(solution)/shard_map/ppermute | solution.py:648
  19.8 11.4 %collective-permute-start.3 = (bf16[128,1024]{1,0:T(8,128)(2,1)S(1)}, bf16[128,1024]{1,0:T(8,128)(2,1)}, u32[]{:S(2)}, u32[]{:S(2)}) collective-permute-start(bf16[128,1024]{1,0:T(8,128)(2,1)S(1)} %bitcast.47), channel_id=1, source_target_pairs={{0,2},{1,3},{2,0},{3,1},{4,6},{5,7},{6,4},{7,5},{8,10},{9,11},{10,... | collective-permute-start | bytes 786440 | tf_op jit(solution)/shard_map/ppermute | solution.py:648
  21.2 23.0 %collective-permute-start.6 = (bf16[4,128,1024]{2,1,0:T(8,128)(2,1)S(1)}, bf16[4,128,1024]{2,1,0:T(8,128)(2,1)}, u32[]{:S(2)}, u32[]{:S(2)}) collective-permute-start(bf16[4,128,1024]{2,1,0:T(8,128)(2,1)S(1)} %pad_maximum_fusion.refs_2_), channel_id=1, source_target_pairs={{0,1},{1,0},{2,3},{3,2},{4,5},{5,4},{6,7},{7,6},{8,9},{9,8},{10,11... | collective-permute-start | bytes 3145736 | tf_op jit(solution)/shard_map/ppermute | solution.py:648
  33.0 11.2 %copy-start.4 = (f32[272,128]{1,0:T(8,128)S(1)}, f32[272,128]{1,0:T(8,128)}, u32[]{:S(2)}) copy-start(f32[272,128]{1,0:T(8,128)} %constant.24.clone.refs_4_.refs_6_) | copy-start | bytes 417796
  33.0 11.2 %copy-start.7 = (s32[3]{0:T(128)S(1)}, s32[3]{0:T(128)}, u32[]{:S(2)}) copy-start(s32[3]{0:T(128)} %pad_add_fusion.refs_0_) | copy-start | bytes 40
  33.0 23.8 %collective-permute-start.13 = (bf16[1024,128]{1,0:T(8,128)(2,1)}, bf16[1024,128]{1,0:T(8,128)(2,1)}, u32[]{:S(2)}, u32[]{:S(2)}) collective-permute-start(bf16[1024,128]{1,0:T(8,128)(2,1)} %bitcast.18), channel_id=1, source_target_pairs={{0,6},{1,7},{2,4},{3,5},{4,2},{5,3},{6,0},{7,1},{8,14},{9,15},{10,... | collective-permute-start | bytes 786440 | tf_op jit(solution)/shard_map/ppermute | solution.py:648
  35.5 21.3 %collective-permute-start.12 = (bf16[1024,128]{1,0:T(8,128)(2,1)}, bf16[1024,128]{1,0:T(8,128)(2,1)}, u32[]{:S(2)}, u32[]{:S(2)}) collective-permute-start(bf16[1024,128]{1,0:T(8,128)(2,1)} %bitcast.18), channel_id=1, source_target_pairs={{0,4},{1,5},{2,6},{3,7},{4,0},{5,1},{6,2},{7,3},{8,12},{9,13},{10,... | collective-permute-start | bytes 786440 | tf_op jit(solution)/shard_map/ppermute | solution.py:648
  35.5 21.3 %collective-permute-start.11 = (bf16[1024,128]{1,0:T(8,128)(2,1)}, bf16[1024,128]{1,0:T(8,128)(2,1)}, u32[]{:S(2)}, u32[]{:S(2)}) collective-permute-start(bf16[1024,128]{1,0:T(8,128)(2,1)} %bitcast.18), channel_id=1, source_target_pairs={{0,2},{1,3},{2,0},{3,1},{4,6},{5,7},{6,4},{7,5},{8,10},{9,11},{10,... | collective-permute-start | bytes 786440 | tf_op jit(solution)/shard_map/ppermute | solution.py:648
  36.9 48.8 %all-to-all-start.1 = ((bf16[16,64,1792]{2,1,0:T(8,128)(2,1)}), bf16[16,64,1792]{2,1,0:T(8,128)(2,1)}, u32[]{:S(2)}, u32[]{:S(2)}) async-start(bf16[16,64,1792]{2,1,0:T(8,128)(2,1)} %get-tuple-element.96), calls=%async_computation.1 | async-start | bytes 7340032 | tf_op jit(solution)/shard_map/all_to_all | solution.py:676
  56.8 17.6 %copy-start.5 = (bf16[8,128,128]{2,1,0:T(8,128)(2,1)}, bf16[8,128,128]{2,1,0:T(8,128)(2,1)S(1)}, u32[]{:S(2)}) copy-start(bf16[8,128,128]{2,1,0:T(8,128)(2,1)S(1)} %get-tuple-element.88.refs_0_.refs_1_) | copy-start | bytes 786436
  56.8 16.1 %copy-start.3 = (bf16[1,128,1024]{2,1,0:T(8,128)(2,1)S(1)}, bf16[1,128,1024]{2,1,0:T(8,128)(2,1)}, u32[]{:S(2)}) copy-start(bf16[1,128,1024]{2,1,0:T(8,128)(2,1)} %param.14) | copy-start | bytes 786436
  58.3 14.6 %collective-permute-start.14 = (bf16[4,1024,128]{2,1,0:T(8,128)(2,1)S(1)}, bf16[4,1024,128]{2,1,0:T(8,128)(2,1)S(1)}, u32[]{:S(2)}, u32[]{:S(2)}) collective-permute-start(bf16[4,1024,128]{2,1,0:T(8,128)(2,1)S(1)} %pad_maximum_fusion.2.refs_5_), channel_id=1, source_target_pairs={{0,1},{1,0},{2,3},{3,2},{4,5},{5,4},{6,7},{7,6},{8,9},{9,8},{10,11... | collective-permute-start | bytes 3145736 | tf_op jit(solution)/shard_map/ppermute | solution.py:648
  62.6 2.5 %collective-permute-start.7 = (bf16[4,128,128]{2,1,0:T(8,128)(2,1)S(1)}, bf16[4,128,128]{2,1,0:T(8,128)(2,1)S(1)}, u32[]{:S(2)}, u32[]{:S(2)}) collective-permute-start(bf16[4,128,128]{2,1,0:T(8,128)(2,1)S(1)} %slice.21), channel_id=1, source_target_pairs={{0,1},{1,0},{2,3},{3,2},{4,5},{5,4},{6,7},{7,6},{8,9},{9,8},{10,11... | collective-permute-start | bytes 393224 | tf_op jit(solution)/shard_map/ppermute | solution.py:648
  65.1 5.1 %collective-permute-start.8 = (bf16[2,128,128]{2,1,0:T(8,128)(2,1)S(1)}, bf16[2,128,128]{2,1,0:T(8,128)(2,1)S(1)}, u32[]{:S(2)}, u32[]{:S(2)}) collective-permute-start(bf16[2,128,128]{2,1,0:T(8,128)(2,1)S(1)} %get-tuple-element.90), channel_id=1, source_target_pairs={{0,2},{1,3},{2,0},{3,1},{4,6},{5,7},{6,4},{7,5},{8,10},{9,11},{10,... | collective-permute-start | bytes 196616 | tf_op jit(solution)/shard_map/ppermute | solution.py:648
  66.4 5.1 %collective-permute-start.9 = (bf16[2,128,128]{2,1,0:T(8,128)(2,1)S(1)}, bf16[2,128,128]{2,1,0:T(8,128)(2,1)S(1)}, u32[]{:S(2)}, u32[]{:S(2)}) collective-permute-start(bf16[2,128,128]{2,1,0:T(8,128)(2,1)S(1)} %get-tuple-element.91), channel_id=1, source_target_pairs={{0,4},{1,5},{2,6},{3,7},{4,0},{5,1},{6,2},{7,3},{8,12},{9,13},{10,... | collective-permute-start | bytes 196616 | tf_op jit(solution)/shard_map/ppermute | solution.py:648
  68.2 4.7 %collective-permute-start.10 = (bf16[2,128,128]{2,1,0:T(8,128)(2,1)S(1)}, bf16[2,128,128]{2,1,0:T(8,128)(2,1)S(1)}, u32[]{:S(2)}, u32[]{:S(2)}) collective-permute-start(bf16[2,128,128]{2,1,0:T(8,128)(2,1)S(1)} %get-tuple-element.92), channel_id=1, source_target_pairs={{0,6},{1,7},{2,4},{3,5},{4,2},{5,3},{6,0},{7,1},{8,14},{9,15},{10,... | collective-permute-start | bytes 196616 | tf_op jit(solution)/shard_map/ppermute | solution.py:648
  75.3 10.4 %collective-permute-start.17 = (bf16[128,1024]{1,0:T(8,128)(2,1)S(1)}, bf16[128,1024]{1,0:T(8,128)(2,1)S(1)}, u32[]{:S(2)}, u32[]{:S(2)}) collective-permute-start(bf16[128,1024]{1,0:T(8,128)(2,1)S(1)} %get-tuple-element.97), channel_id=1, source_target_pairs={{0,6},{1,7},{2,4},{3,5},{4,2},{5,3},{6,0},{7,1},{8,14},{9,15},{10,... | collective-permute-start | bytes 786440 | tf_op jit(solution)/shard_map/ppermute | solution.py:648
  76.3 9.4 %collective-permute-start.16 = (bf16[128,1024]{1,0:T(8,128)(2,1)S(1)}, bf16[128,1024]{1,0:T(8,128)(2,1)}, u32[]{:S(2)}, u32[]{:S(2)}) collective-permute-start(bf16[128,1024]{1,0:T(8,128)(2,1)S(1)} %get-tuple-element.97), channel_id=1, source_target_pairs={{0,4},{1,5},{2,6},{3,7},{4,0},{5,1},{6,2},{7,3},{8,12},{9,13},{10,... | collective-permute-start | bytes 786440 | tf_op jit(solution)/shard_map/ppermute | solution.py:648
  76.3 12.9 %collective-permute-start.15 = (bf16[128,1024]{1,0:T(8,128)(2,1)S(1)}, bf16[128,1024]{1,0:T(8,128)(2,1)}, u32[]{:S(2)}, u32[]{:S(2)}) collective-permute-start(bf16[128,1024]{1,0:T(8,128)(2,1)S(1)} %get-tuple-element.97), channel_id=1, source_target_pairs={{0,2},{1,3},{2,0},{3,1},{4,6},{5,7},{6,4},{7,5},{8,10},{9,11},{10,... | collective-permute-start | bytes 786440 | tf_op jit(solution)/shard_map/ppermute | solution.py:648
  79.1 14.8 %collective-permute-start.19 = (bf16[4,128,1024]{2,1,0:T(8,128)(2,1)S(1)}, bf16[4,128,1024]{2,1,0:T(8,128)(2,1)}, u32[]{:S(2)}, u32[]{:S(2)}) collective-permute-start(bf16[4,128,1024]{2,1,0:T(8,128)(2,1)S(1)} %pad_maximum_fusion.1.refs_2_), channel_id=1, source_target_pairs={{0,1},{1,0},{2,3},{3,2},{4,5},{5,4},{6,7},{7,6},{8,9},{9,8},{10,11... | collective-permute-start | bytes 3145736 | tf_op jit(solution)/shard_map/ppermute | solution.py:648
  90.4 5.8 %collective-permute-start.18 = (bf16[4,128,1024]{2,1,0:T(8,128)(2,1)S(1)}, bf16[4,128,1024]{2,1,0:T(8,128)(2,1)S(1)}, u32[]{:S(2)}, u32[]{:S(2)}) collective-permute-start(bf16[4,128,1024]{2,1,0:T(8,128)(2,1)S(1)} %pad_maximum_fusion.3.refs_0_), channel_id=1, source_target_pairs={{0,1},{1,0},{2,3},{3,2},{4,5},{5,4},{6,7},{7,6},{8,9},{9,8},{10,11... | collective-permute-start | bytes 3145736 | tf_op jit(solution)/shard_map/ppermute | solution.py:648
  106.7 7.7 %copy-start.12 = (bf16[2,4,128,1792]{3,2,1,0:T(8,128)(2,1)}, bf16[2,4,128,1792]{3,2,1,0:T(8,128)(2,1)S(1)}, u32[]{:S(2)}) copy-start(bf16[2,4,128,1792]{3,2,1,0:T(8,128)(2,1)S(1)} %get-tuple-element.108.refs_4_.refs_0_) | copy-start | bytes 11010052
  106.7 2.7 %collective-permute-start.20 = (bf16[4,128,1024]{2,1,0:T(8,128)(2,1)S(1)}, bf16[4,128,1024]{2,1,0:T(8,128)(2,1)S(1)}, u32[]{:S(2)}, u32[]{:S(2)}) collective-permute-start(bf16[4,128,1024]{2,1,0:T(8,128)(2,1)S(1)} %get-tuple-element.100), channel_id=1, source_target_pairs={{0,1},{1,0},{2,3},{3,2},{4,5},{5,4},{6,7},{7,6},{8,9},{9,8},{10,11... | collective-permute-start | bytes 3145736 | tf_op jit(solution)/shard_map/ppermute | solution.py:648
  111.1 18.1 %collective-permute-start.21 = (bf16[128,1024]{1,0:T(8,128)(2,1)}, bf16[128,1024]{1,0:T(8,128)(2,1)S(1)}, u32[]{:S(2)}, u32[]{:S(2)}) collective-permute-start(bf16[128,1024]{1,0:T(8,128)(2,1)} %get-tuple-element.103), channel_id=1, source_target_pairs={{0,2},{1,3},{2,0},{3,1},{4,6},{5,7},{6,4},{7,5},{8,10},{9,11},{10,... | collective-permute-start | bytes 786440 | tf_op jit(solution)/shard_map/ppermute | solution.py:648
  112.9 16.3 %collective-permute-start.22 = (bf16[128,1024]{1,0:T(8,128)(2,1)}, bf16[128,1024]{1,0:T(8,128)(2,1)}, u32[]{:S(2)}, u32[]{:S(2)}) collective-permute-start(bf16[128,1024]{1,0:T(8,128)(2,1)} %get-tuple-element.104), channel_id=1, source_target_pairs={{0,4},{1,5},{2,6},{3,7},{4,0},{5,1},{6,2},{7,3},{8,12},{9,13},{10,... | collective-permute-start | bytes 786440 | tf_op jit(solution)/shard_map/ppermute | solution.py:648
  114.1 15.0 %collective-permute-start.23 = (bf16[128,1024]{1,0:T(8,128)(2,1)S(1)}, bf16[128,1024]{1,0:T(8,128)(2,1)}, u32[]{:S(2)}, u32[]{:S(2)}) collective-permute-start(bf16[128,1024]{1,0:T(8,128)(2,1)S(1)} %get-tuple-element.105), channel_id=1, source_target_pairs={{0,6},{1,7},{2,4},{3,5},{4,2},{5,3},{6,0},{7,1},{8,14},{9,15},{10,... | collective-permute-start | bytes 786440 | tf_op jit(solution)/shard_map/ppermute | solution.py:648
  122.6 6.6 %copy-start.20 = (f32[128,1024]{1,0:T(8,128)S(1)}, f32[128,1024]{1,0:T(8,128)}, u32[]{:S(2)}) copy-start(f32[128,1024]{1,0:T(8,128)} %copy-done.19) | copy-start | bytes 1572868
  122.6 66.3 %all-to-all-start.3 = ((bf16[16,64,1792]{2,1,0:T(8,128)(2,1)}), bf16[16,64,1792]{2,1,0:T(8,128)(2,1)}, u32[]{:S(2)}, u32[]{:S(2)}) async-start(bf16[16,64,1792]{2,1,0:T(8,128)(2,1)} %bitcast.44), calls=%async_computation.3 | async-start | bytes 7340032 | tf_op jit(solution)/shard_map/all_to_all | solution.py:676
  130.2 6.2 %copy-start.13 = (bf16[2,4,128,1792]{3,2,1,0:T(8,128)(2,1)S(1)}, bf16[2,4,128,1792]{3,2,1,0:T(8,128)(2,1)}, u32[]{:S(2)}) copy-start(bf16[2,4,128,1792]{3,2,1,0:T(8,128)(2,1)} %copy-done.12) | copy-start | bytes 11010052
  132.5 19.5 %copy-start.6 = (bf16[8,128,128]{2,1,0:T(8,128)(2,1)S(1)}, bf16[8,128,128]{2,1,0:T(8,128)(2,1)}, u32[]{:S(2)}) copy-start(bf16[8,128,128]{2,1,0:T(8,128)(2,1)} %copy-done.5) | copy-start | bytes 786436
  132.5 7.7 %collective-permute-start.26 = (bf16[128,1024]{1,0:T(8,128)(2,1)S(1)}, bf16[128,1024]{1,0:T(8,128)(2,1)S(1)}, u32[]{:S(2)}, u32[]{:S(2)}) collective-permute-start(bf16[128,1024]{1,0:T(8,128)(2,1)S(1)} %get-tuple-element.111), channel_id=1, source_target_pairs={{0,6},{1,7},{2,4},{3,5},{4,2},{5,3},{6,0},{7,1},{8,14},{9,15},{10,... | collective-permute-start | bytes 786440 | tf_op jit(solution)/shard_map/ppermute | solution.py:648
  134.6 6.1 %collective-permute-start.25 = (bf16[128,1024]{1,0:T(8,128)(2,1)S(1)}, bf16[128,1024]{1,0:T(8,128)(2,1)S(1)}, u32[]{:S(2)}, u32[]{:S(2)}) collective-permute-start(bf16[128,1024]{1,0:T(8,128)(2,1)S(1)} %get-tuple-element.111), channel_id=1, source_target_pairs={{0,4},{1,5},{2,6},{3,7},{4,0},{5,1},{6,2},{7,3},{8,12},{9,13},{10,... | collective-permute-start | bytes 786440 | tf_op jit(solution)/shard_map/ppermute | solution.py:648
  134.6 12.0 %collective-permute-start.24 = (bf16[128,1024]{1,0:T(8,128)(2,1)S(1)}, bf16[128,1024]{1,0:T(8,128)(2,1)S(1)}, u32[]{:S(2)}, u32[]{:S(2)}) collective-permute-start(bf16[128,1024]{1,0:T(8,128)(2,1)S(1)} %get-tuple-element.111), channel_id=1, source_target_pairs={{0,2},{1,3},{2,0},{3,1},{4,6},{5,7},{6,4},{7,5},{8,10},{9,11},{10,... | collective-permute-start | bytes 786440 | tf_op jit(solution)/shard_map/ppermute | solution.py:648
  140.2 12.8 %copy-start.14 = (bf16[4,128,1024]{2,1,0:T(8,128)(2,1)}, bf16[4,128,1024]{2,1,0:T(8,128)(2,1)S(1)}, u32[]{:S(2)}) copy-start(bf16[4,128,1024]{2,1,0:T(8,128)(2,1)S(1)} %get-tuple-element.109.refs_0_) | copy-start | bytes 3145732
  146.7 5.2 %collective-permute-start.27 = (bf16[4,128,1024]{2,1,0:T(8,128)(2,1)S(1)}, bf16[4,128,1024]{2,1,0:T(8,128)(2,1)S(1)}, u32[]{:S(2)}, u32[]{:S(2)}) collective-permute-start(bf16[4,128,1024]{2,1,0:T(8,128)(2,1)S(1)} %pad_maximum_fusion.4.refs_2_.refs_3_), channel_id=1, source_target_pairs={{0,1},{1,0},{2,3},{3,2},{4,5},{5,4},{6,7},{7,6},{8,9},{9,8},{10,11... | collective-permute-start | bytes 3145736 | tf_op jit(solution)/shard_map/ppermute | solution.py:648
  162.8 5.9 %collective-permute-start.32 = (bf16[4,128,1024]{2,1,0:T(8,128)(2,1)S(1)}, bf16[4,128,1024]{2,1,0:T(8,128)(2,1)S(1)}, u32[]{:S(2)}, u32[]{:S(2)}) collective-permute-start(bf16[4,128,1024]{2,1,0:T(8,128)(2,1)S(1)} %get-tuple-element.123), channel_id=1, source_target_pairs={{0,1},{1,0},{2,3},{3,2},{4,5},{5,4},{6,7},{7,6},{8,9},{9,8},{10,11... | collective-permute-start | bytes 3145736 | tf_op jit(solution)/shard_map/ppermute | solution.py:648
  163.3 2.6 %collective-permute-start.36 = (bf16[4,128,128]{2,1,0:T(8,128)(2,1)S(1)}, bf16[4,128,128]{2,1,0:T(8,128)(2,1)S(1)}, u32[]{:S(2)}, u32[]{:S(2)}) collective-permute-start(bf16[4,128,128]{2,1,0:T(8,128)(2,1)S(1)} %slice.28), channel_id=1, source_target_pairs={{0,1},{1,0},{2,3},{3,2},{4,5},{5,4},{6,7},{7,6},{8,9},{9,8},{10,11... | collective-permute-start | bytes 393224 | tf_op jit(solution)/shard_map/ppermute | solution.py:648
  163.5 35.4 %collective-permute-start.28 = (bf16[4,128,1024]{2,1,0:T(8,128)(2,1)S(1)}, bf16[4,128,1024]{2,1,0:T(8,128)(2,1)}, u32[]{:S(2)}, u32[]{:S(2)}) collective-permute-start(bf16[4,128,1024]{2,1,0:T(8,128)(2,1)S(1)} %get-tuple-element.117), channel_id=1, source_target_pairs={{0,1},{1,0},{2,3},{3,2},{4,5},{5,4},{6,7},{7,6},{8,9},{9,8},{10,11... | collective-permute-start | bytes 3145736 | tf_op jit(solution)/shard_map/ppermute | solution.py:648
  165.9 5.1 %collective-permute-start.37 = (bf16[2,128,128]{2,1,0:T(8,128)(2,1)S(1)}, bf16[2,128,128]{2,1,0:T(8,128)(2,1)S(1)}, u32[]{:S(2)}, u32[]{:S(2)}) collective-permute-start(bf16[2,128,128]{2,1,0:T(8,128)(2,1)S(1)} %get-tuple-element.132), channel_id=1, source_target_pairs={{0,2},{1,3},{2,0},{3,1},{4,6},{5,7},{6,4},{7,5},{8,10},{9,11},{10,... | collective-permute-start | bytes 196616 | tf_op jit(solution)/shard_map/ppermute | solution.py:648
  167.2 18.6 %copy-start.11 = (bf16[2,4,128,1024]{3,2,1,0:T(8,128)(2,1)S(1)}, bf16[2,4,128,1024]{3,2,1,0:T(8,128)(2,1)}, u32[]{:S(2)}) copy-start(bf16[2,4,128,1024]{3,2,1,0:T(8,128)(2,1)} %copy-done.10) | copy-start | bytes 6291460
  167.2 5.9 %collective-permute-start.38 = (bf16[2,128,128]{2,1,0:T(8,128)(2,1)S(1)}, bf16[2,128,128]{2,1,0:T(8,128)(2,1)S(1)}, u32[]{:S(2)}, u32[]{:S(2)}) collective-permute-start(bf16[2,128,128]{2,1,0:T(8,128)(2,1)S(1)} %get-tuple-element.133), channel_id=1, source_target_pairs={{0,4},{1,5},{2,6},{3,7},{4,0},{5,1},{6,2},{7,3},{8,12},{9,13},{10,... | collective-permute-start | bytes 196616 | tf_op jit(solution)/shard_map/ppermute | solution.py:648
  168.9 19.3 %copy-start.24 = (bf16[128,1024]{1,0:T(8,128)(2,1)}, bf16[128,1024]{1,0:T(8,128)(2,1)S(1)}, u32[]{:S(2)}) copy-start(bf16[128,1024]{1,0:T(8,128)(2,1)S(1)} %get-tuple-element.124.refs_0_) | copy-start | bytes 786436
  169.0 19.3 %collective-permute-start.33 = (bf16[128,1024]{1,0:T(8,128)(2,1)S(1)}, bf16[128,1024]{1,0:T(8,128)(2,1)S(1)}, u32[]{:S(2)}, u32[]{:S(2)}) collective-permute-start(bf16[128,1024]{1,0:T(8,128)(2,1)S(1)} %get-tuple-element.125), channel_id=1, source_target_pairs={{0,2},{1,3},{2,0},{3,1},{4,6},{5,7},{6,4},{7,5},{8,10},{9,11},{10,... | collective-permute-start | bytes 786440 | tf_op jit(solution)/shard_map/ppermute | solution.py:648
  169.7 18.5 %collective-permute-start.34 = (bf16[128,1024]{1,0:T(8,128)(2,1)S(1)}, bf16[128,1024]{1,0:T(8,128)(2,1)S(1)}, u32[]{:S(2)}, u32[]{:S(2)}) collective-permute-start(bf16[128,1024]{1,0:T(8,128)(2,1)S(1)} %get-tuple-element.126), channel_id=1, source_target_pairs={{0,4},{1,5},{2,6},{3,7},{4,0},{5,1},{6,2},{7,3},{8,12},{9,13},{10,... | collective-permute-start | bytes 786440 | tf_op jit(solution)/shard_map/ppermute | solution.py:648
  171.0 17.2 %collective-permute-start.35 = (bf16[128,1024]{1,0:T(8,128)(2,1)S(1)}, bf16[128,1024]{1,0:T(8,128)(2,1)S(1)}, u32[]{:S(2)}, u32[]{:S(2)}) collective-permute-start(bf16[128,1024]{1,0:T(8,128)(2,1)S(1)} %get-tuple-element.127), channel_id=1, source_target_pairs={{0,6},{1,7},{2,4},{3,5},{4,2},{5,3},{6,0},{7,1},{8,14},{9,15},{10,... | collective-permute-start | bytes 786440 | tf_op jit(solution)/shard_map/ppermute | solution.py:648
  173.1 12.6 %collective-permute-start.39 = (bf16[2,128,128]{2,1,0:T(8,128)(2,1)S(1)}, bf16[2,128,128]{2,1,0:T(8,128)(2,1)S(1)}, u32[]{:S(2)}, u32[]{:S(2)}) collective-permute-start(bf16[2,128,128]{2,1,0:T(8,128)(2,1)S(1)} %get-tuple-element.134), channel_id=1, source_target_pairs={{0,6},{1,7},{2,4},{3,5},{4,2},{5,3},{6,0},{7,1},{8,14},{9,15},{10,... | collective-permute-start | bytes 196616 | tf_op jit(solution)/shard_map/ppermute | solution.py:648
  188.9 21.3 %all-to-all-start.2 = ((bf16[16,80,384]{2,1,0:T(8,128)(2,1)}), bf16[16,80,384]{2,1,0:T(8,128)(2,1)S(1)}, u32[]{:S(2)}, u32[]{:S(2)}) async-start(bf16[16,80,384]{2,1,0:T(8,128)(2,1)} %attention_sums.1), calls=%async_computation.2 | async-start | bytes 1966080 | tf_op jit(solution)/shard_map/all_to_all | solution.py:676
  195.6 3.3 %copy-start.15 = (bf16[4,128,1024]{2,1,0:T(8,128)(2,1)S(1)}, bf16[4,128,1024]{2,1,0:T(8,128)(2,1)}, u32[]{:S(2)}) copy-start(bf16[4,128,1024]{2,1,0:T(8,128)(2,1)} %copy-done.14) | copy-start | bytes 3145732
  198.9 11.4 %copy-start.30 = (bf16[64,1792]{1,0:T(8,128)(2,1)S(1)}, bf16[64,1792]{1,0:T(8,128)(2,1)}, u32[]{:S(2)}) copy-start(bf16[64,1792]{1,0:T(8,128)(2,1)} %get-tuple-element.137.refs_2_) | copy-start | bytes 688132
  198.9 11.4 %copy-start.31 = (bf16[64,256]{1,0:T(8,128)(2,1)S(1)}, bf16[64,256]{1,0:T(8,128)(2,1)}, u32[]{:S(2)}) copy-start(bf16[64,256]{1,0:T(8,128)(2,1)} %get-tuple-element.84.refs_1_) | copy-start | bytes 98308
  198.9 20.1 %collective-permute-start.40 = (bf16[64,1792]{1,0:T(8,128)(2,1)}, bf16[64,1792]{1,0:T(8,128)(2,1)}, u32[]{:S(2)}, u32[]{:S(2)}) collective-permute-start(bf16[64,1792]{1,0:T(8,128)(2,1)} %get-tuple-element.145), channel_id=1, source_target_pairs={{0,4},{1,5},{2,6},{3,7},{4,0},{5,1},{6,2},{7,3},{8,12},{9,13},{10,... | collective-permute-start | bytes 688136 | tf_op jit(solution)/shard_map/ppermute | solution.py:648
  201.3 21.9 %collective-permute-start.29 = (bf16[128,1024]{1,0:T(8,128)(2,1)S(1)}, bf16[128,1024]{1,0:T(8,128)(2,1)S(1)}, u32[]{:S(2)}, u32[]{:S(2)}) collective-permute-start(bf16[128,1024]{1,0:T(8,128)(2,1)S(1)} %get-tuple-element.119), channel_id=1, source_target_pairs={{0,2},{1,3},{2,0},{3,1},{4,6},{5,7},{6,4},{7,5},{8,10},{9,11},{10,... | collective-permute-start | bytes 786440 | tf_op jit(solution)/shard_map/ppermute | solution.py:648
  204.1 19.1 %collective-permute-start.30 = (bf16[128,1024]{1,0:T(8,128)(2,1)S(1)}, bf16[128,1024]{1,0:T(8,128)(2,1)S(1)}, u32[]{:S(2)}, u32[]{:S(2)}) collective-permute-start(bf16[128,1024]{1,0:T(8,128)(2,1)S(1)} %get-tuple-element.120), channel_id=1, source_target_pairs={{0,4},{1,5},{2,6},{3,7},{4,0},{5,1},{6,2},{7,3},{8,12},{9,13},{10,... | collective-permute-start | bytes 786440 | tf_op jit(solution)/shard_map/ppermute | solution.py:648
  204.1 19.1 %collective-permute-start.31 = (bf16[128,1024]{1,0:T(8,128)(2,1)S(1)}, bf16[128,1024]{1,0:T(8,128)(2,1)}, u32[]{:S(2)}, u32[]{:S(2)}) collective-permute-start(bf16[128,1024]{1,0:T(8,128)(2,1)S(1)} %get-tuple-element.121), channel_id=1, source_target_pairs={{0,6},{1,7},{2,4},{3,5},{4,2},{5,3},{6,0},{7,1},{8,14},{9,15},{10,... | collective-permute-start | bytes 786440 | tf_op jit(solution)/shard_map/ppermute | solution.py:648
  212.3 15.1 %all-to-all-start.4 = ((bf16[8,80,384]{2,1,0:T(8,128)(2,1)}), bf16[8,80,384]{2,1,0:T(8,128)(2,1)S(1)}, u32[]{:S(2)}, u32[]{:S(2)}) async-start(bf16[8,80,384]{2,1,0:T(8,128)(2,1)} %attention_total.1), calls=%async_computation.4 | async-start | bytes 983040 | tf_op jit(solution)/shard_map/all_to_all | solution.py:860
  219.0 3.1 %copy-start.9 = (bf16[128,1024]{1,0:T(8,128)(2,1)S(1)}, bf16[128,1024]{1,0:T(8,128)(2,1)}, u32[]{:S(2)}) copy-start(bf16[128,1024]{1,0:T(8,128)(2,1)} %copy-done.8) | copy-start | bytes 786436
  223.2 4.2 %copy-start.32 = (f32[8,128]{1,0:T(8,128)S(1)}, f32[8,128]{1,0:T(8,128)}, u32[]{:S(2)}) copy-start(f32[8,128]{1,0:T(8,128)} %get-tuple-element.129.refs_0_) | copy-start | bytes 12292
  (15 other events, 17.9 us)

commit v4 on v3

--- a/solution.py
+++ b/solution.py
@@ -342,7 +342,7 @@
     return 1.0 / (1.0 + jnp.exp(-value))
 
 
-def feed_kernel(feed_mine, feed_other, seed_mine, seed_other, weight, state, keep, give):
+def feed_kernel(feed_rows, seed_rows, weight, state, result_out):
     low = lanes() < half_head
 
     def grads(gate, up, grad):
@@ -356,9 +356,10 @@
 
     starts = [0, main, 2 * main, 3 * main, 3 * main + piece, packed]
 
-    def step(chip, carry):
-        feed = jnp.concatenate([feed_mine[chip], feed_other[chip]], axis=0)
-        seed = jnp.concatenate([seed_mine[chip], seed_other[chip]], axis=0)
+    def step(index, carry):
+        blocks = pl.ds(2 * index, 2)
+        feed = feed_rows[blocks].reshape(2 * piece, width)
+        seed = seed_rows[blocks].reshape(2 * piece, width)
         first = grads(
             dot(feed, weight[:, :main]),
             dot(feed, weight[:, main : 2 * main]),
@@ -369,20 +370,20 @@
         made = [value.astype(bf16) for value in first]
         made.append(jnp.where(low, rest[0], swapped_halves(rest[1])).astype(bf16))
         made.append(jnp.where(low, rest[2], 0.0).astype(bf16))
-        for index, value in enumerate(made):
-            state[0, chip, :, starts[index] : starts[index + 1]] = value[:piece]
-            state[1, chip, :, starts[index] : starts[index + 1]] = value[piece:]
+        for number, value in enumerate(made):
+            span = slice(starts[number], starts[number + 1])
+            state[blocks, :, span] = value.reshape(2, piece, value.shape[1])
         result = dot_nt(made[0], weight[:, :main]) + dot_nt(made[1], weight[:, main : 2 * main])
         result = result + dot_nt(made[3], weight[:, 3 * main : 3 * main + piece])
-        result = result.astype(bf16)
-        keep[chip] = result[:piece]
-        give[chip] = result[piece:]
+        result_out[blocks] = result.astype(bf16).reshape(2, piece, width)
         return carry
 
-    lax.fori_loop(0, 4, step, 0)
-
-
-def feed_sums_kernel(feed_mine, feed_other, seed_mine, seed_other, state, sums):
+    lax.fori_loop(0, 2, step, 0)
+
+
+def feed_sums_kernel(
+    feed_mine, feed_other, seed_mine, seed_other, state_mine, state_other, sums
+):
     rows = 4 * piece
 
     def step(block, carry):
@@ -391,11 +392,11 @@
         def both(mine, other, low, high):
             total = dot_tn(
                 mine[:, :, columns].reshape(rows, 2 * piece),
-                state[0, :, :, low:high].reshape(rows, high - low),
+                state_mine[:, :, low:high].reshape(rows, high - low),
             )
             total = total + dot_tn(
                 other[:, :, columns].reshape(rows, 2 * piece),
-                state[1, :, :, low:high].reshape(rows, high - low),
+                state_other[:, :, low:high].reshape(rows, high - low),
             )
             sums[columns, low:high] = total.astype(bf16)
 
@@ -408,12 +409,12 @@
     lax.fori_loop(0, 4, step, 0)
 
 
-def feed_out_kernel(state, weight, keep, give):
+def feed_out_kernel(state_mine, state_other, weight, keep, give):
     rows = 4 * piece
-    for core, ref in ((1, give), (0, keep)):
-        hidden = state[core, :, :, 2 * main : 3 * main].reshape(rows, main)
+    for state, ref in ((state_other, give), (state_mine, keep)):
+        hidden = state[:, :, 2 * main : 3 * main].reshape(rows, main)
         result = dot_nt(hidden, weight[:, 2 * main : 3 * main])
-        hidden = state[core, :, :, 3 * main + piece :].reshape(rows, piece)
+        hidden = state[:, :, 3 * main + piece :].reshape(rows, piece)
         result = result + dot_nt(hidden, weight[:, 3 * main + piece :])
         ref[...] = result.astype(bf16).reshape(4, piece, width)
 
@@ -762,18 +763,22 @@
     feed_mine, feed_other = line_gather(feed_input, feed_full)
     rows = (feed_mine, feed_other, seed_mine, seed_other)
     line_shape = shape((4, piece, width), bf16)
-    state, grad_keep, grad_give = call(
+    halves = [shape((4, piece, packed), bf16), line_shape]
+    state_mine, grad_keep = call(
+        feed_kernel, halves, feed_mine, seed_mine, feed_full, micros=6, name="feed_forward"
+    )
+    state_other, grad_give = call(
         feed_kernel,
-        [shape((2, 4, piece, packed), bf16), line_shape, line_shape],
-        *rows, feed_full,
-        micros=11,
+        halves,
+        feed_other, after(seed_other, grad_keep), feed_full,
+        micros=6,
         name="feed_forward",
     )
     grad_feed = line_reduce(grad_keep, grad_give)
     (sums,) = call(
         feed_sums_kernel,
         [shape((width, packed), bf16)],
-        *rows, state,
+        *rows, state_mine, state_other,
         micros=8,
         name="feed_sums",
     )
@@ -787,7 +792,7 @@
     (out_keep, out_give) = call(
         feed_out_kernel,
         [line_shape, line_shape],
-        after(state, grad_branch), feed_full,
+        after(state_mine, grad_branch), state_other, feed_full,
         micros=4,
         name="feed_out",
     )

time: 231 us -> 232 us (level)
  Pallas kernels: 68.6 us -> 71.9 us
    pallas_call x22 -> x23, Pallas kernels: 68.6 us -> 71.9 us  [call(): pl.pallas_call(run, out_shape=tuple(outs), in_specs=[smem if i not in arr...]
    unnamed x66 -> x70, local copies, waits for them, and re-layouts: 9.9 us -> 10.5 us
  transfers between devices with their start and end apart: 46 -> 46, of which waited for: 17 -> 16; matrix products, arithmetic and copies ran while one was open for 2% -> 2% of each run, Pallas kernels for 24% -> 27%
where the time goes in v4:
time: 232 us; the launch traced here: 231 us
  starting transfers between devices  89.2 us (38%)
  Pallas kernels  71.9 us (31%)
  waiting for transfers between devices  51.5 us (22%)
  local copies, waits for them, and re-layouts  12.4 us (5%)
  other arithmetic  4.52 us (2%)
    pallas_call x23, Pallas kernels, call(): pl.pallas_call(run, out_shape=tuple(outs), in_specs=[smem if i not in arr...  71.9 us
    ppermute x41, starting transfers between devices, swap(): return lax.ppermute(value, line, [(i, i ^ bits) for i in range(8)])  54.1 us
    ppermute x41, waiting for transfers between devices, swap(): return lax.ppermute(value, line, [(i, i ^ bits) for i in range(8)])  40.1 us
    all_to_all x4, starting transfers between devices, across(): return lax.all_to_all(value, 'shard', 0, 0, tiled=True)  28.5 us
    unnamed x70, local copies, waits for them, and re-layouts  10.5 us
    all_to_all x4, waiting for transfers between devices, across(): return lax.all_to_all(value, 'shard', 0, 0, tiled=True)  8.02 us
    all_to_all x1, starting transfers between devices, on_device(): final = lax.all_to_all(final, line, 0, 0, tiled=True)  6.6 us
  transfers between devices with their start and end apart: 46, of which 16 were waited for; matrix products, arithmetic and copies ran while one was open for 2% of the time, Pallas kernels for 27%

profile of v4, /device:TPU:1, one launch (start us, length us, event | category | flops | bytes accessed | tf_op | source)
XLA Modules:
  0.0 230.8 jit_solution(17314616674936905914)
XLA Ops:
  0.6 3.4 %collective-permute-start.2 = (bf16[128,1024]{1,0:T(8,128)(2,1)}, bf16[128,1024]{1,0:T(8,128)(2,1)S(1)}, u32[]{:S(2)}, u32[]{:S(2)}) collective-permute-start(bf16[128,1024]{1,0:T(8,128)(2,1)} %bitcast.49), channel_id=1, source_target_pairs={{0,6},{1,7},{2,4},{3,5},{4,2},{5,3},{6,0},{7,1},{8,14},{9,15},{10,... | collective-permute-start | bytes 786440 | tf_op jit(solution)/shard_map/ppermute | solution.py:649
  4.0 1.3 collective-permute-start
  5.9 3.1 %pack.1 = (bf16[16,80,384]{2,1,0:T(8,128)(2,1)}, bf16[64,256]{1,0:T(8,128)(2,1)}, f32[8,128]{1,0:T(8,128)}) custom-call(s32[3]{0:T(128)} %pad_add_fusion.refs_0_, bf16[1,64]{1,0:T(2,128)(2,1)} %bitcast.66, bf16[1,64]{1,0:T(2,128)(2,1)} %bitcast.67, bf16[1,4]{1,0:T(2,128)(2,1)} %bitcast.68, bf16[1,4]{1,0:T(2,128)(2,1)} %bitcast.69, bf16[64,1024]{1,0:T(8,128)(2,1)} %refs_5_.1, ...), custom_call_target="tpu_custom_call" | custom-call | flops 6000000000 | bytes 1048576 | tf_op jit(solution)/shard_map/pack/pallas_call | solution.py:89
  9.0 8.0 %all-to-all-start = ((bf16[16,80,384]{2,1,0:T(8,128)(2,1)}), bf16[16,80,384]{2,1,0:T(8,128)(2,1)S(1)}, u32[]{:S(2)}, u32[]{:S(2)}) async-start(bf16[16,80,384]{2,1,0:T(8,128)(2,1)} %get-tuple-element.83), calls=%async_computation | async-start | bytes 1966080 | tf_op jit(solution)/shard_map/all_to_all | solution.py:677
  17.2 2.6 %collective-permute-start.5 = (bf16[128,1024]{1,0:T(8,128)(2,1)S(1)}, bf16[128,1024]{1,0:T(8,128)(2,1)S(1)}, u32[]{:S(2)}, u32[]{:S(2)}) collective-permute-start(bf16[128,1024]{1,0:T(8,128)(2,1)S(1)} %bitcast.45), channel_id=1, source_target_pairs={{0,6},{1,7},{2,4},{3,5},{4,2},{5,3},{6,0},{7,1},{8,14},{9,15},{10,... | collective-permute-start | bytes 786440 | tf_op jit(solution)/shard_map/ppermute | solution.py:649
  19.8 1.4 collective-permute-start.3
  21.2 2.6 %collective-permute-start.6 = (bf16[4,128,1024]{2,1,0:T(8,128)(2,1)S(1)}, bf16[4,128,1024]{2,1,0:T(8,128)(2,1)}, u32[]{:S(2)}, u32[]{:S(2)}) collective-permute-start(bf16[4,128,1024]{2,1,0:T(8,128)(2,1)S(1)} %pad_maximum_fusion.refs_2_), channel_id=1, source_target_pairs={{0,1},{1,0},{2,3},{3,2},{4,5},{5,4},{6,7},{7,6},{8,9},{9,8},{10,11... | collective-permute-start | bytes 3145736 | tf_op jit(solution)/shard_map/ppermute | solution.py:649
  23.8 4.1 %feed_pack.1 = (bf16[16,64,1792]{2,1,0:T(8,128)(2,1)}, bf16[64,1792]{1,0:T(8,128)(2,1)}) custom-call(s32[3]{0:T(128)} %pad_add_fusion.refs_0_, bf16[64,1152]{1,0:T(8,128)(2,1)} %refs_1_.1, bf16[64,1152]{1,0:T(8,128)(2,1)} %refs_2_.1, bf16[64,1152]{1,0:T(8,128)(2,1)} %bitcast.65), custom_call_target="tpu_custom_call" | custom-call | flops 12000000000 | bytes 1048576 | tf_op jit(solution)/shard_map/feed_pack/pallas_call | solution.py:89
  27.9 3.3 %collective-permute-done.3 = bf16[128,1024]{1,0:T(8,128)(2,1)} collective-permute-done((bf16[128,1024]{1,0:T(8,128)(2,1)S(1)}, bf16[128,1024]{1,0:T(8,128)(2,1)}, u32[]{:S(2)}, u32[]{:S(2)}) %collective-permute-start.3) | collective-permute-done | bytes 262176 | tf_op jit(solution)/shard_map/ppermute | solution.py:649
  31.1 1.1 pad_maximum_fusion.1.refs_1_.refs_2_
  33.0 2.5 %collective-permute-start.13 = (bf16[1024,128]{1,0:T(8,128)(2,1)}, bf16[1024,128]{1,0:T(8,128)(2,1)}, u32[]{:S(2)}, u32[]{:S(2)}) collective-permute-start(bf16[1024,128]{1,0:T(8,128)(2,1)} %bitcast.18), channel_id=1, source_target_pairs={{0,6},{1,7},{2,4},{3,5},{4,2},{5,3},{6,0},{7,1},{8,14},{9,15},{10,... | collective-permute-start | bytes 786440 | tf_op jit(solution)/shard_map/ppermute | solution.py:649
  35.5 1.4 collective-permute-start.11
  36.9 7.3 %all-to-all-start.1 = ((bf16[16,64,1792]{2,1,0:T(8,128)(2,1)}), bf16[16,64,1792]{2,1,0:T(8,128)(2,1)}, u32[]{:S(2)}, u32[]{:S(2)}) async-start(bf16[16,64,1792]{2,1,0:T(8,128)(2,1)} %get-tuple-element.98), calls=%async_computation.1 | async-start | bytes 7340032 | tf_op jit(solution)/shard_map/all_to_all | solution.py:677
  44.2 11.3 %attention_forward.1 = (bf16[8,128,128]{2,1,0:T(8,128)(2,1)S(1)}, bf16[2,4,128,1024]{3,2,1,0:T(8,128)(2,1)S(1)}, f32[4,1,512]{2,1,0:T(1,128)S(1)}, f32[16,384]{1,0:T(8,128)S(1)}, f32[1100,128,128]{2,1,0:T(8,128)}) custom-call(s32[3]{0:T(128)S(1)} %copy-done.7, bf16[16,80,384]{2,1,0:T(8,128)(2,1)S(1)} %all-to-all-done.refs_1_, ...), custom_call_target="tpu_custom_call" | custom-call | flops 35999997952 | bytes 1048576 | tf_op jit(solution)/shard_map/attention_forward/pallas_call | solution.py:89
  55.5 1.4 copy-done.10
  56.9 1.4 pad_maximum_fusion.2.refs_5_
  58.3 4.3 %collective-permute-start.14 = (bf16[4,1024,128]{2,1,0:T(8,128)(2,1)S(1)}, bf16[4,1024,128]{2,1,0:T(8,128)(2,1)S(1)}, u32[]{:S(2)}, u32[]{:S(2)}) collective-permute-start(bf16[4,1024,128]{2,1,0:T(8,128)(2,1)S(1)} %pad_maximum_fusion.2.refs_5_), channel_id=1, source_target_pairs={{0,1},{1,0},{2,3},{3,2},{4,5},{5,4},{6,7},{7,6},{8,9},{9,8},{10,11... | collective-permute-start | bytes 3145736 | tf_op jit(solution)/shard_map/ppermute | solution.py:649
  62.7 2.4 %collective-permute-done.7.refs_1_ = bf16[4,128,128]{2,1,0:T(8,128)(2,1)S(1)} collective-permute-done((bf16[4,128,128]{2,1,0:T(8,128)(2,1)S(1)}, bf16[4,128,128]{2,1,0:T(8,128)(2,1)S(1)}, u32[]{:S(2)}, u32[]{:S(2)}) %collective-permute-start.7) | collective-permute-done | bytes 131104 | tf_op jit(solution)/shard_map/ppermute | solution.py:649
  65.1 1.4 collective-permute-start.8
  66.5 1.7 collective-permute-start.9
  68.4 1.8 collective-permute-done.8.refs_2_
  70.2 1.4 collective-permute-done.9.refs_3_
  71.6 1.4 collective-permute-done.10.refs_4_
  72.9 1.5 branch.1
  75.3 1.1 collective-permute-start.17
  76.4 2.8 %collective-permute-start.15 = (bf16[128,1024]{1,0:T(8,128)(2,1)S(1)}, bf16[128,1024]{1,0:T(8,128)(2,1)}, u32[]{:S(2)}, u32[]{:S(2)}) collective-permute-start(bf16[128,1024]{1,0:T(8,128)(2,1)S(1)} %get-tuple-element.99), channel_id=1, source_target_pairs={{0,2},{1,3},{2,0},{3,1},{4,6},{5,7},{6,4},{7,5},{8,10},{9,11},{10,... | collective-permute-start | bytes 786440 | tf_op jit(solution)/shard_map/ppermute | solution.py:649
  79.2 2.5 %collective-permute-start.19 = (bf16[4,128,1024]{2,1,0:T(8,128)(2,1)S(1)}, bf16[4,128,1024]{2,1,0:T(8,128)(2,1)}, u32[]{:S(2)}, u32[]{:S(2)}) collective-permute-start(bf16[4,128,1024]{2,1,0:T(8,128)(2,1)S(1)} %pad_maximum_fusion.1.refs_1_.refs_2_), channel_id=1, source_target_pairs={{0,1},{1,0},{2,3},{3,2},{4,5},{5,4},{6,7},{7,6},{8,9},{9,8},{10,11... | collective-permute-start | bytes 3145736 | tf_op jit(solution)/shard_map/ppermute | solution.py:649
  81.7 4.0 %all-to-all-done.1 = bf16[16,64,1792]{2,1,0:T(8,128)(2,1)} async-done(((bf16[16,64,1792]{2,1,0:T(8,128)(2,1)}), bf16[16,64,1792]{2,1,0:T(8,128)(2,1)}, u32[]{:S(2)}, u32[]{:S(2)}) %all-to-all-start.1) | async-done | bytes 3670048 | tf_op jit(solution)/shard_map/all_to_all | solution.py:677
  85.7 3.5 %collective-permute-done.15 = bf16[128,1024]{1,0:T(8,128)(2,1)} collective-permute-done((bf16[128,1024]{1,0:T(8,128)(2,1)S(1)}, bf16[128,1024]{1,0:T(8,128)(2,1)}, u32[]{:S(2)}, u32[]{:S(2)}) %collective-permute-start.15) | collective-permute-done | bytes 262176 | tf_op jit(solution)/shard_map/ppermute | solution.py:649
  89.2 1.2 pad_maximum_fusion.3.refs_0_
  90.4 3.5 %collective-permute-start.18 = (bf16[4,128,1024]{2,1,0:T(8,128)(2,1)S(1)}, bf16[4,128,1024]{2,1,0:T(8,128)(2,1)S(1)}, u32[]{:S(2)}, u32[]{:S(2)}) collective-permute-start(bf16[4,128,1024]{2,1,0:T(8,128)(2,1)S(1)} %pad_maximum_fusion.3.refs_0_), channel_id=1, source_target_pairs={{0,1},{1,0},{2,3},{3,2},{4,5},{5,4},{6,7},{7,6},{8,9},{9,8},{10,11... | collective-permute-start | bytes 3145736 | tf_op jit(solution)/shard_map/ppermute | solution.py:649
  93.9 6.1 %feed_forward.2 = (bf16[4,128,1792]{2,1,0:T(8,128)(2,1)S(1)}, bf16[4,128,1024]{2,1,0:T(8,128)(2,1)S(1)}) custom-call(bf16[4,128,1024]{2,1,0:T(8,128)(2,1)S(1)} %pad_maximum_fusion.3.refs_0_, bf16[4,128,1024]{2,1,0:T(8,128)(2,1)S(1)} %pad_maximum_fusion.1.refs_1_.refs_2_, bf16[1024,1792]{1,0:T(8,128)(2,1)} %bitcast.23.refs_2_), custom_call_target="tpu_custom_call" | custom-call | flops 6000000000 | bytes 1048576 | tf_op jit(solution)/shard_map/feed_forward/pallas_call | solution.py:89
  100.0 7.1 %feed_forward.3 = (bf16[4,128,1792]{2,1,0:T(8,128)(2,1)S(1)}, bf16[4,128,1024]{2,1,0:T(8,128)(2,1)S(1)}) custom-call(bf16[4,128,1024]{2,1,0:T(8,128)(2,1)S(1)} %collective-permute-done.18.refs_0_.refs_1_, bf16[4,128,1024]{2,1,0:T(8,128)(2,1)} %collective-permute-done.19.refs_1_.refs_3_, bf16[1024,1792]{1,0:T(8,128)(2,1)} %bitcast.23.refs_2_), custom_call_target="tpu_custom_call" | custom-call | flops 6000000000 | bytes 1048576 | tf_op jit(solution)/shard_map/feed_forward/pallas_call | solution.py:89
  107.2 2.6 %collective-permute-done.20.refs_1_ = bf16[4,128,1024]{2,1,0:T(8,128)(2,1)S(1)} collective-permute-done((bf16[4,128,1024]{2,1,0:T(8,128)(2,1)S(1)}, bf16[4,128,1024]{2,1,0:T(8,128)(2,1)S(1)}, u32[]{:S(2)}, u32[]{:S(2)}) %collective-permute-start.20) | collective-permute-done | bytes 1048608 | tf_op jit(solution)/shard_map/ppermute | solution.py:649
  111.5 1.8 collective-permute-start.21
  113.3 1.3 collective-permute-start.22
  114.8 6.5 %feed_sums.1 = bf16[1024,1792]{1,0:T(8,128)(2,1)S(1)} custom-call(bf16[4,128,1024]{2,1,0:T(8,128)(2,1)S(1)} %pad_maximum_fusion.3.refs_0_, bf16[4,128,1024]{2,1,0:T(8,128)(2,1)S(1)} %collective-permute-done.18.refs_0_.refs_1_, bf16[4,128,1024]{2,1,0:T(8,128)(2,1)S(1)} %pad_maximum_fusion.1.refs_1_.refs_2_, ...), custom_call_target="tpu_custom_call" | custom-call | flops 8000000000 | bytes 1048576 | tf_op jit(solution)/shard_map/feed_sums/pallas_call | solution.py:89
  121.2 1.8 copy-done
  123.0 6.6 %all-to-all-start.3 = ((bf16[16,64,1792]{2,1,0:T(8,128)(2,1)}), bf16[16,64,1792]{2,1,0:T(8,128)(2,1)}, u32[]{:S(2)}, u32[]{:S(2)}) async-start(bf16[16,64,1792]{2,1,0:T(8,128)(2,1)} %bitcast.44), calls=%async_computation.3 | async-start | bytes 7340032 | tf_op jit(solution)/shard_map/all_to_all | solution.py:677
  130.6 1.5 grad_mixed.1
  132.2 2.2 collective-permute-start.26
  134.3 1.8 collective-permute-start.24
  136.1 4.0 %feed_out.1 = (bf16[4,128,1024]{2,1,0:T(8,128)(2,1)S(1)}, bf16[4,128,1024]{2,1,0:T(8,128)(2,1)}) custom-call(bf16[4,128,1792]{2,1,0:T(8,128)(2,1)S(1)} %copy-done.15, bf16[4,128,1792]{2,1,0:T(8,128)(2,1)S(1)} %copy-done.17, bf16[1024,1792]{1,0:T(8,128)(2,1)} %bitcast.23.refs_2_), custom_call_target="tpu_custom_call" | custom-call | flops 4000000000 | bytes 1048576 | tf_op jit(solution)/shard_map/feed_out/pallas_call | solution.py:89
  140.7 5.9 %collective-permute-done.24 = bf16[128,1024]{1,0:T(8,128)(2,1)S(1)} collective-permute-done((bf16[128,1024]{1,0:T(8,128)(2,1)S(1)}, bf16[128,1024]{1,0:T(8,128)(2,1)S(1)}, u32[]{:S(2)}, u32[]{:S(2)}) %collective-permute-start.24) | collective-permute-done | bytes 262176 | tf_op jit(solution)/shard_map/ppermute | solution.py:649
  146.7 2.7 %collective-permute-start.27 = (bf16[4,128,1024]{2,1,0:T(8,128)(2,1)S(1)}, bf16[4,128,1024]{2,1,0:T(8,128)(2,1)S(1)}, u32[]{:S(2)}, u32[]{:S(2)}) collective-permute-start(bf16[4,128,1024]{2,1,0:T(8,128)(2,1)S(1)} %pad_maximum_fusion.4.refs_2_.refs_3_), channel_id=1, source_target_pairs={{0,1},{1,0},{2,3},{3,2},{4,5},{5,4},{6,7},{7,6},{8,9},{9,8},{10,11... | collective-permute-start | bytes 3145736 | tf_op jit(solution)/shard_map/ppermute | solution.py:649
  149.4 2.3 collective-permute-done.27.refs_3_.refs_4_
  152.7 9.8 %attention_backward.1 = (bf16[4,128,1024]{2,1,0:T(8,128)(2,1)S(1)}, bf16[4,128,1024]{2,1,0:T(8,128)(2,1)S(1)}, bf16[2,4,128,256]{3,2,1,0:T(8,128)(2,1)S(1)}, f32[8,128]{1,0:T(8,128)S(1)}) custom-call(s32[3]{0:T(128)S(1)} %copy-done.7, bf16[16,80,384]{2,1,0:T(8,128)(2,1)S(1)} %all-to-all-done.refs_1_, ...), custom_call_target="tpu_custom_call" | custom-call | flops 6000000000 | bytes 1048576 | tf_op jit(solution)/shard_map/attention_backward/pallas_call | solution.py:89
  163.6 2.1 collective-permute-done.36.refs_1_
  165.7 1.3 collective-permute-start.37
  167.0 1.5 collective-permute-start.38
  170.8 2.1 collective-permute-start.35
  173.5 12.7 %collective-permute-done.39.refs_6_ = bf16[2,128,128]{2,1,0:T(8,128)(2,1)S(1)} collective-permute-done((bf16[2,128,128]{2,1,0:T(8,128)(2,1)S(1)}, bf16[2,128,128]{2,1,0:T(8,128)(2,1)S(1)}, u32[]{:S(2)}, u32[]{:S(2)}) %collective-permute-start.39) | collective-permute-done | bytes 65568 | tf_op jit(solution)/shard_map/ppermute | solution.py:649
  186.2 2.4 %attention_sums.1 = bf16[16,80,384]{2,1,0:T(8,128)(2,1)} custom-call(s32[3]{0:T(128)S(1)} %copy-done.7, bf16[2,4,128,1024]{3,2,1,0:T(8,128)(2,1)S(1)} %copy-done.11, bf16[2,4,128,256]{3,2,1,0:T(8,128)(2,1)S(1)} %get-tuple-element.120.refs_2_, bf16[2,128,128]{2,1,0:T(8,128)(2,1)S(1)} %get-tuple-element.135.refs_3_, ...), custom_call_target="tpu_custom_call" | custom-call | flops 2000000000 | bytes 1048576 | tf_op jit(solution)/shard_map/attention_sums/pallas_call | solution.py:89
  189.3 6.6 %all-to-all-start.2 = ((bf16[16,80,384]{2,1,0:T(8,128)(2,1)}), bf16[16,80,384]{2,1,0:T(8,128)(2,1)S(1)}, u32[]{:S(2)}, u32[]{:S(2)}) async-start(bf16[16,80,384]{2,1,0:T(8,128)(2,1)} %attention_sums.1), calls=%async_computation.2 | async-start | bytes 1966080 | tf_op jit(solution)/shard_map/all_to_all | solution.py:677
  195.9 3.3 %feed_total.1 = (f32[64,1792]{1,0:T(8,128)S(1)}, bf16[64,1792]{1,0:T(8,128)(2,1)}) custom-call(bf16[16,64,1792]{2,1,0:T(8,128)(2,1)} %all-to-all-done.3.refs_0_), custom_call_target="tpu_custom_call" | custom-call | flops 2000000000 | bytes 1048576 | tf_op jit(solution)/shard_map/feed_total/pallas_call | solution.py:89
  200.0 2.1 meet.4
  202.8 2.4 %collective-permute-start.29 = (bf16[128,1024]{1,0:T(8,128)(2,1)}, bf16[128,1024]{1,0:T(8,128)(2,1)S(1)}, u32[]{:S(2)}, u32[]{:S(2)}) collective-permute-start(bf16[128,1024]{1,0:T(8,128)(2,1)} %get-tuple-element.123), channel_id=1, source_target_pairs={{0,2},{1,3},{2,0},{3,1},{4,6},{5,7},{6,4},{7,5},{8,10},{9,11},{10,... | collective-permute-start | bytes 786440 | tf_op jit(solution)/shard_map/ppermute | solution.py:649
  205.2 1.4 collective-permute-start.31
  206.6 4.0 %all-to-all-done.2.refs_0_ = bf16[16,80,384]{2,1,0:T(8,128)(2,1)S(1)} async-done(((bf16[16,80,384]{2,1,0:T(8,128)(2,1)}), bf16[16,80,384]{2,1,0:T(8,128)(2,1)S(1)}, u32[]{:S(2)}, u32[]{:S(2)}) %all-to-all-start.2) | async-done | bytes 983072 | tf_op jit(solution)/shard_map/all_to_all | solution.py:677
  213.6 6.6 %all-to-all-start.4 = ((bf16[8,80,384]{2,1,0:T(8,128)(2,1)}), bf16[8,80,384]{2,1,0:T(8,128)(2,1)S(1)}, u32[]{:S(2)}, u32[]{:S(2)}) async-start(bf16[8,80,384]{2,1,0:T(8,128)(2,1)} %attention_total.1), calls=%async_computation.4 | async-start | bytes 983040 | tf_op jit(solution)/shard_map/all_to_all | solution.py:865
  220.3 2.0 feed_outputs.1
  222.4 1.0 input_gradient.1
  223.5 1.9 output.1
  225.4 3.3 %all-to-all-done.4.refs_1_ = bf16[8,80,384]{2,1,0:T(8,128)(2,1)S(1)} async-done(((bf16[8,80,384]{2,1,0:T(8,128)(2,1)}), bf16[8,80,384]{2,1,0:T(8,128)(2,1)S(1)}, u32[]{:S(2)}, u32[]{:S(2)}) %all-to-all-start.4) | async-done | bytes 491552 | tf_op jit(solution)/shard_map/all_to_all | solution.py:865
  (133 shorter events, 18.7 us)
Async XLA Ops:
  0.6 16.4 %collective-permute-start.2 = (bf16[128,1024]{1,0:T(8,128)(2,1)}, bf16[128,1024]{1,0:T(8,128)(2,1)S(1)}, u32[]{:S(2)}, u32[]{:S(2)}) collective-permute-start(bf16[128,1024]{1,0:T(8,128)(2,1)} %bitcast.49), channel_id=1, source_target_pairs={{0,6},{1,7},{2,4},{3,5},{4,2},{5,3},{6,0},{7,1},{8,14},{9,15},{10,... | collective-permute-start | bytes 786440 | tf_op jit(solution)/shard_map/ppermute | solution.py:649
  4.0 13.0 %collective-permute-start.1 = (bf16[128,1024]{1,0:T(8,128)(2,1)}, bf16[128,1024]{1,0:T(8,128)(2,1)S(1)}, u32[]{:S(2)}, u32[]{:S(2)}) collective-permute-start(bf16[128,1024]{1,0:T(8,128)(2,1)} %bitcast.50), channel_id=1, source_target_pairs={{0,4},{1,5},{2,6},{3,7},{4,0},{5,1},{6,2},{7,3},{8,12},{9,13},{10,... | collective-permute-start | bytes 786440 | tf_op jit(solution)/shard_map/ppermute | solution.py:649
  4.0 13.0 %collective-permute-start = (bf16[128,1024]{1,0:T(8,128)(2,1)}, bf16[128,1024]{1,0:T(8,128)(2,1)S(1)}, u32[]{:S(2)}, u32[]{:S(2)}) collective-permute-start(bf16[128,1024]{1,0:T(8,128)(2,1)} %bitcast.51), channel_id=1, source_target_pairs={{0,2},{1,3},{2,0},{3,1},{4,6},{5,7},{6,4},{7,5},{8,10},{9,11},{10,... | collective-permute-start | bytes 786440 | tf_op jit(solution)/shard_map/ppermute | solution.py:649
  5.9 11.2 %copy-start.2 = (bf16[1,128,1024]{2,1,0:T(8,128)(2,1)S(1)}, bf16[1,128,1024]{2,1,0:T(8,128)(2,1)}, u32[]{:S(2)}) copy-start(bf16[1,128,1024]{2,1,0:T(8,128)(2,1)} %param.14) | copy-start | bytes 786436
  9.0 8.2 %copy-start.1 = (bf16[1,128,1024]{2,1,0:T(8,128)(2,1)S(1)}, bf16[1,128,1024]{2,1,0:T(8,128)(2,1)}, u32[]{:S(2)}) copy-start(bf16[1,128,1024]{2,1,0:T(8,128)(2,1)} %param.15) | copy-start | bytes 786436
  9.0 23.2 %all-to-all-start = ((bf16[16,80,384]{2,1,0:T(8,128)(2,1)}), bf16[16,80,384]{2,1,0:T(8,128)(2,1)S(1)}, u32[]{:S(2)}, u32[]{:S(2)}) async-start(bf16[16,80,384]{2,1,0:T(8,128)(2,1)} %get-tuple-element.83), calls=%async_computation | async-start | bytes 1966080 | tf_op jit(solution)/shard_map/all_to_all | solution.py:677
  17.2 10.6 %collective-permute-start.5 = (bf16[128,1024]{1,0:T(8,128)(2,1)S(1)}, bf16[128,1024]{1,0:T(8,128)(2,1)S(1)}, u32[]{:S(2)}, u32[]{:S(2)}) collective-permute-start(bf16[128,1024]{1,0:T(8,128)(2,1)S(1)} %bitcast.45), channel_id=1, source_target_pairs={{0,6},{1,7},{2,4},{3,5},{4,2},{5,3},{6,0},{7,1},{8,14},{9,15},{10,... | collective-permute-start | bytes 786440 | tf_op jit(solution)/shard_map/ppermute | solution.py:649
  19.8 8.1 %collective-permute-start.4 = (bf16[128,1024]{1,0:T(8,128)(2,1)S(1)}, bf16[128,1024]{1,0:T(8,128)(2,1)S(1)}, u32[]{:S(2)}, u32[]{:S(2)}) collective-permute-start(bf16[128,1024]{1,0:T(8,128)(2,1)S(1)} %bitcast.46), channel_id=1, source_target_pairs={{0,4},{1,5},{2,6},{3,7},{4,0},{5,1},{6,2},{7,3},{8,12},{9,13},{10,... | collective-permute-start | bytes 786440 | tf_op jit(solution)/shard_map/ppermute | solution.py:649
  19.8 11.4 %collective-permute-start.3 = (bf16[128,1024]{1,0:T(8,128)(2,1)S(1)}, bf16[128,1024]{1,0:T(8,128)(2,1)}, u32[]{:S(2)}, u32[]{:S(2)}) collective-permute-start(bf16[128,1024]{1,0:T(8,128)(2,1)S(1)} %bitcast.47), channel_id=1, source_target_pairs={{0,2},{1,3},{2,0},{3,1},{4,6},{5,7},{6,4},{7,5},{8,10},{9,11},{10,... | collective-permute-start | bytes 786440 | tf_op jit(solution)/shard_map/ppermute | solution.py:649
  21.2 23.0 %collective-permute-start.6 = (bf16[4,128,1024]{2,1,0:T(8,128)(2,1)S(1)}, bf16[4,128,1024]{2,1,0:T(8,128)(2,1)}, u32[]{:S(2)}, u32[]{:S(2)}) collective-permute-start(bf16[4,128,1024]{2,1,0:T(8,128)(2,1)S(1)} %pad_maximum_fusion.refs_2_), channel_id=1, source_target_pairs={{0,1},{1,0},{2,3},{3,2},{4,5},{5,4},{6,7},{7,6},{8,9},{9,8},{10,11... | collective-permute-start | bytes 3145736 | tf_op jit(solution)/shard_map/ppermute | solution.py:649
  33.0 11.2 %copy-start.4 = (f32[272,128]{1,0:T(8,128)S(1)}, f32[272,128]{1,0:T(8,128)}, u32[]{:S(2)}) copy-start(f32[272,128]{1,0:T(8,128)} %constant.24.clone.refs_4_.refs_6_) | copy-start | bytes 417796
  33.0 11.2 %copy-start.7 = (s32[3]{0:T(128)S(1)}, s32[3]{0:T(128)}, u32[]{:S(2)}) copy-start(s32[3]{0:T(128)} %pad_add_fusion.refs_0_) | copy-start | bytes 40
  33.0 23.8 %collective-permute-start.13 = (bf16[1024,128]{1,0:T(8,128)(2,1)}, bf16[1024,128]{1,0:T(8,128)(2,1)}, u32[]{:S(2)}, u32[]{:S(2)}) collective-permute-start(bf16[1024,128]{1,0:T(8,128)(2,1)} %bitcast.18), channel_id=1, source_target_pairs={{0,6},{1,7},{2,4},{3,5},{4,2},{5,3},{6,0},{7,1},{8,14},{9,15},{10,... | collective-permute-start | bytes 786440 | tf_op jit(solution)/shard_map/ppermute | solution.py:649
  35.5 21.4 %collective-permute-start.12 = (bf16[1024,128]{1,0:T(8,128)(2,1)}, bf16[1024,128]{1,0:T(8,128)(2,1)}, u32[]{:S(2)}, u32[]{:S(2)}) collective-permute-start(bf16[1024,128]{1,0:T(8,128)(2,1)} %bitcast.18), channel_id=1, source_target_pairs={{0,4},{1,5},{2,6},{3,7},{4,0},{5,1},{6,2},{7,3},{8,12},{9,13},{10,... | collective-permute-start | bytes 786440 | tf_op jit(solution)/shard_map/ppermute | solution.py:649
  35.5 21.4 %collective-permute-start.11 = (bf16[1024,128]{1,0:T(8,128)(2,1)}, bf16[1024,128]{1,0:T(8,128)(2,1)}, u32[]{:S(2)}, u32[]{:S(2)}) collective-permute-start(bf16[1024,128]{1,0:T(8,128)(2,1)} %bitcast.18), channel_id=1, source_target_pairs={{0,2},{1,3},{2,0},{3,1},{4,6},{5,7},{6,4},{7,5},{8,10},{9,11},{10,... | collective-permute-start | bytes 786440 | tf_op jit(solution)/shard_map/ppermute | solution.py:649
  36.9 48.8 %all-to-all-start.1 = ((bf16[16,64,1792]{2,1,0:T(8,128)(2,1)}), bf16[16,64,1792]{2,1,0:T(8,128)(2,1)}, u32[]{:S(2)}, u32[]{:S(2)}) async-start(bf16[16,64,1792]{2,1,0:T(8,128)(2,1)} %get-tuple-element.98), calls=%async_computation.1 | async-start | bytes 7340032 | tf_op jit(solution)/shard_map/all_to_all | solution.py:677
  56.9 17.6 %copy-start.5 = (bf16[8,128,128]{2,1,0:T(8,128)(2,1)}, bf16[8,128,128]{2,1,0:T(8,128)(2,1)S(1)}, u32[]{:S(2)}) copy-start(bf16[8,128,128]{2,1,0:T(8,128)(2,1)S(1)} %get-tuple-element.90.refs_0_.refs_1_) | copy-start | bytes 786436
  56.9 16.1 %copy-start.3 = (bf16[1,128,1024]{2,1,0:T(8,128)(2,1)S(1)}, bf16[1,128,1024]{2,1,0:T(8,128)(2,1)}, u32[]{:S(2)}) copy-start(bf16[1,128,1024]{2,1,0:T(8,128)(2,1)} %param.14) | copy-start | bytes 786436
  58.3 14.6 %collective-permute-start.14 = (bf16[4,1024,128]{2,1,0:T(8,128)(2,1)S(1)}, bf16[4,1024,128]{2,1,0:T(8,128)(2,1)S(1)}, u32[]{:S(2)}, u32[]{:S(2)}) collective-permute-start(bf16[4,1024,128]{2,1,0:T(8,128)(2,1)S(1)} %pad_maximum_fusion.2.refs_5_), channel_id=1, source_target_pairs={{0,1},{1,0},{2,3},{3,2},{4,5},{5,4},{6,7},{7,6},{8,9},{9,8},{10,11... | collective-permute-start | bytes 3145736 | tf_op jit(solution)/shard_map/ppermute | solution.py:649
  62.6 2.5 %collective-permute-start.7 = (bf16[4,128,128]{2,1,0:T(8,128)(2,1)S(1)}, bf16[4,128,128]{2,1,0:T(8,128)(2,1)S(1)}, u32[]{:S(2)}, u32[]{:S(2)}) collective-permute-start(bf16[4,128,128]{2,1,0:T(8,128)(2,1)S(1)} %slice.21), channel_id=1, source_target_pairs={{0,1},{1,0},{2,3},{3,2},{4,5},{5,4},{6,7},{7,6},{8,9},{9,8},{10,11... | collective-permute-start | bytes 393224 | tf_op jit(solution)/shard_map/ppermute | solution.py:649
  65.1 5.1 %collective-permute-start.8 = (bf16[2,128,128]{2,1,0:T(8,128)(2,1)S(1)}, bf16[2,128,128]{2,1,0:T(8,128)(2,1)S(1)}, u32[]{:S(2)}, u32[]{:S(2)}) collective-permute-start(bf16[2,128,128]{2,1,0:T(8,128)(2,1)S(1)} %get-tuple-element.92), channel_id=1, source_target_pairs={{0,2},{1,3},{2,0},{3,1},{4,6},{5,7},{6,4},{7,5},{8,10},{9,11},{10,... | collective-permute-start | bytes 196616 | tf_op jit(solution)/shard_map/ppermute | solution.py:649
  66.5 5.1 %collective-permute-start.9 = (bf16[2,128,128]{2,1,0:T(8,128)(2,1)S(1)}, bf16[2,128,128]{2,1,0:T(8,128)(2,1)S(1)}, u32[]{:S(2)}, u32[]{:S(2)}) collective-permute-start(bf16[2,128,128]{2,1,0:T(8,128)(2,1)S(1)} %get-tuple-element.93), channel_id=1, source_target_pairs={{0,4},{1,5},{2,6},{3,7},{4,0},{5,1},{6,2},{7,3},{8,12},{9,13},{10,... | collective-permute-start | bytes 196616 | tf_op jit(solution)/shard_map/ppermute | solution.py:649
  68.2 4.7 %collective-permute-start.10 = (bf16[2,128,128]{2,1,0:T(8,128)(2,1)S(1)}, bf16[2,128,128]{2,1,0:T(8,128)(2,1)S(1)}, u32[]{:S(2)}, u32[]{:S(2)}) collective-permute-start(bf16[2,128,128]{2,1,0:T(8,128)(2,1)S(1)} %get-tuple-element.94), channel_id=1, source_target_pairs={{0,6},{1,7},{2,4},{3,5},{4,2},{5,3},{6,0},{7,1},{8,14},{9,15},{10,... | collective-permute-start | bytes 196616 | tf_op jit(solution)/shard_map/ppermute | solution.py:649
  75.3 10.4 %collective-permute-start.17 = (bf16[128,1024]{1,0:T(8,128)(2,1)S(1)}, bf16[128,1024]{1,0:T(8,128)(2,1)S(1)}, u32[]{:S(2)}, u32[]{:S(2)}) collective-permute-start(bf16[128,1024]{1,0:T(8,128)(2,1)S(1)} %get-tuple-element.99), channel_id=1, source_target_pairs={{0,6},{1,7},{2,4},{3,5},{4,2},{5,3},{6,0},{7,1},{8,14},{9,15},{10,... | collective-permute-start | bytes 786440 | tf_op jit(solution)/shard_map/ppermute | solution.py:649
  76.4 9.3 %collective-permute-start.16 = (bf16[128,1024]{1,0:T(8,128)(2,1)S(1)}, bf16[128,1024]{1,0:T(8,128)(2,1)}, u32[]{:S(2)}, u32[]{:S(2)}) collective-permute-start(bf16[128,1024]{1,0:T(8,128)(2,1)S(1)} %get-tuple-element.99), channel_id=1, source_target_pairs={{0,4},{1,5},{2,6},{3,7},{4,0},{5,1},{6,2},{7,3},{8,12},{9,13},{10,... | collective-permute-start | bytes 786440 | tf_op jit(solution)/shard_map/ppermute | solution.py:649
  76.4 12.9 %collective-permute-start.15 = (bf16[128,1024]{1,0:T(8,128)(2,1)S(1)}, bf16[128,1024]{1,0:T(8,128)(2,1)}, u32[]{:S(2)}, u32[]{:S(2)}) collective-permute-start(bf16[128,1024]{1,0:T(8,128)(2,1)S(1)} %get-tuple-element.99), channel_id=1, source_target_pairs={{0,2},{1,3},{2,0},{3,1},{4,6},{5,7},{6,4},{7,5},{8,10},{9,11},{10,... | collective-permute-start | bytes 786440 | tf_op jit(solution)/shard_map/ppermute | solution.py:649
  79.2 20.9 %collective-permute-start.19 = (bf16[4,128,1024]{2,1,0:T(8,128)(2,1)S(1)}, bf16[4,128,1024]{2,1,0:T(8,128)(2,1)}, u32[]{:S(2)}, u32[]{:S(2)}) collective-permute-start(bf16[4,128,1024]{2,1,0:T(8,128)(2,1)S(1)} %pad_maximum_fusion.1.refs_1_.refs_2_), channel_id=1, source_target_pairs={{0,1},{1,0},{2,3},{3,2},{4,5},{5,4},{6,7},{7,6},{8,9},{9,8},{10,11... | collective-permute-start | bytes 3145736 | tf_op jit(solution)/shard_map/ppermute | solution.py:649
  90.4 9.6 %collective-permute-start.18 = (bf16[4,128,1024]{2,1,0:T(8,128)(2,1)S(1)}, bf16[4,128,1024]{2,1,0:T(8,128)(2,1)S(1)}, u32[]{:S(2)}, u32[]{:S(2)}) collective-permute-start(bf16[4,128,1024]{2,1,0:T(8,128)(2,1)S(1)} %pad_maximum_fusion.3.refs_0_), channel_id=1, source_target_pairs={{0,1},{1,0},{2,3},{3,2},{4,5},{5,4},{6,7},{7,6},{8,9},{9,8},{10,11... | collective-permute-start | bytes 3145736 | tf_op jit(solution)/shard_map/ppermute | solution.py:649
  100.0 14.8 %copy-start.14 = (bf16[4,128,1792]{2,1,0:T(8,128)(2,1)}, bf16[4,128,1792]{2,1,0:T(8,128)(2,1)S(1)}, u32[]{:S(2)}) copy-start(bf16[4,128,1792]{2,1,0:T(8,128)(2,1)S(1)} %get-tuple-element.112.refs_4_.refs_0_) | copy-start | bytes 5505028
  107.1 7.7 %copy-start.16 = (bf16[4,128,1792]{2,1,0:T(8,128)(2,1)}, bf16[4,128,1792]{2,1,0:T(8,128)(2,1)S(1)}, u32[]{:S(2)}) copy-start(bf16[4,128,1792]{2,1,0:T(8,128)(2,1)S(1)} %get-tuple-element.105.refs_5_.refs_1_) | copy-start | bytes 5505028
  107.1 2.7 %collective-permute-start.20 = (bf16[4,128,1024]{2,1,0:T(8,128)(2,1)S(1)}, bf16[4,128,1024]{2,1,0:T(8,128)(2,1)S(1)}, u32[]{:S(2)}, u32[]{:S(2)}) collective-permute-start(bf16[4,128,1024]{2,1,0:T(8,128)(2,1)S(1)} %get-tuple-element.103), channel_id=1, source_target_pairs={{0,1},{1,0},{2,3},{3,2},{4,5},{5,4},{6,7},{7,6},{8,9},{9,8},{10,11... | collective-permute-start | bytes 3145736 | tf_op jit(solution)/shard_map/ppermute | solution.py:649
  111.5 18.1 %collective-permute-start.21 = (bf16[128,1024]{1,0:T(8,128)(2,1)}, bf16[128,1024]{1,0:T(8,128)(2,1)S(1)}, u32[]{:S(2)}, u32[]{:S(2)}) collective-permute-start(bf16[128,1024]{1,0:T(8,128)(2,1)} %get-tuple-element.107), channel_id=1, source_target_pairs={{0,2},{1,3},{2,0},{3,1},{4,6},{5,7},{6,4},{7,5},{8,10},{9,11},{10,... | collective-permute-start | bytes 786440 | tf_op jit(solution)/shard_map/ppermute | solution.py:649
  113.3 16.3 %collective-permute-start.22 = (bf16[128,1024]{1,0:T(8,128)(2,1)}, bf16[128,1024]{1,0:T(8,128)(2,1)}, u32[]{:S(2)}, u32[]{:S(2)}) collective-permute-start(bf16[128,1024]{1,0:T(8,128)(2,1)} %get-tuple-element.108), channel_id=1, source_target_pairs={{0,4},{1,5},{2,6},{3,7},{4,0},{5,1},{6,2},{7,3},{8,12},{9,13},{10,... | collective-permute-start | bytes 786440 | tf_op jit(solution)/shard_map/ppermute | solution.py:649
  114.6 15.1 %collective-permute-start.23 = (bf16[128,1024]{1,0:T(8,128)(2,1)S(1)}, bf16[128,1024]{1,0:T(8,128)(2,1)}, u32[]{:S(2)}, u32[]{:S(2)}) collective-permute-start(bf16[128,1024]{1,0:T(8,128)(2,1)S(1)} %get-tuple-element.109), channel_id=1, source_target_pairs={{0,6},{1,7},{2,4},{3,5},{4,2},{5,3},{6,0},{7,1},{8,14},{9,15},{10,... | collective-permute-start | bytes 786440 | tf_op jit(solution)/shard_map/ppermute | solution.py:649
  123.0 6.6 %copy-start.22 = (f32[128,1024]{1,0:T(8,128)S(1)}, f32[128,1024]{1,0:T(8,128)}, u32[]{:S(2)}) copy-start(f32[128,1024]{1,0:T(8,128)} %copy-done.21) | copy-start | bytes 1572868
  123.0 66.2 %all-to-all-start.3 = ((bf16[16,64,1792]{2,1,0:T(8,128)(2,1)}), bf16[16,64,1792]{2,1,0:T(8,128)(2,1)}, u32[]{:S(2)}, u32[]{:S(2)}) async-start(bf16[16,64,1792]{2,1,0:T(8,128)(2,1)} %bitcast.44), calls=%async_computation.3 | async-start | bytes 7340032 | tf_op jit(solution)/shard_map/all_to_all | solution.py:677
  130.6 5.5 %copy-start.15 = (bf16[4,128,1792]{2,1,0:T(8,128)(2,1)S(1)}, bf16[4,128,1792]{2,1,0:T(8,128)(2,1)}, u32[]{:S(2)}) copy-start(bf16[4,128,1792]{2,1,0:T(8,128)(2,1)} %copy-done.14) | copy-start | bytes 5505028
  130.6 5.5 %copy-start.17 = (bf16[4,128,1792]{2,1,0:T(8,128)(2,1)S(1)}, bf16[4,128,1792]{2,1,0:T(8,128)(2,1)}, u32[]{:S(2)}) copy-start(bf16[4,128,1792]{2,1,0:T(8,128)(2,1)} %copy-done.16) | copy-start | bytes 5505028
  132.1 8.0 %copy-start.24 = (f32[128,1024]{1,0:T(8,128)}, f32[128,1024]{1,0:T(8,128)S(1)}, u32[]{:S(2)}) copy-start(f32[128,1024]{1,0:T(8,128)S(1)} %get-tuple-element.132.refs_5_) | copy-start | bytes 1572868
  132.1 19.6 %copy-start.6 = (bf16[8,128,128]{2,1,0:T(8,128)(2,1)S(1)}, bf16[8,128,128]{2,1,0:T(8,128)(2,1)}, u32[]{:S(2)}) copy-start(bf16[8,128,128]{2,1,0:T(8,128)(2,1)} %copy-done.5) | copy-start | bytes 786436
  132.2 7.9 %collective-permute-start.26 = (bf16[128,1024]{1,0:T(8,128)(2,1)S(1)}, bf16[128,1024]{1,0:T(8,128)(2,1)S(1)}, u32[]{:S(2)}, u32[]{:S(2)}) collective-permute-start(bf16[128,1024]{1,0:T(8,128)(2,1)S(1)} %get-tuple-element.115), channel_id=1, source_target_pairs={{0,6},{1,7},{2,4},{3,5},{4,2},{5,3},{6,0},{7,1},{8,14},{9,15},{10,... | collective-permute-start | bytes 786440 | tf_op jit(solution)/shard_map/ppermute | solution.py:649
  134.3 6.4 %collective-permute-start.25 = (bf16[128,1024]{1,0:T(8,128)(2,1)S(1)}, bf16[128,1024]{1,0:T(8,128)(2,1)S(1)}, u32[]{:S(2)}, u32[]{:S(2)}) collective-permute-start(bf16[128,1024]{1,0:T(8,128)(2,1)S(1)} %get-tuple-element.115), channel_id=1, source_target_pairs={{0,4},{1,5},{2,6},{3,7},{4,0},{5,1},{6,2},{7,3},{8,12},{9,13},{10,... | collective-permute-start | bytes 786440 | tf_op jit(solution)/shard_map/ppermute | solution.py:649
  134.3 12.3 %collective-permute-start.24 = (bf16[128,1024]{1,0:T(8,128)(2,1)S(1)}, bf16[128,1024]{1,0:T(8,128)(2,1)S(1)}, u32[]{:S(2)}, u32[]{:S(2)}) collective-permute-start(bf16[128,1024]{1,0:T(8,128)(2,1)S(1)} %get-tuple-element.115), channel_id=1, source_target_pairs={{0,2},{1,3},{2,0},{3,1},{4,6},{5,7},{6,4},{7,5},{8,10},{9,11},{10,... | collective-permute-start | bytes 786440 | tf_op jit(solution)/shard_map/ppermute | solution.py:649
  140.1 12.6 %copy-start.12 = (bf16[4,128,1024]{2,1,0:T(8,128)(2,1)}, bf16[4,128,1024]{2,1,0:T(8,128)(2,1)S(1)}, u32[]{:S(2)}) copy-start(bf16[4,128,1024]{2,1,0:T(8,128)(2,1)S(1)} %get-tuple-element.113.refs_0_) | copy-start | bytes 3145732
  146.7 5.0 %collective-permute-start.27 = (bf16[4,128,1024]{2,1,0:T(8,128)(2,1)S(1)}, bf16[4,128,1024]{2,1,0:T(8,128)(2,1)S(1)}, u32[]{:S(2)}, u32[]{:S(2)}) collective-permute-start(bf16[4,128,1024]{2,1,0:T(8,128)(2,1)S(1)} %pad_maximum_fusion.4.refs_2_.refs_3_), channel_id=1, source_target_pairs={{0,1},{1,0},{2,3},{3,2},{4,5},{5,4},{6,7},{7,6},{8,9},{9,8},{10,11... | collective-permute-start | bytes 3145736 | tf_op jit(solution)/shard_map/ppermute | solution.py:649
  162.6 5.9 %collective-permute-start.32 = (bf16[4,128,1024]{2,1,0:T(8,128)(2,1)S(1)}, bf16[4,128,1024]{2,1,0:T(8,128)(2,1)S(1)}, u32[]{:S(2)}, u32[]{:S(2)}) collective-permute-start(bf16[4,128,1024]{2,1,0:T(8,128)(2,1)S(1)} %get-tuple-element.127), channel_id=1, source_target_pairs={{0,1},{1,0},{2,3},{3,2},{4,5},{5,4},{6,7},{7,6},{8,9},{9,8},{10,11... | collective-permute-start | bytes 3145736 | tf_op jit(solution)/shard_map/ppermute | solution.py:649
  163.0 2.6 %collective-permute-start.36 = (bf16[4,128,128]{2,1,0:T(8,128)(2,1)S(1)}, bf16[4,128,128]{2,1,0:T(8,128)(2,1)S(1)}, u32[]{:S(2)}, u32[]{:S(2)}) collective-permute-start(bf16[4,128,128]{2,1,0:T(8,128)(2,1)S(1)} %slice.28), channel_id=1, source_target_pairs={{0,1},{1,0},{2,3},{3,2},{4,5},{5,4},{6,7},{7,6},{8,9},{9,8},{10,11... | collective-permute-start | bytes 393224 | tf_op jit(solution)/shard_map/ppermute | solution.py:649
  163.2 36.8 %collective-permute-start.28 = (bf16[4,128,1024]{2,1,0:T(8,128)(2,1)}, bf16[4,128,1024]{2,1,0:T(8,128)(2,1)}, u32[]{:S(2)}, u32[]{:S(2)}) collective-permute-start(bf16[4,128,1024]{2,1,0:T(8,128)(2,1)} %get-tuple-element.121), channel_id=1, source_target_pairs={{0,1},{1,0},{2,3},{3,2},{4,5},{5,4},{6,7},{7,6},{8,9},{9,8},{10,11... | collective-permute-start | bytes 3145736 | tf_op jit(solution)/shard_map/ppermute | solution.py:649
  165.7 5.1 %collective-permute-start.37 = (bf16[2,128,128]{2,1,0:T(8,128)(2,1)S(1)}, bf16[2,128,128]{2,1,0:T(8,128)(2,1)S(1)}, u32[]{:S(2)}, u32[]{:S(2)}) collective-permute-start(bf16[2,128,128]{2,1,0:T(8,128)(2,1)S(1)} %get-tuple-element.136), channel_id=1, source_target_pairs={{0,2},{1,3},{2,0},{3,1},{4,6},{5,7},{6,4},{7,5},{8,10},{9,11},{10,... | collective-permute-start | bytes 196616 | tf_op jit(solution)/shard_map/ppermute | solution.py:649
  167.0 19.2 %copy-start.11 = (bf16[2,4,128,1024]{3,2,1,0:T(8,128)(2,1)S(1)}, bf16[2,4,128,1024]{3,2,1,0:T(8,128)(2,1)}, u32[]{:S(2)}) copy-start(bf16[2,4,128,1024]{3,2,1,0:T(8,128)(2,1)} %copy-done.10) | copy-start | bytes 6291460
  167.0 5.9 %collective-permute-start.38 = (bf16[2,128,128]{2,1,0:T(8,128)(2,1)S(1)}, bf16[2,128,128]{2,1,0:T(8,128)(2,1)S(1)}, u32[]{:S(2)}, u32[]{:S(2)}) collective-permute-start(bf16[2,128,128]{2,1,0:T(8,128)(2,1)S(1)} %get-tuple-element.137), channel_id=1, source_target_pairs={{0,4},{1,5},{2,6},{3,7},{4,0},{5,1},{6,2},{7,3},{8,12},{9,13},{10,... | collective-permute-start | bytes 196616 | tf_op jit(solution)/shard_map/ppermute | solution.py:649
  169.4 19.2 %collective-permute-start.33 = (bf16[128,1024]{1,0:T(8,128)(2,1)S(1)}, bf16[128,1024]{1,0:T(8,128)(2,1)S(1)}, u32[]{:S(2)}, u32[]{:S(2)}) collective-permute-start(bf16[128,1024]{1,0:T(8,128)(2,1)S(1)} %get-tuple-element.129), channel_id=1, source_target_pairs={{0,2},{1,3},{2,0},{3,1},{4,6},{5,7},{6,4},{7,5},{8,10},{9,11},{10,... | collective-permute-start | bytes 786440 | tf_op jit(solution)/shard_map/ppermute | solution.py:649
  170.1 18.5 %collective-permute-start.34 = (bf16[128,1024]{1,0:T(8,128)(2,1)S(1)}, bf16[128,1024]{1,0:T(8,128)(2,1)S(1)}, u32[]{:S(2)}, u32[]{:S(2)}) collective-permute-start(bf16[128,1024]{1,0:T(8,128)(2,1)S(1)} %get-tuple-element.130), channel_id=1, source_target_pairs={{0,4},{1,5},{2,6},{3,7},{4,0},{5,1},{6,2},{7,3},{8,12},{9,13},{10,... | collective-permute-start | bytes 786440 | tf_op jit(solution)/shard_map/ppermute | solution.py:649
  170.8 17.8 %collective-permute-start.35 = (bf16[128,1024]{1,0:T(8,128)(2,1)S(1)}, bf16[128,1024]{1,0:T(8,128)(2,1)S(1)}, u32[]{:S(2)}, u32[]{:S(2)}) collective-permute-start(bf16[128,1024]{1,0:T(8,128)(2,1)S(1)} %get-tuple-element.131), channel_id=1, source_target_pairs={{0,6},{1,7},{2,4},{3,5},{4,2},{5,3},{6,0},{7,1},{8,14},{9,15},{10,... | collective-permute-start | bytes 786440 | tf_op jit(solution)/shard_map/ppermute | solution.py:649
  172.9 13.3 %collective-permute-start.39 = (bf16[2,128,128]{2,1,0:T(8,128)(2,1)S(1)}, bf16[2,128,128]{2,1,0:T(8,128)(2,1)S(1)}, u32[]{:S(2)}, u32[]{:S(2)}) collective-permute-start(bf16[2,128,128]{2,1,0:T(8,128)(2,1)S(1)} %get-tuple-element.138), channel_id=1, source_target_pairs={{0,6},{1,7},{2,4},{3,5},{4,2},{5,3},{6,0},{7,1},{8,14},{9,15},{10,... | collective-permute-start | bytes 196616 | tf_op jit(solution)/shard_map/ppermute | solution.py:649
  189.3 21.3 %all-to-all-start.2 = ((bf16[16,80,384]{2,1,0:T(8,128)(2,1)}), bf16[16,80,384]{2,1,0:T(8,128)(2,1)S(1)}, u32[]{:S(2)}, u32[]{:S(2)}) async-start(bf16[16,80,384]{2,1,0:T(8,128)(2,1)} %attention_sums.1), calls=%async_computation.2 | async-start | bytes 1966080 | tf_op jit(solution)/shard_map/all_to_all | solution.py:677
  200.0 10.6 %copy-start.33 = (bf16[64,256]{1,0:T(8,128)(2,1)S(1)}, bf16[64,256]{1,0:T(8,128)(2,1)}, u32[]{:S(2)}) copy-start(bf16[64,256]{1,0:T(8,128)(2,1)} %get-tuple-element.86.refs_1_) | copy-start | bytes 98308
  200.0 20.2 %collective-permute-start.40 = (bf16[64,1792]{1,0:T(8,128)(2,1)}, bf16[64,1792]{1,0:T(8,128)(2,1)}, u32[]{:S(2)}, u32[]{:S(2)}) collective-permute-start(bf16[64,1792]{1,0:T(8,128)(2,1)} %get-tuple-element.149), channel_id=1, source_target_pairs={{0,4},{1,5},{2,6},{3,7},{4,0},{5,1},{6,2},{7,3},{8,12},{9,13},{10,... | collective-permute-start | bytes 688136 | tf_op jit(solution)/shard_map/ppermute | solution.py:649
  202.8 20.6 %collective-permute-start.29 = (bf16[128,1024]{1,0:T(8,128)(2,1)}, bf16[128,1024]{1,0:T(8,128)(2,1)S(1)}, u32[]{:S(2)}, u32[]{:S(2)}) collective-permute-start(bf16[128,1024]{1,0:T(8,128)(2,1)} %get-tuple-element.123), channel_id=1, source_target_pairs={{0,2},{1,3},{2,0},{3,1},{4,6},{5,7},{6,4},{7,5},{8,10},{9,11},{10,... | collective-permute-start | bytes 786440 | tf_op jit(solution)/shard_map/ppermute | solution.py:649
  205.2 18.2 %collective-permute-start.30 = (bf16[128,1024]{1,0:T(8,128)(2,1)}, bf16[128,1024]{1,0:T(8,128)(2,1)}, u32[]{:S(2)}, u32[]{:S(2)}) collective-permute-start(bf16[128,1024]{1,0:T(8,128)(2,1)} %get-tuple-element.124), channel_id=1, source_target_pairs={{0,4},{1,5},{2,6},{3,7},{4,0},{5,1},{6,2},{7,3},{8,12},{9,13},{10,... | collective-permute-start | bytes 786440 | tf_op jit(solution)/shard_map/ppermute | solution.py:649
  205.2 18.2 %collective-permute-start.31 = (bf16[128,1024]{1,0:T(8,128)(2,1)S(1)}, bf16[128,1024]{1,0:T(8,128)(2,1)}, u32[]{:S(2)}, u32[]{:S(2)}) collective-permute-start(bf16[128,1024]{1,0:T(8,128)(2,1)S(1)} %get-tuple-element.125), channel_id=1, source_target_pairs={{0,6},{1,7},{2,4},{3,5},{4,2},{5,3},{6,0},{7,1},{8,14},{9,15},{10,... | collective-permute-start | bytes 786440 | tf_op jit(solution)/shard_map/ppermute | solution.py:649
  212.6 7.7 %copy-start.20 = (f32[64,1792]{1,0:T(8,128)S(1)}, f32[64,1792]{1,0:T(8,128)}, u32[]{:S(2)}) copy-start(f32[64,1792]{1,0:T(8,128)} %copy-done.18) | copy-start | bytes 1376260
  213.6 15.1 %all-to-all-start.4 = ((bf16[8,80,384]{2,1,0:T(8,128)(2,1)}), bf16[8,80,384]{2,1,0:T(8,128)(2,1)S(1)}, u32[]{:S(2)}, u32[]{:S(2)}) async-start(bf16[8,80,384]{2,1,0:T(8,128)(2,1)} %attention_total.1), calls=%async_computation.4 | async-start | bytes 983040 | tf_op jit(solution)/shard_map/all_to_all | solution.py:865
  223.5 5.3 %copy-start.34 = (f32[8,128]{1,0:T(8,128)S(1)}, f32[8,128]{1,0:T(8,128)}, u32[]{:S(2)}) copy-start(f32[8,128]{1,0:T(8,128)} %get-tuple-element.133.refs_0_) | copy-start | bytes 12292
  (17 other events, 23.1 us)
